TPU v7x, 256 devices: a whole 4x4x8 slice. The times are simulated.
256 devices in a mesh: tm: 64 (over z, y, core), sensor: 4 (over x).
Axes of the slice: x: 4, y: 4, z: 8, core: 2. Of those that a mesh axis runs over, the one named last changes fastest.
Arguments:
- observations: bfloat16 [16384, 16384], P(('sensor', 'tm')), may hold values from -6 to 6
- sensor_map: bfloat16 [16384, 128], P('sensor'), may hold values from -0.046875 to 0.046875
- noise_precision: bfloat16 [128, 128, 128], P('sensor'), may hold values from -0.0031496063 to 1.4, as said below
- availability: int32 [64, 128], P('tm', 'sensor'), may hold values from 0 to 1
- decay_rate: float32 [128], replicated, may hold values from 6.1035157e-06 to 0.03
- prior_mean: float32 [128], replicated, may hold values from -6 to 6
Outputs:
- filtered_states: float32 [16384, 128], P('tm')
Inputs may be any that keep to these rules, and one draw needn't show every extreme that they name: `noise_precision`: each block is symmetric, its diagonal lies in 0.6 to 1.4 and exceeds the sum of magnitudes of the rest of its row.
All inputs are finite; a program needn't handle non-finite values.
Results may differ from a plain program's by a relative error of at most 0.0019.
Values may be sent and summed in bfloat16 or wider, within the bound.
No kernel may reach another device: no remote copies, remote signals or barrier semaphores. Data moves between devices by JAX's collectives and lax.ppermute only.
A program may use at most 128 MiB of HBM per device.

v0:
```python
import jax
import jax.numpy as jnp
from jax import lax
from jax.sharding import PartitionSpec as P

TB_DEV = 256


def from_behind(block, axis, distance):
    devices = range(lax.axis_size(axis))
    route = [(i - distance, i) for i in devices if i - distance in devices]
    return lax.ppermute(block, axis, route)


def on_device(observations, sensor_map, noise_precision, availability, decay_rate, prior_mean):
    mode_count = sensor_map.shape[1]
    block_size = noise_precision.shape[1]
    group_blocks = noise_precision.shape[0]
    group_rows = sensor_map.shape[0]
    block_steps = TB_DEV
    time_index = lax.axis_index("tm")
    contract = (((0,), (0,)), ((), ()))
    received = lax.all_to_all(observations, "tm", split_axis=1, concat_axis=0, tiled=True)
    weighted = jnp.einsum(
        "bij,bjm->bim",
        noise_precision,
        sensor_map.reshape(group_blocks, block_size, mode_count),
        preferred_element_type=jnp.float32,
    ).astype(jnp.bfloat16)
    kept_blocks = availability[0].astype(jnp.bfloat16)
    masked = (weighted * kept_blocks[:, None, None]).reshape(group_rows, mode_count)
    info_rows = lax.dot_general(received, masked, contract, preferred_element_type=jnp.float32)
    info_matrix = lax.dot_general(sensor_map, masked, contract, preferred_element_type=jnp.float32)
    combined = jnp.concatenate([info_rows, info_matrix], 0)
    combined = lax.psum(combined, "sensor")
    info_rows = combined[:block_steps]
    info_matrix = combined[block_steps:]
    retain = jnp.exp(-decay_rate)
    identity = jnp.eye(mode_count, dtype=jnp.float32)
    transition = (identity - decay_rate[:, None] * info_matrix) * retain[None, :]
    levels = block_steps.bit_length() - 1
    powers = []
    current_power = transition
    for level in range(levels):
        powers.append(current_power)
        current_power = jnp.dot(current_power, current_power, precision=lax.Precision.HIGHEST)
    block_matrix = current_power

    def sweep(rows):
        for level in range(levels):
            offset = 2**level
            moved = jnp.dot(rows[:-offset], powers[level].T, precision=lax.Precision.HIGHEST)
            rows = rows + jnp.pad(moved, ((offset, 0), (0, 0)))
        return rows

    drive = decay_rate[None, :] * info_rows
    partial_rows = sweep(drive)
    block_offset = partial_rows[-1]

    def relay_step(position, incoming):
        leaving = jnp.dot(block_matrix, incoming, precision=lax.Precision.HIGHEST) + block_offset
        arriving = from_behind(leaving, "tm", 1)
        return jnp.where(time_index == position + 1, arriving, incoming)

    entry_state = lax.fori_loop(0, lax.axis_size("tm") - 1, relay_step, prior_mean)
    start_push = jnp.dot(transition, entry_state, precision=lax.Precision.HIGHEST)
    seeded = drive.at[0].add(start_push)
    return sweep(seeded)


def solution(mesh):
    return jax.shard_map(
        on_device,
        mesh=mesh,
        in_specs=(
            P(("sensor", "tm"), None),
            P("sensor", None),
            P("sensor", None, None),
            P("tm", "sensor"),
            P(),
            P(),
        ),
        out_specs=P("tm", None),
        check_vma=False,
    )
```

profile of v0, /device:TPU:128, one launch (start us, length us, event | category | flops | bytes accessed | tf_op | source)
XLA Modules:
  0.0 667.1 jit_solution(15781803504071090081)
XLA Ops:
  9.8 10.8 %all-to-all-start = ((bf16[64,64,256]{2,0,1:T(8,128)(2,1)}), bf16[64,64,256]{2,0,1:T(8,128)(2,1)}, u32[]{:S(2)}, u32[]{:S(2)}) async-start(bf16[64,64,256]{2,0,1:T(8,128)(2,1)} %bitcast.60), calls=%async_computation | async-start | bytes 4194304 | tf_op jit(solution)/shard_map/all_to_all | solution.py:23
  21.7 46.3 %all-to-all-done = bf16[64,64,256]{2,0,1:T(8,128)(2,1)} async-done(((bf16[64,64,256]{2,0,1:T(8,128)(2,1)}), bf16[64,64,256]{2,0,1:T(8,128)(2,1)}, u32[]{:S(2)}, u32[]{:S(2)}) %all-to-all-start) | async-done | bytes 2097184 | tf_op jit(solution)/shard_map/all_to_all | solution.py:23
  70.8 47.0 %all-reduce.18.cloned.1.call-done = f32[384,128]{0,1:T(8,128)} async-done(((f32[384,128]{0,1:T(8,128)}), f32[384,128]{0,1:T(8,128)}) %all-reduce.18.cloned.1.call-update) | async-done | bytes 196624 | tf_op jit(solution)/shard_map/psum | solution.py:35
  126.5 529.3 %while.14 = (s32[]{:T(128)}, f32[128]{0:T(128)S(1)}, s32[]{:T(128)}, f32[128,128]{1,0:T(8,128)S(1)}, f32[128]{0:T(128)S(1)}, /*index=5*/s32[]{:T(128)}) while((s32[]{:T(128)}, f32[128]{0:T(128)S(1)}, s32[]{:T(128)}, f32[128,128]{1,0:T(8,128)S(1)}, f32[128]{0:T(128)S(1)}, /*index=5*/s32[]{:T(128)}) %tuple.37), condition=%wide.region_2.3_spmd, body=%wide.region_1.2_spmd.sunk | while | flops 196867 | bytes 70775 | solution.py:65
  128.7 6.2 collective-permute-done
  137.1 6.2 collective-permute-done
  145.5 6.2 collective-permute-done
  153.9 6.2 collective-permute-done
  170.7 6.2 collective-permute-done
  179.1 6.2 collective-permute-done
  187.5 6.2 collective-permute-done
  195.9 6.2 collective-permute-done
  204.3 6.2 collective-permute-done
  212.7 6.2 collective-permute-done
  221.1 6.2 collective-permute-done
  229.5 6.2 collective-permute-done
  237.9 6.2 collective-permute-done
  246.3 6.2 collective-permute-done
  254.7 6.2 collective-permute-done
  263.1 6.2 collective-permute-done
  271.5 6.2 collective-permute-done
  279.9 6.2 collective-permute-done
  288.3 6.2 collective-permute-done
  296.7 6.2 collective-permute-done
  305.1 6.2 collective-permute-done
  313.5 6.2 collective-permute-done
  330.3 6.2 collective-permute-done
  338.7 6.2 collective-permute-done
  347.1 6.2 collective-permute-done
  355.5 6.2 collective-permute-done
  363.9 6.2 collective-permute-done
  372.3 6.2 collective-permute-done
  380.7 6.2 collective-permute-done
  389.1 6.2 collective-permute-done
  397.5 6.2 collective-permute-done
  405.9 6.2 collective-permute-done
  414.3 6.2 collective-permute-done
  422.7 6.2 collective-permute-done
  431.1 6.2 collective-permute-done
  439.5 6.2 collective-permute-done
  447.9 6.2 collective-permute-done
  456.3 6.2 collective-permute-done
  464.7 6.2 collective-permute-done
  473.2 6.2 collective-permute-done
  490.0 6.2 collective-permute-done
  498.4 6.2 collective-permute-done
  506.8 6.2 collective-permute-done
  515.2 6.2 collective-permute-done
  (273 shorter events, 273.3 us)
Async XLA Ops:
  9.8 58.1 %all-to-all-start = ((bf16[64,64,256]{2,0,1:T(8,128)(2,1)}), bf16[64,64,256]{2,0,1:T(8,128)(2,1)}, u32[]{:S(2)}, u32[]{:S(2)}) async-start(bf16[64,64,256]{2,0,1:T(8,128)(2,1)} %bitcast.60), calls=%async_computation | async-start | bytes 4194304 | tf_op jit(solution)/shard_map/all_to_all | solution.py:23
  20.6 97.2 %all-reduce.18.cloned.1.call-start = ((), (), s32[]{:S(2)}) async-start(), calls=%async_computation.1 | async-start | bytes 393216 | tf_op jit(solution)/shard_map/psum | solution.py:35
  135.1 8.2 %collective-permute-start = (f32[128]{0:T(128)S(1)}, f32[128]{0:T(128)S(1)}, u32[]{:S(2)}, u32[]{:S(2)}) collective-permute-start(f32[128]{0:T(128)S(1)} %fusion.91), channel_id=1, source_target_pairs={{0,4},{4,8},{8,12},{12,16},{16,20},{20,24},{24,28},{28,32},{32,36}... | collective-permute-start | bytes 1544 | tf_op jit(solution)/shard_map/while/body/eval_jaxpr/ppermute | solution.py:12
  143.5 8.2 %collective-permute-start = (f32[128]{0:T(128)S(1)}, f32[128]{0:T(128)S(1)}, u32[]{:S(2)}, u32[]{:S(2)}) collective-permute-start(f32[128]{0:T(128)S(1)} %fusion.91), channel_id=1, source_target_pairs={{0,4},{4,8},{8,12},{12,16},{16,20},{20,24},{24,28},{28,32},{32,36}... | collective-permute-start | bytes 1544 | tf_op jit(solution)/shard_map/while/body/eval_jaxpr/ppermute | solution.py:12
  151.9 8.2 %collective-permute-start = (f32[128]{0:T(128)S(1)}, f32[128]{0:T(128)S(1)}, u32[]{:S(2)}, u32[]{:S(2)}) collective-permute-start(f32[128]{0:T(128)S(1)} %fusion.91), channel_id=1, source_target_pairs={{0,4},{4,8},{8,12},{12,16},{16,20},{20,24},{24,28},{28,32},{32,36}... | collective-permute-start | bytes 1544 | tf_op jit(solution)/shard_map/while/body/eval_jaxpr/ppermute | solution.py:12
  168.7 8.2 %collective-permute-start = (f32[128]{0:T(128)S(1)}, f32[128]{0:T(128)S(1)}, u32[]{:S(2)}, u32[]{:S(2)}) collective-permute-start(f32[128]{0:T(128)S(1)} %fusion.91), channel_id=1, source_target_pairs={{0,4},{4,8},{8,12},{12,16},{16,20},{20,24},{24,28},{28,32},{32,36}... | collective-permute-start | bytes 1544 | tf_op jit(solution)/shard_map/while/body/eval_jaxpr/ppermute | solution.py:12
  177.1 8.2 %collective-permute-start = (f32[128]{0:T(128)S(1)}, f32[128]{0:T(128)S(1)}, u32[]{:S(2)}, u32[]{:S(2)}) collective-permute-start(f32[128]{0:T(128)S(1)} %fusion.91), channel_id=1, source_target_pairs={{0,4},{4,8},{8,12},{12,16},{16,20},{20,24},{24,28},{28,32},{32,36}... | collective-permute-start | bytes 1544 | tf_op jit(solution)/shard_map/while/body/eval_jaxpr/ppermute | solution.py:12
  185.5 8.2 %collective-permute-start = (f32[128]{0:T(128)S(1)}, f32[128]{0:T(128)S(1)}, u32[]{:S(2)}, u32[]{:S(2)}) collective-permute-start(f32[128]{0:T(128)S(1)} %fusion.91), channel_id=1, source_target_pairs={{0,4},{4,8},{8,12},{12,16},{16,20},{20,24},{24,28},{28,32},{32,36}... | collective-permute-start | bytes 1544 | tf_op jit(solution)/shard_map/while/body/eval_jaxpr/ppermute | solution.py:12
  193.9 8.2 %collective-permute-start = (f32[128]{0:T(128)S(1)}, f32[128]{0:T(128)S(1)}, u32[]{:S(2)}, u32[]{:S(2)}) collective-permute-start(f32[128]{0:T(128)S(1)} %fusion.91), channel_id=1, source_target_pairs={{0,4},{4,8},{8,12},{12,16},{16,20},{20,24},{24,28},{28,32},{32,36}... | collective-permute-start | bytes 1544 | tf_op jit(solution)/shard_map/while/body/eval_jaxpr/ppermute | solution.py:12
  202.3 8.2 %collective-permute-start = (f32[128]{0:T(128)S(1)}, f32[128]{0:T(128)S(1)}, u32[]{:S(2)}, u32[]{:S(2)}) collective-permute-start(f32[128]{0:T(128)S(1)} %fusion.91), channel_id=1, source_target_pairs={{0,4},{4,8},{8,12},{12,16},{16,20},{20,24},{24,28},{28,32},{32,36}... | collective-permute-start | bytes 1544 | tf_op jit(solution)/shard_map/while/body/eval_jaxpr/ppermute | solution.py:12
  210.7 8.2 %collective-permute-start = (f32[128]{0:T(128)S(1)}, f32[128]{0:T(128)S(1)}, u32[]{:S(2)}, u32[]{:S(2)}) collective-permute-start(f32[128]{0:T(128)S(1)} %fusion.91), channel_id=1, source_target_pairs={{0,4},{4,8},{8,12},{12,16},{16,20},{20,24},{24,28},{28,32},{32,36}... | collective-permute-start | bytes 1544 | tf_op jit(solution)/shard_map/while/body/eval_jaxpr/ppermute | solution.py:12
  227.5 8.2 %collective-permute-start = (f32[128]{0:T(128)S(1)}, f32[128]{0:T(128)S(1)}, u32[]{:S(2)}, u32[]{:S(2)}) collective-permute-start(f32[128]{0:T(128)S(1)} %fusion.91), channel_id=1, source_target_pairs={{0,4},{4,8},{8,12},{12,16},{16,20},{20,24},{24,28},{28,32},{32,36}... | collective-permute-start | bytes 1544 | tf_op jit(solution)/shard_map/while/body/eval_jaxpr/ppermute | solution.py:12
  235.9 8.2 %collective-permute-start = (f32[128]{0:T(128)S(1)}, f32[128]{0:T(128)S(1)}, u32[]{:S(2)}, u32[]{:S(2)}) collective-permute-start(f32[128]{0:T(128)S(1)} %fusion.91), channel_id=1, source_target_pairs={{0,4},{4,8},{8,12},{12,16},{16,20},{20,24},{24,28},{28,32},{32,36}... | collective-permute-start | bytes 1544 | tf_op jit(solution)/shard_map/while/body/eval_jaxpr/ppermute | solution.py:12
  244.3 8.2 %collective-permute-start = (f32[128]{0:T(128)S(1)}, f32[128]{0:T(128)S(1)}, u32[]{:S(2)}, u32[]{:S(2)}) collective-permute-start(f32[128]{0:T(128)S(1)} %fusion.91), channel_id=1, source_target_pairs={{0,4},{4,8},{8,12},{12,16},{16,20},{20,24},{24,28},{28,32},{32,36}... | collective-permute-start | bytes 1544 | tf_op jit(solution)/shard_map/while/body/eval_jaxpr/ppermute | solution.py:12
  261.1 8.2 %collective-permute-start = (f32[128]{0:T(128)S(1)}, f32[128]{0:T(128)S(1)}, u32[]{:S(2)}, u32[]{:S(2)}) collective-permute-start(f32[128]{0:T(128)S(1)} %fusion.91), channel_id=1, source_target_pairs={{0,4},{4,8},{8,12},{12,16},{16,20},{20,24},{24,28},{28,32},{32,36}... | collective-permute-start | bytes 1544 | tf_op jit(solution)/shard_map/while/body/eval_jaxpr/ppermute | solution.py:12
  269.5 8.2 %collective-permute-start = (f32[128]{0:T(128)S(1)}, f32[128]{0:T(128)S(1)}, u32[]{:S(2)}, u32[]{:S(2)}) collective-permute-start(f32[128]{0:T(128)S(1)} %fusion.91), channel_id=1, source_target_pairs={{0,4},{4,8},{8,12},{12,16},{16,20},{20,24},{24,28},{28,32},{32,36}... | collective-permute-start | bytes 1544 | tf_op jit(solution)/shard_map/while/body/eval_jaxpr/ppermute | solution.py:12
  277.9 8.2 %collective-permute-start = (f32[128]{0:T(128)S(1)}, f32[128]{0:T(128)S(1)}, u32[]{:S(2)}, u32[]{:S(2)}) collective-permute-start(f32[128]{0:T(128)S(1)} %fusion.91), channel_id=1, source_target_pairs={{0,4},{4,8},{8,12},{12,16},{16,20},{20,24},{24,28},{28,32},{32,36}... | collective-permute-start | bytes 1544 | tf_op jit(solution)/shard_map/while/body/eval_jaxpr/ppermute | solution.py:12
  294.7 8.2 %collective-permute-start = (f32[128]{0:T(128)S(1)}, f32[128]{0:T(128)S(1)}, u32[]{:S(2)}, u32[]{:S(2)}) collective-permute-start(f32[128]{0:T(128)S(1)} %fusion.91), channel_id=1, source_target_pairs={{0,4},{4,8},{8,12},{12,16},{16,20},{20,24},{24,28},{28,32},{32,36}... | collective-permute-start | bytes 1544 | tf_op jit(solution)/shard_map/while/body/eval_jaxpr/ppermute | solution.py:12
  303.1 8.2 %collective-permute-start = (f32[128]{0:T(128)S(1)}, f32[128]{0:T(128)S(1)}, u32[]{:S(2)}, u32[]{:S(2)}) collective-permute-start(f32[128]{0:T(128)S(1)} %fusion.91), channel_id=1, source_target_pairs={{0,4},{4,8},{8,12},{12,16},{16,20},{20,24},{24,28},{28,32},{32,36}... | collective-permute-start | bytes 1544 | tf_op jit(solution)/shard_map/while/body/eval_jaxpr/ppermute | solution.py:12
  311.5 8.2 %collective-permute-start = (f32[128]{0:T(128)S(1)}, f32[128]{0:T(128)S(1)}, u32[]{:S(2)}, u32[]{:S(2)}) collective-permute-start(f32[128]{0:T(128)S(1)} %fusion.91), channel_id=1, source_target_pairs={{0,4},{4,8},{8,12},{12,16},{16,20},{20,24},{24,28},{28,32},{32,36}... | collective-permute-start | bytes 1544 | tf_op jit(solution)/shard_map/while/body/eval_jaxpr/ppermute | solution.py:12
  328.3 8.2 %collective-permute-start = (f32[128]{0:T(128)S(1)}, f32[128]{0:T(128)S(1)}, u32[]{:S(2)}, u32[]{:S(2)}) collective-permute-start(f32[128]{0:T(128)S(1)} %fusion.91), channel_id=1, source_target_pairs={{0,4},{4,8},{8,12},{12,16},{16,20},{20,24},{24,28},{28,32},{32,36}... | collective-permute-start | bytes 1544 | tf_op jit(solution)/shard_map/while/body/eval_jaxpr/ppermute | solution.py:12
  336.7 8.2 %collective-permute-start = (f32[128]{0:T(128)S(1)}, f32[128]{0:T(128)S(1)}, u32[]{:S(2)}, u32[]{:S(2)}) collective-permute-start(f32[128]{0:T(128)S(1)} %fusion.91), channel_id=1, source_target_pairs={{0,4},{4,8},{8,12},{12,16},{16,20},{20,24},{24,28},{28,32},{32,36}... | collective-permute-start | bytes 1544 | tf_op jit(solution)/shard_map/while/body/eval_jaxpr/ppermute | solution.py:12
  345.1 8.2 %collective-permute-start = (f32[128]{0:T(128)S(1)}, f32[128]{0:T(128)S(1)}, u32[]{:S(2)}, u32[]{:S(2)}) collective-permute-start(f32[128]{0:T(128)S(1)} %fusion.91), channel_id=1, source_target_pairs={{0,4},{4,8},{8,12},{12,16},{16,20},{20,24},{24,28},{28,32},{32,36}... | collective-permute-start | bytes 1544 | tf_op jit(solution)/shard_map/while/body/eval_jaxpr/ppermute | solution.py:12
  353.5 8.2 %collective-permute-start = (f32[128]{0:T(128)S(1)}, f32[128]{0:T(128)S(1)}, u32[]{:S(2)}, u32[]{:S(2)}) collective-permute-start(f32[128]{0:T(128)S(1)} %fusion.91), channel_id=1, source_target_pairs={{0,4},{4,8},{8,12},{12,16},{16,20},{20,24},{24,28},{28,32},{32,36}... | collective-permute-start | bytes 1544 | tf_op jit(solution)/shard_map/while/body/eval_jaxpr/ppermute | solution.py:12
  361.9 8.2 %collective-permute-start = (f32[128]{0:T(128)S(1)}, f32[128]{0:T(128)S(1)}, u32[]{:S(2)}, u32[]{:S(2)}) collective-permute-start(f32[128]{0:T(128)S(1)} %fusion.91), channel_id=1, source_target_pairs={{0,4},{4,8},{8,12},{12,16},{16,20},{20,24},{24,28},{28,32},{32,36}... | collective-permute-start | bytes 1544 | tf_op jit(solution)/shard_map/while/body/eval_jaxpr/ppermute | solution.py:12
  370.4 8.2 %collective-permute-start = (f32[128]{0:T(128)S(1)}, f32[128]{0:T(128)S(1)}, u32[]{:S(2)}, u32[]{:S(2)}) collective-permute-start(f32[128]{0:T(128)S(1)} %fusion.91), channel_id=1, source_target_pairs={{0,4},{4,8},{8,12},{12,16},{16,20},{20,24},{24,28},{28,32},{32,36}... | collective-permute-start | bytes 1544 | tf_op jit(solution)/shard_map/while/body/eval_jaxpr/ppermute | solution.py:12
  387.2 8.2 %collective-permute-start = (f32[128]{0:T(128)S(1)}, f32[128]{0:T(128)S(1)}, u32[]{:S(2)}, u32[]{:S(2)}) collective-permute-start(f32[128]{0:T(128)S(1)} %fusion.91), channel_id=1, source_target_pairs={{0,4},{4,8},{8,12},{12,16},{16,20},{20,24},{24,28},{28,32},{32,36}... | collective-permute-start | bytes 1544 | tf_op jit(solution)/shard_map/while/body/eval_jaxpr/ppermute | solution.py:12
  395.6 8.2 %collective-permute-start = (f32[128]{0:T(128)S(1)}, f32[128]{0:T(128)S(1)}, u32[]{:S(2)}, u32[]{:S(2)}) collective-permute-start(f32[128]{0:T(128)S(1)} %fusion.91), channel_id=1, source_target_pairs={{0,4},{4,8},{8,12},{12,16},{16,20},{20,24},{24,28},{28,32},{32,36}... | collective-permute-start | bytes 1544 | tf_op jit(solution)/shard_map/while/body/eval_jaxpr/ppermute | solution.py:12
  404.0 8.2 %collective-permute-start = (f32[128]{0:T(128)S(1)}, f32[128]{0:T(128)S(1)}, u32[]{:S(2)}, u32[]{:S(2)}) collective-permute-start(f32[128]{0:T(128)S(1)} %fusion.91), channel_id=1, source_target_pairs={{0,4},{4,8},{8,12},{12,16},{16,20},{20,24},{24,28},{28,32},{32,36}... | collective-permute-start | bytes 1544 | tf_op jit(solution)/shard_map/while/body/eval_jaxpr/ppermute | solution.py:12
  420.8 8.2 %collective-permute-start = (f32[128]{0:T(128)S(1)}, f32[128]{0:T(128)S(1)}, u32[]{:S(2)}, u32[]{:S(2)}) collective-permute-start(f32[128]{0:T(128)S(1)} %fusion.91), channel_id=1, source_target_pairs={{0,4},{4,8},{8,12},{12,16},{16,20},{20,24},{24,28},{28,32},{32,36}... | collective-permute-start | bytes 1544 | tf_op jit(solution)/shard_map/while/body/eval_jaxpr/ppermute | solution.py:12
  429.2 8.2 %collective-permute-start = (f32[128]{0:T(128)S(1)}, f32[128]{0:T(128)S(1)}, u32[]{:S(2)}, u32[]{:S(2)}) collective-permute-start(f32[128]{0:T(128)S(1)} %fusion.91), channel_id=1, source_target_pairs={{0,4},{4,8},{8,12},{12,16},{16,20},{20,24},{24,28},{28,32},{32,36}... | collective-permute-start | bytes 1544 | tf_op jit(solution)/shard_map/while/body/eval_jaxpr/ppermute | solution.py:12
  437.6 8.2 %collective-permute-start = (f32[128]{0:T(128)S(1)}, f32[128]{0:T(128)S(1)}, u32[]{:S(2)}, u32[]{:S(2)}) collective-permute-start(f32[128]{0:T(128)S(1)} %fusion.91), channel_id=1, source_target_pairs={{0,4},{4,8},{8,12},{12,16},{16,20},{20,24},{24,28},{28,32},{32,36}... | collective-permute-start | bytes 1544 | tf_op jit(solution)/shard_map/while/body/eval_jaxpr/ppermute | solution.py:12
  454.4 8.2 %collective-permute-start = (f32[128]{0:T(128)S(1)}, f32[128]{0:T(128)S(1)}, u32[]{:S(2)}, u32[]{:S(2)}) collective-permute-start(f32[128]{0:T(128)S(1)} %fusion.91), channel_id=1, source_target_pairs={{0,4},{4,8},{8,12},{12,16},{16,20},{20,24},{24,28},{28,32},{32,36}... | collective-permute-start | bytes 1544 | tf_op jit(solution)/shard_map/while/body/eval_jaxpr/ppermute | solution.py:12
  462.8 8.2 %collective-permute-start = (f32[128]{0:T(128)S(1)}, f32[128]{0:T(128)S(1)}, u32[]{:S(2)}, u32[]{:S(2)}) collective-permute-start(f32[128]{0:T(128)S(1)} %fusion.91), channel_id=1, source_target_pairs={{0,4},{4,8},{8,12},{12,16},{16,20},{20,24},{24,28},{28,32},{32,36}... | collective-permute-start | bytes 1544 | tf_op jit(solution)/shard_map/while/body/eval_jaxpr/ppermute | solution.py:12
  471.2 8.2 %collective-permute-start = (f32[128]{0:T(128)S(1)}, f32[128]{0:T(128)S(1)}, u32[]{:S(2)}, u32[]{:S(2)}) collective-permute-start(f32[128]{0:T(128)S(1)} %fusion.91), channel_id=1, source_target_pairs={{0,4},{4,8},{8,12},{12,16},{16,20},{20,24},{24,28},{28,32},{32,36}... | collective-permute-start | bytes 1544 | tf_op jit(solution)/shard_map/while/body/eval_jaxpr/ppermute | solution.py:12
  488.0 8.2 %collective-permute-start = (f32[128]{0:T(128)S(1)}, f32[128]{0:T(128)S(1)}, u32[]{:S(2)}, u32[]{:S(2)}) collective-permute-start(f32[128]{0:T(128)S(1)} %fusion.91), channel_id=1, source_target_pairs={{0,4},{4,8},{8,12},{12,16},{16,20},{20,24},{24,28},{28,32},{32,36}... | collective-permute-start | bytes 1544 | tf_op jit(solution)/shard_map/while/body/eval_jaxpr/ppermute | solution.py:12
  496.4 8.2 %collective-permute-start = (f32[128]{0:T(128)S(1)}, f32[128]{0:T(128)S(1)}, u32[]{:S(2)}, u32[]{:S(2)}) collective-permute-start(f32[128]{0:T(128)S(1)} %fusion.91), channel_id=1, source_target_pairs={{0,4},{4,8},{8,12},{12,16},{16,20},{20,24},{24,28},{28,32},{32,36}... | collective-permute-start | bytes 1544 | tf_op jit(solution)/shard_map/while/body/eval_jaxpr/ppermute | solution.py:12
  504.8 8.2 %collective-permute-start = (f32[128]{0:T(128)S(1)}, f32[128]{0:T(128)S(1)}, u32[]{:S(2)}, u32[]{:S(2)}) collective-permute-start(f32[128]{0:T(128)S(1)} %fusion.91), channel_id=1, source_target_pairs={{0,4},{4,8},{8,12},{12,16},{16,20},{20,24},{24,28},{28,32},{32,36}... | collective-permute-start | bytes 1544 | tf_op jit(solution)/shard_map/while/body/eval_jaxpr/ppermute | solution.py:12
  513.2 8.2 %collective-permute-start = (f32[128]{0:T(128)S(1)}, f32[128]{0:T(128)S(1)}, u32[]{:S(2)}, u32[]{:S(2)}) collective-permute-start(f32[128]{0:T(128)S(1)} %fusion.91), channel_id=1, source_target_pairs={{0,4},{4,8},{8,12},{12,16},{16,20},{20,24},{24,28},{28,32},{32,36}... | collective-permute-start | bytes 1544 | tf_op jit(solution)/shard_map/while/body/eval_jaxpr/ppermute | solution.py:12
  521.6 8.2 %collective-permute-start = (f32[128]{0:T(128)S(1)}, f32[128]{0:T(128)S(1)}, u32[]{:S(2)}, u32[]{:S(2)}) collective-permute-start(f32[128]{0:T(128)S(1)} %fusion.91), channel_id=1, source_target_pairs={{0,4},{4,8},{8,12},{12,16},{16,20},{20,24},{24,28},{28,32},{32,36}... | collective-permute-start | bytes 1544 | tf_op jit(solution)/shard_map/while/body/eval_jaxpr/ppermute | solution.py:12
  530.0 8.2 %collective-permute-start = (f32[128]{0:T(128)S(1)}, f32[128]{0:T(128)S(1)}, u32[]{:S(2)}, u32[]{:S(2)}) collective-permute-start(f32[128]{0:T(128)S(1)} %fusion.91), channel_id=1, source_target_pairs={{0,4},{4,8},{8,12},{12,16},{16,20},{20,24},{24,28},{28,32},{32,36}... | collective-permute-start | bytes 1544 | tf_op jit(solution)/shard_map/while/body/eval_jaxpr/ppermute | solution.py:12
  546.8 8.2 %collective-permute-start = (f32[128]{0:T(128)S(1)}, f32[128]{0:T(128)S(1)}, u32[]{:S(2)}, u32[]{:S(2)}) collective-permute-start(f32[128]{0:T(128)S(1)} %fusion.91), channel_id=1, source_target_pairs={{0,4},{4,8},{8,12},{12,16},{16,20},{20,24},{24,28},{28,32},{32,36}... | collective-permute-start | bytes 1544 | tf_op jit(solution)/shard_map/while/body/eval_jaxpr/ppermute | solution.py:12
  555.2 8.2 %collective-permute-start = (f32[128]{0:T(128)S(1)}, f32[128]{0:T(128)S(1)}, u32[]{:S(2)}, u32[]{:S(2)}) collective-permute-start(f32[128]{0:T(128)S(1)} %fusion.91), channel_id=1, source_target_pairs={{0,4},{4,8},{8,12},{12,16},{16,20},{20,24},{24,28},{28,32},{32,36}... | collective-permute-start | bytes 1544 | tf_op jit(solution)/shard_map/while/body/eval_jaxpr/ppermute | solution.py:12
  563.6 8.2 %collective-permute-start = (f32[128]{0:T(128)S(1)}, f32[128]{0:T(128)S(1)}, u32[]{:S(2)}, u32[]{:S(2)}) collective-permute-start(f32[128]{0:T(128)S(1)} %fusion.91), channel_id=1, source_target_pairs={{0,4},{4,8},{8,12},{12,16},{16,20},{20,24},{24,28},{28,32},{32,36}... | collective-permute-start | bytes 1544 | tf_op jit(solution)/shard_map/while/body/eval_jaxpr/ppermute | solution.py:12
  580.4 8.2 %collective-permute-start = (f32[128]{0:T(128)S(1)}, f32[128]{0:T(128)S(1)}, u32[]{:S(2)}, u32[]{:S(2)}) collective-permute-start(f32[128]{0:T(128)S(1)} %fusion.91), channel_id=1, source_target_pairs={{0,4},{4,8},{8,12},{12,16},{16,20},{20,24},{24,28},{28,32},{32,36}... | collective-permute-start | bytes 1544 | tf_op jit(solution)/shard_map/while/body/eval_jaxpr/ppermute | solution.py:12
  588.8 8.2 %collective-permute-start = (f32[128]{0:T(128)S(1)}, f32[128]{0:T(128)S(1)}, u32[]{:S(2)}, u32[]{:S(2)}) collective-permute-start(f32[128]{0:T(128)S(1)} %fusion.91), channel_id=1, source_target_pairs={{0,4},{4,8},{8,12},{12,16},{16,20},{20,24},{24,28},{28,32},{32,36}... | collective-permute-start | bytes 1544 | tf_op jit(solution)/shard_map/while/body/eval_jaxpr/ppermute | solution.py:12
  597.2 8.2 %collective-permute-start = (f32[128]{0:T(128)S(1)}, f32[128]{0:T(128)S(1)}, u32[]{:S(2)}, u32[]{:S(2)}) collective-permute-start(f32[128]{0:T(128)S(1)} %fusion.91), channel_id=1, source_target_pairs={{0,4},{4,8},{8,12},{12,16},{16,20},{20,24},{24,28},{28,32},{32,36}... | collective-permute-start | bytes 1544 | tf_op jit(solution)/shard_map/while/body/eval_jaxpr/ppermute | solution.py:12
  614.0 8.2 %collective-permute-start = (f32[128]{0:T(128)S(1)}, f32[128]{0:T(128)S(1)}, u32[]{:S(2)}, u32[]{:S(2)}) collective-permute-start(f32[128]{0:T(128)S(1)} %fusion.91), channel_id=1, source_target_pairs={{0,4},{4,8},{8,12},{12,16},{16,20},{20,24},{24,28},{28,32},{32,36}... | collective-permute-start | bytes 1544 | tf_op jit(solution)/shard_map/while/body/eval_jaxpr/ppermute | solution.py:12
  (23 other events, 759.6 us)
Sparse Core Ops, SparseCore 0:
  70.9 46.8 all-reduce.17
where the time goes:
time: 670 us; the launch traced here: 667 us
  waiting for transfers between devices  487 us (73%)
  starting transfers between devices  134 us (20%)
  matrix products  22.3 us (3%)
  between operations  13.8 us (2%)
    ppermute x63, waiting for transfers between devices, from_behind(): return lax.ppermute(block, axis, route)  393 us
    ppermute x63, starting transfers between devices, from_behind(): return lax.ppermute(block, axis, route)  123 us
    psum x1, waiting for transfers between devices, on_device(): combined = lax.psum(combined, 'sensor')  47 us
    all_to_all x1, waiting for transfers between devices, on_device(): lax.all_to_all(observations, 'tm', split_axis=1, concat_axis=0, tiled=True)  46.3 us
  transfers between devices with their start and end apart: 65, of which 65 were waited for; matrix products, arithmetic and copies ran while one was open for 0% of the time, Pallas kernels for 0%

commit v1 on v0

v1 whole, which is shorter than its diff:
```python
import jax
import jax.numpy as jnp
import numpy as np
from jax import lax
from jax.sharding import Mesh, PartitionSpec as P

NZ, NY, NC, NX = 8, 4, 2, 4
BLOCK_AXES = ("y", "c")
HIGHEST = lax.Precision.HIGHEST


def dot(a, b):
    return jnp.dot(a, b, precision=HIGHEST)


def xor_over_x(block, distance):
    return lax.ppermute(block, "x", [(i, i ^ distance) for i in range(NX)])


def sum_over_x(block):
    first, second, third = (xor_over_x(block, d) for d in (1, 2, 3))
    return (block + first) + (second + third)


def in_order_of_x(blocks, x):
    stacked = jnp.stack(blocks)
    return jnp.stack([lax.dynamic_index_in_dim(stacked, g ^ x, 0, False) for g in range(NX)])


def rows_to_block(piece, distance):
    route = []
    for z in range(NZ):
        for x in range(NX):
            part = 2 * (x // 2) + z % 2
            route.append((z * NX + x, (z // 2 * 2 + x % 2) * NX + (part ^ distance)))
    return lax.ppermute(piece, ("z", "x"), route)


def on_device(observations, sensor_map, noise_precision, availability, decay_rate, prior_mean):
    modes = sensor_map.shape[1]
    sblk = noise_precision.shape[1]
    rows = observations.shape[0]
    z, y, c, x = (lax.axis_index(a) for a in "zycx")
    place = y * NC + c

    sent = observations.reshape(rows, NZ // 2, 2, NY, NC, 2, 128)
    sent = sent.transpose(3, 4, 5, 2, 0, 1, 6).reshape(NY * NC * NX, rows, NZ // 2 * 128)
    received = lax.all_to_all(sent, ("y", "c", "x"), split_axis=0, concat_axis=0, tiled=True)

    weighted = jnp.einsum(
        "bij,bjm->bim",
        noise_precision,
        sensor_map.reshape(-1, sblk, modes),
        preferred_element_type=jnp.float32,
    ).astype(jnp.bfloat16)
    kept = availability[0].astype(jnp.bfloat16)
    masked_own = (weighted * kept[:, None, None]).reshape(-1, modes)
    contract = (((0,), (0,)), ((), ()))
    info_matrix = sum_over_x(
        lax.dot_general(sensor_map, masked_own, contract, preferred_element_type=jnp.float32)
    )

    kept_plane = lax.all_to_all(kept.reshape(NZ, -1), "z", split_axis=0, concat_axis=0, tiled=True)
    plane = lax.dynamic_slice_in_dim(weighted.reshape(-1, modes), z * NY * sblk, NY * sblk)
    label = jnp.zeros((16, modes), jnp.bfloat16).at[:NZ, :NY].set(kept_plane)
    packet = jnp.concatenate([plane, label], 0)
    packets = in_order_of_x([packet] + [xor_over_x(packet, d) for d in (1, 2, 3)], x)
    plane = packets[:, : NY * sblk].reshape(NX, NY, NC, rows, modes).transpose(1, 2, 0, 3, 4)
    kept_all = packets[:, NY * sblk : NY * sblk + NZ, :NY].reshape(NX, NZ // 2, 2, NY)
    kept_all = lax.dynamic_index_in_dim(kept_all, x % 2, 2, False)
    masked = plane[None] * kept_all.transpose(1, 2, 0)[:, :, None, :, None, None]
    masked = masked.reshape(NZ // 2, -1, modes)

    retain = jnp.exp(-decay_rate)
    identity = jnp.eye(modes, dtype=jnp.float32)
    transition = (identity - decay_rate[:, None] * info_matrix) * retain[None, :]
    powers = [transition]
    for _ in range(8):
        powers.append(dot(powers[-1], powers[-1]))
    blocks = lax.all_gather(powers[8], BLOCK_AXES)
    suffix, own_suffix = identity, identity
    for j in reversed(range(NY * NC)):
        own_suffix = jnp.where(place == j, suffix, own_suffix)
        suffix = dot(suffix, blocks[j])
    plane_product = suffix
    planes = lax.all_gather(plane_product, "z")
    lead, within = identity, []
    for j in reversed(range(NY * NC)):
        before = j < place
        within.append(jnp.where(before, lead, 0.0))
        lead = jnp.where(before, dot(lead, blocks[j]), lead)
    across = []
    for j in reversed(range(NZ)):
        before = j < z
        across.append(jnp.where(before, lead, 0.0))
        lead = jnp.where(before, dot(lead, planes[j]), lead)
    to_entry = jnp.concatenate(across[::-1] + within[::-1], 1)
    from_prior = dot(lead, prior_mean)

    partial = jnp.einsum(
        "kmt,mkn->mtn",
        received.reshape(-1, NZ // 2, 128),
        masked,
        preferred_element_type=jnp.float32,
    )
    partial = partial.reshape(NZ, -1, modes)
    piece = jnp.sum(lax.all_to_all(partial, "z", split_axis=0, concat_axis=0, tiled=True), 0)
    pieces = in_order_of_x([rows_to_block(piece, d) for d in range(NX)], x)
    drive = decay_rate[None, :] * pieces.reshape(-1, modes)

    tail = drive
    for level in range(8):
        tail = tail.reshape(-1, 2, modes)
        tail = dot(tail[:, 0], powers[level].T) + tail[:, 1]
    offset = tail[0]
    onward = dot(own_suffix, offset)
    same_plane = (jnp.arange(NZ) == z)[:, None, None]
    sends = jnp.broadcast_to(
        jnp.where(same_plane, offset[None, None], onward[None, None]), (NZ, NY * NC, modes)
    ).reshape(-1, modes)
    offsets = lax.all_to_all(sends, ("z", "y", "c"), split_axis=0, concat_axis=0, tiled=True)
    offsets = offsets.reshape(NZ, NY * NC, modes)
    own_plane = lax.dynamic_index_in_dim(offsets, z, 0, False)
    vector = jnp.concatenate([jnp.sum(offsets, 1).reshape(-1), own_plane.reshape(-1)])
    entry = from_prior + dot(to_entry, vector)

    swept = drive
    for level in range(8):
        shift = 2**level
        moved = dot(swept[:-shift], powers[level].T)
        swept = swept + jnp.pad(moved, ((shift, 0), (0, 0)))
    grown = dot(entry[None, :], transition.T)
    for level in range(8):
        grown = jnp.concatenate([grown, dot(grown, powers[level].T)], 0)
    return swept + grown


def solution(mesh):
    fine = Mesh(mesh.devices.reshape(NZ, NY, NC, NX), ("z", "y", "c", "x"))
    return jax.shard_map(
        on_device,
        mesh=fine,
        in_specs=(
            P(("x", "z", "y", "c"), None),
            P("x", None),
            P("x", None, None),
            P(("z", "y", "c"), "x"),
            P(),
            P(),
        ),
        out_specs=P(("z", "y", "c"), None),
        check_vma=False,
    )
```

time: 670 us -> 170 us (0.25)
  the two profiles are of different devices: /device:TPU:128 before, /device:TPU:1 now
where the time goes in v1:
time: 170 us
  starting transfers between devices  52.5 us (31%)
  blocking collectives  48.3 us (28%)
  matrix products  24.1 us (14%)
  waiting for transfers between devices  21.3 us (13%)
  local copies, waits for them, and re-layouts  18.8 us (11%)
  other arithmetic  3.56 us (2%)
    all_gather x1, blocking collectives, on_device(): blocks = lax.all_gather(powers[8], BLOCK_AXES)  27.3 us
    all_gather x1, blocking collectives, on_device(): planes = lax.all_gather(plane_product, 'z')  21 us
    dot_general x59, matrix products, dot(): return jnp.dot(a, b, precision=HIGHEST)  16 us
    all_to_all x1, starting transfers between devices, on_device(): lax.all_to_all(sends, ('z', 'y', 'c'), split_axis=0, concat_axis=0, tiled...  14.4 us
    all_to_all x1, waiting for transfers between devices, on_device(): lax.all_to_all(sends, ('z', 'y', 'c'), split_axis=0, concat_axis=0, tiled...  9.14 us
    all_to_all x1, starting transfers between devices, on_device(): lax.all_to_all(sent, ('y', 'c', 'x'), split_axis=0, concat_axis=0, tiled=...  8.63 us
    ppermute x6, starting transfers between devices, xor_over_x(): return lax.ppermute(block, 'x', [(i, i ^ distance) for i in range(NX)])  8.59 us
    all_to_all x1, starting transfers between devices, on_device(): lax.all_to_all(kept.reshape(NZ, -1), 'z', split_axis=0, concat_axis=0, ti...  8.34 us
  transfers between devices with their start and end apart: 14, of which 4 were waited for; matrix products, arithmetic and copies ran while one was open for 14% of the time, Pallas kernels for 0%

profile of v1, /device:TPU:1, one launch (start us, length us, event | category | flops | bytes accessed | tf_op | source)
XLA Modules:
  0.0 169.7 jit_solution(12504357652959716501)
XLA Ops:
  0.0 0.7 convert_bitcast_fusion
  0.8 0.5 copy-done
  1.2 2.6 %broadcast_multiply_fusion = (bf16[32,128,128]{2,1,0:T(8,128)(2,1)S(1)}, bf16[32,128,128]{2,1,0:T(8,128)(2,1)}) fusion(bf16[32]{0:T(256)(128)(2,1)S(1)} %convert_bitcast_fusion, bf16[32,128,128]{2,1,0:T(8,128)(2,1)} %param.10, bf16[32,128,128]{2,1,0:T(8,128)(2,1)S(1)} %bitcast.196), kind=kOutput, calls=%fused_computation.39 | convolution fusion | flops 135266304 | bytes 4194368 | tf_op jit(solution)/shard_map/bij,bjm->bim/dot_general | solution.py:50
  3.9 0.5 convolution_bitcast_fusion
  4.4 2.1 %collective-permute-start.7 = (f32[128,128]{0,1:T(8,128)S(1)}, f32[128,128]{0,1:T(8,128)S(1)}, u32[]{:S(2)}, u32[]{:S(2)}) collective-permute-start(f32[128,128]{0,1:T(8,128)S(1)} %convolution_bitcast_fusion), channel_id=1, source_target_pairs={{0,1},{1,0},{2,3},{3,2},{4,5},{5,4},{6,7},{7,6},{8,9},{9,8},{10,11... | collective-permute-start | bytes 196616 | tf_op jit(solution)/shard_map/ppermute | solution.py:17
  6.5 2.5 %collective-permute-start.8 = (f32[128,128]{0,1:T(8,128)S(1)}, f32[128,128]{0,1:T(8,128)S(1)}, u32[]{:S(2)}, u32[]{:S(2)}) collective-permute-start(f32[128,128]{0,1:T(8,128)S(1)} %convolution_bitcast_fusion), channel_id=1, source_target_pairs={{0,2},{1,3},{2,0},{3,1},{4,6},{5,7},{6,4},{7,5},{8,10},{9,11},{10,... | collective-permute-start | bytes 196616 | tf_op jit(solution)/shard_map/ppermute | solution.py:17
  9.0 0.7 convert_element_type.54
  9.7 8.3 %all-to-all-start = ((bf16[8,1,4]{2,1,0:T(2,128)(2,1)}), bf16[8,1,4]{2,1,0:T(2,128)(2,1)S(1)}, u32[]{:S(2)}, u32[]{:S(2)}) async-start(bf16[8,1,4]{2,1,0:T(2,128)(2,1)} %convert_element_type.54), calls=%async_computation | async-start | bytes 8192 | tf_op jit(solution)/shard_map/all_to_all | solution.py:63
  18.0 0.6 iota_compare_fusion.4
  18.6 2.7 %reshape.200 = bf16[64,4,2,4,2,2,128]{6,5,4,3,2,1,0:T(2,128)(2,1)} reshape(bf16[64,16384]{1,0:T(8,128)(2,1)S(1)} %copy-done.6) | data formatting | bytes 4194304 | tf_op jit(solution)/shard_map/reshape | solution.py:46
  21.4 2.7 %copy.66 = bf16[4,2,2,2,64,4,128]{6,5,4,3,2,1,0:T(4,128)(2,1)S(1)} copy(bf16[4,2,2,2,64,4,128]{6,2,1,0,3,5,4:T(2,128)(2,1)} %bitcast.197) | data formatting | bytes 4194304 | tf_op jit(solution)/shard_map/transpose | solution.py:47
  24.0 2.2 %reshape.201 = bf16[32,64,512]{2,1,0:T(8,128)(2,1)} reshape(bf16[4,2,2,2,64,4,128]{6,5,4,3,2,1,0:T(4,128)(2,1)S(1)} %copy.66) | data formatting | bytes 4194304 | tf_op jit(solution)/shard_map/reshape | solution.py:47
  26.3 0.9 constant_dynamic-slice_fusion.9
  27.2 8.6 %all-to-all-start.1 = ((bf16[32,64,512]{2,1,0:T(8,128)(2,1)}), bf16[32,64,512]{2,1,0:T(8,128)(2,1)S(1)}, u32[]{:S(2)}, u32[]{:S(2)}) async-start(bf16[32,64,512]{2,1,0:T(8,128)(2,1)} %reshape.201), calls=%async_computation.1 | async-start | bytes 4194304 | tf_op jit(solution)/shard_map/all_to_all | solution.py:48
  36.1 1.5 collective-permute-start
  37.6 2.4 %collective-permute-start.1 = (bf16[528,128]{1,0:T(8,128)(2,1)S(1)}, bf16[528,128]{1,0:T(8,128)(2,1)S(1)}, u32[]{:S(2)}, u32[]{:S(2)}) collective-permute-start(bf16[528,128]{1,0:T(8,128)(2,1)S(1)} %get-tuple-element.22), channel_id=1, source_target_pairs={{0,2},{1,3},{2,0},{3,1},{4,6},{5,7},{6,4},{7,5},{8,10},{9,11},{10,... | collective-permute-start | bytes 405512 | tf_op jit(solution)/shard_map/ppermute | solution.py:17
  40.1 0.9 fusion.25
  41.5 0.6 copy-done.1
  43.4 27.3 %all-gather = f32[1024,128]{1,0:T(8,128)S(1)} all-gather(f32[128,128]{1,0:T(8,128)S(1)} %fusion.116), channel_id=2, replica_groups=mesh['z'=8,'y'=4,'c'=2,'x'=4] {'y','c'}, dimensions={0}, use_global_device_ids=true | all-gather | bytes 589824 | tf_op jit(solution)/shard_map/all_gather | solution.py:80
  72.7 0.6 copy-done.21
  73.6 21.0 %all-gather.1 = f32[1024,128]{1,0:T(8,128)S(1)} all-gather(f32[128,128]{1,0:T(8,128)S(1)} %fusion.47), channel_id=3, replica_groups=mesh['z'=8,'y'=4,'c'=2,'x'=4] {'z'}, dimensions={0}, use_global_device_ids=true | all-gather | bytes 589824 | tf_op jit(solution)/shard_map/all_gather | solution.py:86
  95.8 0.3 convolution_select_fusion.10
  96.1 0.3 convolution_select_fusion.9
  96.4 0.3 convolution_select_fusion.8
  96.7 0.3 convolution_select_fusion.7
  97.0 0.3 convolution_select_fusion.6
  98.5 0.9 select_dynamic-update-slice_fusion.14
  99.6 0.9 copy-done.9
  100.8 0.8 copy.64
  101.8 0.7 mul.68
  102.5 0.9 mul.69
  103.3 2.1 %reshape.202 = bf16[2048,4,128]{2,1,0:T(4,128)(2,1)} reshape(bf16[32,64,512]{2,1,0:T(8,128)(2,1)S(1)} %all-to-all-done.1) | data formatting | bytes 4194304 | tf_op jit(solution)/shard_map/reshape | solution.py:102
  105.5 5.0 %fusion = f32[4,128,128]{1,2,0:T(8,128)} fusion(bf16[2048,4,128]{2,1,0:T(4,128)(2,1)} %reshape.202, bf16[4,2048]{1,0:T(4,128)(2,1)S(1)} %mul.69, bf16[2048,128]{1,0:T(8,128)(2,1)} %bitcast.202), kind=kOutput, calls=%fused_computation | convolution fusion | flops 272629760 | bytes 2899968 | tf_op jit(solution)/shard_map/kmt,mkn->mtn/dot_general | solution.py:100
  110.4 5.9 %all-to-all-start.2 = ((f32[8,64,128]{2,1,0:T(8,128)}), f32[8,64,128]{2,1,0:T(8,128)S(1)}, u32[]{:S(2)}, u32[]{:S(2)}) async-start(f32[8,64,128]{2,1,0:T(8,128)} %bitcast.204), calls=%async_computation.2 | async-start | bytes 524288 | tf_op jit(solution)/shard_map/all_to_all | solution.py:107
  116.4 1.1 convolution_select_fusion
  117.6 8.1 %all-to-all-done.2 = f32[8,64,128]{2,1,0:T(8,128)S(1)} async-done(((f32[8,64,128]{2,1,0:T(8,128)}), f32[8,64,128]{2,1,0:T(8,128)S(1)}, u32[]{:S(2)}, u32[]{:S(2)}) %all-to-all-start.2) | async-done | bytes 262176 | tf_op jit(solution)/shard_map/all_to_all | solution.py:107
  125.7 0.7 collective-permute-start.3
  126.4 2.8 %collective-permute-start.4 = (f32[64,128]{1,0:T(8,128)S(1)}, f32[64,128]{1,0:T(8,128)S(1)}, u32[]{:S(2)}, u32[]{:S(2)}) collective-permute-start(f32[64,128]{1,0:T(8,128)S(1)} %reduce_sum.18), channel_id=1, source_target_pairs={{0,1},{1,33},{2,3},{3,35},{32,0},{33,32},{34,2},{35,34},{64,65},{6... | collective-permute-start | bytes 98312 | tf_op jit(solution)/shard_map/ppermute | solution.py:36
  129.2 2.7 %collective-permute-start.5 = (f32[64,128]{1,0:T(8,128)S(1)}, f32[64,128]{1,0:T(8,128)S(1)}, u32[]{:S(2)}, u32[]{:S(2)}) collective-permute-start(f32[64,128]{1,0:T(8,128)S(1)} %reduce_sum.18), channel_id=1, source_target_pairs={{0,2},{1,34},{2,0},{3,32},{32,3},{33,35},{34,1},{35,33},{64,66},{6... | collective-permute-start | bytes 98312 | tf_op jit(solution)/shard_map/ppermute | solution.py:36
  131.8 0.5 collective-permute-start.6
  133.0 0.5 collective-permute-done.5
  133.5 3.5 %collective-permute-done.6 = f32[64,128]{1,0:T(8,128)S(1)} collective-permute-done((f32[64,128]{1,0:T(8,128)S(1)}, f32[64,128]{1,0:T(8,128)S(1)}, u32[]{:S(2)}, u32[]{:S(2)}) %collective-permute-start.6) | collective-permute-done | bytes 32800 | tf_op jit(solution)/shard_map/ppermute | solution.py:36
  138.0 0.4 fusion.17
  141.6 0.6 broadcast_in_dim.62
  142.2 14.4 %all-to-all-start.3 = ((f32[64,1,128]{2,1,0:T(1,128)}), f32[64,1,128]{2,1,0:T(1,128)S(1)}, u32[]{:S(2)}, u32[]{:S(2)}) async-start(f32[64,1,128]{2,1,0:T(1,128)} %bitcast.53), calls=%async_computation.3 | async-start | bytes 65536 | tf_op jit(solution)/shard_map/all_to_all | solution.py:121
  156.9 9.1 %all-to-all-done.3 = f32[64,1,128]{2,1,0:T(1,128)S(1)} async-done(((f32[64,1,128]{2,1,0:T(1,128)}), f32[64,1,128]{2,1,0:T(1,128)S(1)}, u32[]{:S(2)}, u32[]{:S(2)}) %all-to-all-start.3) | async-done | bytes 32800 | tf_op jit(solution)/shard_map/all_to_all | solution.py:121
  166.0 0.7 convolution_bitcast_fusion.1
  169.0 0.7 add_add_fusion
  (181 shorter events, 14.2 us)
Async XLA Ops:
  0.0 1.2 copy-start
  3.9 5.1 %copy-start.30 = (s32[1,32]{1,0:T(1,128)S(1)}, s32[1,32]{1,0:T(1,128)}, u32[]{:S(2)}) copy-start(s32[1,32]{1,0:T(1,128)} %param.11) | copy-start | bytes 388
  3.9 14.8 %copy-start.6 = (bf16[64,16384]{1,0:T(8,128)(2,1)S(1)}, bf16[64,16384]{1,0:T(8,128)(2,1)}, u32[]{:S(2)}) copy-start(bf16[64,16384]{1,0:T(8,128)(2,1)} %param.8) | copy-start | bytes 6291460
  4.4 35.6 %collective-permute-start.7 = (f32[128,128]{0,1:T(8,128)S(1)}, f32[128,128]{0,1:T(8,128)S(1)}, u32[]{:S(2)}, u32[]{:S(2)}) collective-permute-start(f32[128,128]{0,1:T(8,128)S(1)} %convolution_bitcast_fusion), channel_id=1, source_target_pairs={{0,1},{1,0},{2,3},{3,2},{4,5},{5,4},{6,7},{7,6},{8,9},{9,8},{10,11... | collective-permute-start | bytes 196616 | tf_op jit(solution)/shard_map/ppermute | solution.py:17
  6.5 33.6 %collective-permute-start.8 = (f32[128,128]{0,1:T(8,128)S(1)}, f32[128,128]{0,1:T(8,128)S(1)}, u32[]{:S(2)}, u32[]{:S(2)}) collective-permute-start(f32[128,128]{0,1:T(8,128)S(1)} %convolution_bitcast_fusion), channel_id=1, source_target_pairs={{0,2},{1,3},{2,0},{3,1},{4,6},{5,7},{6,4},{7,5},{8,10},{9,11},{10,... | collective-permute-start | bytes 196616 | tf_op jit(solution)/shard_map/ppermute | solution.py:17
  8.9 31.1 %collective-permute-start.9 = (f32[128,128]{0,1:T(8,128)S(1)}, f32[128,128]{0,1:T(8,128)}, u32[]{:S(2)}, u32[]{:S(2)}) collective-permute-start(f32[128,128]{0,1:T(8,128)S(1)} %convolution_bitcast_fusion), channel_id=1, source_target_pairs={{0,3},{1,2},{2,1},{3,0},{4,7},{5,6},{6,5},{7,4},{8,11},{9,10},{10,... | collective-permute-start | bytes 196616 | tf_op jit(solution)/shard_map/ppermute | solution.py:17
  9.7 17.5 %all-to-all-start = ((bf16[8,1,4]{2,1,0:T(2,128)(2,1)}), bf16[8,1,4]{2,1,0:T(2,128)(2,1)S(1)}, u32[]{:S(2)}, u32[]{:S(2)}) async-start(bf16[8,1,4]{2,1,0:T(2,128)(2,1)} %convert_element_type.54), calls=%async_computation | async-start | bytes 8192 | tf_op jit(solution)/shard_map/all_to_all | solution.py:63
  24.0 2.3 %copy-start.26 = (f32[128]{0:T(128)S(1)}, f32[128]{0:T(128)}, u32[]{:S(2)}) copy-start(f32[128]{0:T(128)} %param.12) | copy-start | bytes 1540
  27.2 76.1 %all-to-all-start.1 = ((bf16[32,64,512]{2,1,0:T(8,128)(2,1)}), bf16[32,64,512]{2,1,0:T(8,128)(2,1)S(1)}, u32[]{:S(2)}, u32[]{:S(2)}) async-start(bf16[32,64,512]{2,1,0:T(8,128)(2,1)} %reshape.201), calls=%async_computation.1 | async-start | bytes 4194304 | tf_op jit(solution)/shard_map/all_to_all | solution.py:48
  36.1 63.5 %collective-permute-start = (bf16[528,128]{1,0:T(8,128)(2,1)S(1)}, bf16[528,128]{1,0:T(8,128)(2,1)S(1)}, u32[]{:S(2)}, u32[]{:S(2)}) collective-permute-start(bf16[528,128]{1,0:T(8,128)(2,1)S(1)} %get-tuple-element.22), channel_id=1, source_target_pairs={{0,1},{1,0},{2,3},{3,2},{4,5},{5,4},{6,7},{7,6},{8,9},{9,8},{10,11... | collective-permute-start | bytes 405512 | tf_op jit(solution)/shard_map/ppermute | solution.py:17
  37.6 62.0 %collective-permute-start.1 = (bf16[528,128]{1,0:T(8,128)(2,1)S(1)}, bf16[528,128]{1,0:T(8,128)(2,1)S(1)}, u32[]{:S(2)}, u32[]{:S(2)}) collective-permute-start(bf16[528,128]{1,0:T(8,128)(2,1)S(1)} %get-tuple-element.22), channel_id=1, source_target_pairs={{0,2},{1,3},{2,0},{3,1},{4,6},{5,7},{6,4},{7,5},{8,10},{9,11},{10,... | collective-permute-start | bytes 405512 | tf_op jit(solution)/shard_map/ppermute | solution.py:17
  40.0 59.7 %collective-permute-start.2 = (bf16[528,128]{1,0:T(8,128)(2,1)S(1)}, bf16[528,128]{1,0:T(8,128)(2,1)S(1)}, u32[]{:S(2)}, u32[]{:S(2)}) collective-permute-start(bf16[528,128]{1,0:T(8,128)(2,1)S(1)} %get-tuple-element.22), channel_id=1, source_target_pairs={{0,3},{1,2},{2,1},{3,0},{4,7},{5,6},{6,5},{7,4},{8,11},{9,10},{10,... | collective-permute-start | bytes 405512 | tf_op jit(solution)/shard_map/ppermute | solution.py:17
  41.3 1.9 %copy-start.3 = (f32[128,128]{1,0:T(8,128)}, f32[128,128]{1,0:T(8,128)S(1)}, u32[]{:S(2)}) copy-start(f32[128,128]{1,0:T(8,128)S(1)} %fusion.109) | copy-start | bytes 196612
  41.5 0.6 copy-start.1
  70.9 27.2 %copy-start.7 = (f32[128,128]{0,1:T(8,128)}, f32[128,128]{0,1:T(8,128)S(1)}, u32[]{:S(2)}) copy-start(f32[128,128]{0,1:T(8,128)S(1)} %fusion.42) | copy-start | bytes 196612
  71.2 1.1 copy-start.11
  71.5 0.9 copy-start.13
  71.7 0.7 copy-start.15
  71.9 0.6 copy-start.17
  72.1 0.6 copy-start.19
  72.7 0.6 copy-start.21
  94.6 5.0 %copy-start.5 = (f32[1024,128]{1,0:T(8,128)}, f32[1024,128]{1,0:T(8,128)S(1)}, u32[]{:S(2)}) copy-start(f32[1024,128]{1,0:T(8,128)S(1)} %all-gather.1) | copy-start | bytes 1572868
  94.9 3.3 %copy-start.23 = (f32[128,128]{0,1:T(8,128)}, f32[128,128]{0,1:T(8,128)S(1)}, u32[]{:S(2)}) copy-start(f32[128,128]{0,1:T(8,128)S(1)} %convolution_select_fusion.14) | copy-start | bytes 196612
  99.6 1.0 copy-start.9
  105.4 11.0 %copy-start.10 = (f32[128,2048]{0,1:T(8,128)S(1)}, f32[128,2048]{0,1:T(8,128)}, u32[]{:S(2)}) copy-start(f32[128,2048]{0,1:T(8,128)} %copy-done.9) | copy-start | bytes 3145732
  105.4 11.0 %copy-start.24 = (f32[128,128]{0,1:T(8,128)S(1)}, f32[128,128]{0,1:T(8,128)}, u32[]{:S(2)}) copy-start(f32[128,128]{0,1:T(8,128)} %copy-done.23) | copy-start | bytes 196612
  105.4 11.0 %copy-start.8 = (f32[128,128]{0,1:T(8,128)S(1)}, f32[128,128]{0,1:T(8,128)}, u32[]{:S(2)}) copy-start(f32[128,128]{0,1:T(8,128)} %copy-done.7) | copy-start | bytes 196612
  105.4 11.0 %copy-start.25 = (f32[128,128]{0,1:T(8,128)S(1)}, f32[128,128]{0,1:T(8,128)}, u32[]{:S(2)}) copy-start(f32[128,128]{0,1:T(8,128)} %get-tuple-element.42) | copy-start | bytes 196612
  105.4 27.0 %copy-start.22 = (f32[128,128]{1,0:T(8,128)S(1)}, f32[128,128]{1,0:T(8,128)}, u32[]{:S(2)}) copy-start(f32[128,128]{1,0:T(8,128)} %copy-done.21) | copy-start | bytes 196612
  105.4 27.1 %copy-start.20 = (f32[128,128]{1,0:T(8,128)S(1)}, f32[128,128]{1,0:T(8,128)}, u32[]{:S(2)}) copy-start(f32[128,128]{1,0:T(8,128)} %copy-done.19) | copy-start | bytes 196612
  105.4 27.2 %copy-start.18 = (f32[128,128]{1,0:T(8,128)S(1)}, f32[128,128]{1,0:T(8,128)}, u32[]{:S(2)}) copy-start(f32[128,128]{1,0:T(8,128)} %copy-done.17) | copy-start | bytes 196612
  105.4 27.3 %copy-start.16 = (f32[128,128]{1,0:T(8,128)S(1)}, f32[128,128]{1,0:T(8,128)}, u32[]{:S(2)}) copy-start(f32[128,128]{1,0:T(8,128)} %copy-done.15) | copy-start | bytes 196612
  105.4 27.4 %copy-start.14 = (f32[128,128]{1,0:T(8,128)S(1)}, f32[128,128]{1,0:T(8,128)}, u32[]{:S(2)}) copy-start(f32[128,128]{1,0:T(8,128)} %copy-done.13) | copy-start | bytes 196612
  105.4 27.5 %copy-start.12 = (f32[128,128]{1,0:T(8,128)S(1)}, f32[128,128]{1,0:T(8,128)}, u32[]{:S(2)}) copy-start(f32[128,128]{1,0:T(8,128)} %copy-done.11) | copy-start | bytes 196612
  110.4 26.7 %copy-start.27 = (f32[128]{0:T(128)S(1)}, f32[128]{0:T(128)}, u32[]{:S(2)}) copy-start(f32[128]{0:T(128)} %param.12) | copy-start | bytes 1540
  110.4 27.0 %copy-start.4 = (f32[128,128]{1,0:T(8,128)S(1)}, f32[128,128]{1,0:T(8,128)}, u32[]{:S(2)}) copy-start(f32[128,128]{1,0:T(8,128)} %copy-done.3) | copy-start | bytes 196612
  110.4 15.2 %all-to-all-start.2 = ((f32[8,64,128]{2,1,0:T(8,128)}), f32[8,64,128]{2,1,0:T(8,128)S(1)}, u32[]{:S(2)}, u32[]{:S(2)}) async-start(f32[8,64,128]{2,1,0:T(8,128)} %bitcast.204), calls=%async_computation.2 | async-start | bytes 524288 | tf_op jit(solution)/shard_map/all_to_all | solution.py:107
  116.4 21.4 %copy-start.2 = (f32[128,128]{1,0:T(8,128)S(1)}, f32[128,128]{1,0:T(8,128)}, u32[]{:S(2)}) copy-start(f32[128,128]{1,0:T(8,128)} %copy-done.1) | copy-start | bytes 196612
  125.7 7.3 %collective-permute-start.3 = (f32[64,128]{1,0:T(8,128)S(1)}, f32[64,128]{1,0:T(8,128)S(1)}, u32[]{:S(2)}, u32[]{:S(2)}) collective-permute-start(f32[64,128]{1,0:T(8,128)S(1)} %reduce_sum.18), channel_id=1, source_target_pairs={{0,0},{1,32},{2,2},{3,34},{32,1},{33,33},{34,3},{35,35},{64,64},{6... | collective-permute-start | bytes 98312 | tf_op jit(solution)/shard_map/ppermute | solution.py:36
  126.4 6.7 %collective-permute-start.4 = (f32[64,128]{1,0:T(8,128)S(1)}, f32[64,128]{1,0:T(8,128)S(1)}, u32[]{:S(2)}, u32[]{:S(2)}) collective-permute-start(f32[64,128]{1,0:T(8,128)S(1)} %reduce_sum.18), channel_id=1, source_target_pairs={{0,1},{1,33},{2,3},{3,35},{32,0},{33,32},{34,2},{35,34},{64,65},{6... | collective-permute-start | bytes 98312 | tf_op jit(solution)/shard_map/ppermute | solution.py:36
  129.2 4.3 %collective-permute-start.5 = (f32[64,128]{1,0:T(8,128)S(1)}, f32[64,128]{1,0:T(8,128)S(1)}, u32[]{:S(2)}, u32[]{:S(2)}) collective-permute-start(f32[64,128]{1,0:T(8,128)S(1)} %reduce_sum.18), channel_id=1, source_target_pairs={{0,2},{1,34},{2,0},{3,32},{32,3},{33,35},{34,1},{35,33},{64,66},{6... | collective-permute-start | bytes 98312 | tf_op jit(solution)/shard_map/ppermute | solution.py:36
  131.8 5.2 %collective-permute-start.6 = (f32[64,128]{1,0:T(8,128)S(1)}, f32[64,128]{1,0:T(8,128)S(1)}, u32[]{:S(2)}, u32[]{:S(2)}) collective-permute-start(f32[64,128]{1,0:T(8,128)S(1)} %reduce_sum.18), channel_id=1, source_target_pairs={{0,3},{1,35},{2,1},{3,33},{32,2},{33,34},{34,0},{35,32},{64,67},{6... | collective-permute-start | bytes 98312 | tf_op jit(solution)/shard_map/ppermute | solution.py:36
  138.4 3.1 %copy-start.29 = (pred[8]{0:T(512)(128)(4,1)S(1)}, pred[8]{0:T(512)(128)(4,1)}, u32[]{:S(2)}) copy-start(pred[8]{0:T(512)(128)(4,1)} %iota_compare_fusion.4) | copy-start | bytes 28
  139.0 27.7 %copy-start.28 = (f32[128]{0:T(128)S(1)}, f32[128]{0:T(128)}, u32[]{:S(2)}) copy-start(f32[128]{0:T(128)} %param.13) | copy-start | bytes 1540
  142.2 23.8 %all-to-all-start.3 = ((f32[64,1,128]{2,1,0:T(1,128)}), f32[64,1,128]{2,1,0:T(1,128)S(1)}, u32[]{:S(2)}, u32[]{:S(2)}) async-start(f32[64,1,128]{2,1,0:T(1,128)} %bitcast.53), calls=%async_computation.3 | async-start | bytes 65536 | tf_op jit(solution)/shard_map/all_to_all | solution.py:121

commit v2 on v0

v2 whole, which is shorter than its diff:
```python
import jax
import jax.numpy as jnp
from jax import lax
from jax.experimental import pallas as pl
from jax.experimental.pallas import tpu as pltpu
from jax.sharding import Mesh, PartitionSpec as P

NZ, NY, NC, NX = 8, 4, 2, 4
NK = NZ * NY * NC
STEPS = 256
LEVELS = 8
SCAN = 6
LANES = 128
TAKERS = NY * NC * 2
HIGHEST = lax.Precision.HIGHEST
WHOLE = pl.BlockSpec(memory_space=pltpu.VMEM)
SCALARS = pl.BlockSpec(memory_space=pltpu.SMEM)


def dot(a, b):
    return jnp.dot(a, b, precision=HIGHEST, preferred_element_type=jnp.float32)


def f32(*shape):
    return jax.ShapeDtypeStruct(shape, jnp.float32)


def local(body, name, scalars, arrays, outs, flops, tokens=(), scratch=(), moved=1 << 20):
    inputs = len(scalars) + len(arrays)

    def call(*refs):
        body(*refs[:inputs], *refs[inputs + len(tokens) :])

    return pl.pallas_call(
        call,
        name=name,
        out_shape=outs,
        in_specs=[SCALARS] * len(scalars)
        + [WHOLE] * (len(arrays) + len(tokens)),
        out_specs=[WHOLE] * len(outs),
        scratch_shapes=list(scratch),
        cost_estimate=pl.CostEstimate(flops=flops, bytes_accessed=moved, transcendentals=0),
        compiler_params=pltpu.CompilerParams(vmem_limit_bytes=32 << 20),
    )(*scalars, *arrays, *tokens)


def split(a):
    high = a.astype(jnp.bfloat16)
    return high, (a - high.astype(jnp.float32)).astype(jnp.bfloat16)


def wide(a):
    high, low = split(a)
    return jnp.concatenate([high, low, high], 1)


def tall(a):
    high, low = split(a)
    return jnp.concatenate([high, high, low], 0)


def times(terms, factor):
    return jnp.dot(terms, factor, preferred_element_type=jnp.float32)


def xor_over_x(block, distance):
    return lax.ppermute(block, "x", [(i, i ^ distance) for i in range(NX)])


def rows_to_block(piece, distance):
    route = []
    for z in range(NZ):
        for x in range(NX):
            part = 2 * (x // 2) + z % 2
            route.append((z * NX + x, (z // 2 * 2 + x % 2) * NX + (part ^ distance)))
    return lax.ppermute(piece, ("z", "x"), route)


def order_kernel(rows_ref, *refs):
    out_ref = refs[-1]
    for m in range(NZ // 2):
        for par in range(2):
            for j in range(TAKERS):
                lane = ((m * 2 + par) * TAKERS + j) * LANES
                out_ref[j, par, m] = rows_ref[:, lane : lane + LANES]


def by_taker(observations, *tokens):
    rows = observations.shape[0]
    out = pl.pallas_call(
        order_kernel,
        name="by_taker",
        out_shape=jax.ShapeDtypeStruct((TAKERS, 2, NZ // 2, rows, LANES), jnp.bfloat16),
        in_specs=[WHOLE] * (1 + len(tokens)),
        out_specs=WHOLE,
        cost_estimate=pl.CostEstimate(flops=0, bytes_accessed=4 << 20, transcendentals=0),
        compiler_params=pltpu.CompilerParams(vmem_limit_bytes=32 << 20),
    )(observations, *tokens)
    return out.reshape(TAKERS * 2, NZ // 2 * rows, LANES)


def pack_kernel(kept_ref, noise_ref, map_ref, out_ref, noise_held, map_held, sems):
    first = lax.axis_index("z") * NY + lax.axis_index("c") * 2
    copies = [
        pltpu.make_async_copy(noise_ref.at[pl.ds(first, 2)], noise_held, sems.at[0]),
        pltpu.make_async_copy(map_ref.at[pl.ds(first * LANES, 2 * LANES)], map_held, sems.at[1]),
    ]
    for copy in copies:
        copy.start()
    blocks = kept_ref.shape[1]
    lane = lax.broadcasted_iota(jnp.int32, (16, LANES), 1) - lax.axis_index("x") * blocks
    row = jnp.zeros((16, LANES), jnp.float32)
    for b in range(blocks):
        row = jnp.where(lane == b, kept_ref[0, b].astype(jnp.float32), row)
    out_ref[LANES:, :LANES] = row.astype(jnp.bfloat16)
    out_ref[LANES:, LANES:] = jnp.zeros((16, LANES), jnp.bfloat16)
    for copy in copies:
        copy.wait()
    for b in range(2):
        weights = jnp.dot(
            noise_held[b], map_held[b * LANES : (b + 1) * LANES, :], preferred_element_type=jnp.float32
        )
        out_ref[:LANES, b * LANES : (b + 1) * LANES] = weights.T.astype(jnp.bfloat16)


def pack(availability, noise_precision, sensor_map):
    return pl.pallas_call(
        pack_kernel,
        name="pack",
        out_shape=jax.ShapeDtypeStruct((LANES + 16, 2 * LANES), jnp.bfloat16),
        in_specs=[SCALARS, pl.BlockSpec(memory_space=pl.ANY), pl.BlockSpec(memory_space=pl.ANY)],
        out_specs=WHOLE,
        scratch_shapes=[
            pltpu.VMEM((2, LANES, LANES), jnp.bfloat16),
            pltpu.VMEM((2 * LANES, LANES), jnp.bfloat16),
            pltpu.SemaphoreType.DMA((2,)),
        ],
        cost_estimate=pl.CostEstimate(flops=1 << 23, bytes_accessed=1 << 18, transcendentals=0),
    )(availability, noise_precision, sensor_map)


def gather_kernel(place_ref, own_ref, one_ref, two_ref, three_ref, kept_ref, half_ref):
    refs = (own_ref, one_ref, two_ref, three_ref)
    kept = sum(ref[LANES:, :LANES].astype(jnp.float32)[:NZ] for ref in refs)
    at = lax.broadcasted_iota(jnp.int32, (NZ, LANES), 0)
    kept_ref[...] = jnp.where(at == place_ref[2], kept, 0.0)
    for r, ref in enumerate(refs):
        half_ref[:, 2 * r * LANES : 2 * (r + 1) * LANES] = ref[:LANES]


def weigh_kernel(kept_ref, noise_ref, map_ref, out_ref):
    step = pl.program_id(0)
    blocks, sblk = noise_ref.shape[0], noise_ref.shape[1]
    parts = []
    for b in range(blocks):
        weights = jnp.dot(
            noise_ref[b], map_ref[b * sblk : (b + 1) * sblk, :], preferred_element_type=jnp.float32
        )
        parts.append((weights * kept_ref[0, step * blocks + b].astype(jnp.float32)).astype(jnp.bfloat16))
    share = lax.dot_general(
        jnp.concatenate(parts, 0), map_ref[...], (((0,), (0,)), ((), ())), preferred_element_type=jnp.float32
    )

    @pl.when(step == 0)
    def _():
        out_ref[...] = share

    @pl.when(step > 0)
    def _():
        out_ref[...] += share


def weigh(availability, noise_precision, sensor_map):
    blocks, sblk, _ = noise_precision.shape
    step = blocks // 4
    return pl.pallas_call(
        weigh_kernel,
        name="weigh",
        grid=(4,),
        out_shape=f32(LANES, LANES),
        in_specs=[
            SCALARS,
            pl.BlockSpec((step, sblk, sblk), lambda i: (i, 0, 0)),
            pl.BlockSpec((step * sblk, LANES), lambda i: (i, 0)),
        ],
        out_specs=pl.BlockSpec((LANES, LANES), lambda i: (0, 0)),
        cost_estimate=pl.CostEstimate(flops=4 * blocks * sblk**3, bytes_accessed=2 << 20, transcendentals=0),
    )(availability, noise_precision, sensor_map)


def power_kernel(own_ref, one_ref, two_ref, three_ref, decay_ref, retain_ref, out_ref, block_ref):
    info = (own_ref[...] + one_ref[...]) + (two_ref[...] + three_ref[...])
    row = lax.broadcasted_iota(jnp.int32, info.shape, 0)
    column = lax.broadcasted_iota(jnp.int32, info.shape, 1)
    identity = jnp.where(row == column, 1.0, 0.0)
    power = (identity - decay_ref[...] * info) * retain_ref[...]
    for level in range(LEVELS):
        out_ref[level] = power
        power = dot(power, power)
    block_ref[...] = power


def factor_kernel(power_ref, add_ref, spread_ref):
    for step in range(LEVELS // 2):
        one, two = power_ref[2 * step], power_ref[2 * step + 1]
        for j, power in enumerate((one, two, dot(one, two))):
            terms = tall(power)
            add_ref[step, (2 - j) * 3 * LANES : (3 - j) * 3 * LANES] = terms
            spread_ref[step, :, j * LANES : (j + 1) * LANES] = terms


def joined(upper, total, beside, lead, rest):
    both = dot(jnp.where(upper, beside, total), jnp.where(upper, total, beside))
    new = dot(jnp.where(upper, beside, rest), jnp.where(upper, lead, beside))
    return both, jnp.where(upper, new, lead), jnp.where(upper, rest, new)


def pair_kernel(place_ref, total_ref, got_ref, total_out, lead_out, rest_out, lead_terms, rest_terms):
    row = lax.broadcasted_iota(jnp.int32, (LANES, LANES), 0)
    column = lax.broadcasted_iota(jnp.int32, (LANES, LANES), 1)
    identity = jnp.where(row == column, 1.0, 0.0)
    upper = place_ref[1] % 2 == 1
    total, got = total_ref[...], got_ref[...]
    lead, rest = jnp.where(upper, got, identity), jnp.where(upper, identity, got)
    total_out[...] = dot(jnp.where(upper, got, total), jnp.where(upper, total, got))
    lead_out[...], rest_out[...] = lead, rest
    lead_terms[...], rest_terms[...] = tall(lead), tall(rest)


def quad_kernel(bits_ref, total_ref, one_ref, two_ref, three_ref, lead_ref, rest_ref, total_out, lead_out, rest_out, *terms):
    odd, upper = bits_ref[0] % 2 == 1, bits_ref[0] % 4 >= 2
    two, three = two_ref[...], three_ref[...]
    total, lead, rest = joined(odd, total_ref[...], one_ref[...], lead_ref[...], rest_ref[...])
    terms[0][...], terms[1][...] = tall(lead), tall(rest)
    beside = dot(jnp.where(odd, three, two), jnp.where(odd, two, three))
    total, lead, rest = joined(upper, total, beside, lead, rest)
    terms[2][...], terms[3][...] = tall(lead), tall(rest)
    total_out[...], lead_out[...], rest_out[...] = total, lead, rest


def mask_kernel(place_ref, kept_ref, own_ref, other_ref, plane_ref, mask_ref):
    x, z, c = place_ref[0], place_ref[2], place_ref[3]
    half = NZ // 2
    zs = lax.broadcasted_iota(jnp.int32, (NZ, NZ), 1)
    pick = lax.broadcasted_iota(jnp.int32, (NZ, NZ), 0) * 2 + x % 2
    kept = jnp.dot(
        jnp.where(zs == pick, 1.0, 0.0).astype(jnp.bfloat16),
        kept_ref[...].astype(jnp.bfloat16),
        preferred_element_type=jnp.float32,
    ).astype(jnp.bfloat16)
    width = NY * LANES
    block = lax.broadcasted_iota(jnp.int32, (LANES, width), 0)
    lane = lax.broadcasted_iota(jnp.int32, (LANES, width), 1) // LANES
    for r in range(NX):
        own, other = own_ref[:, r * width // 2 : (r + 1) * width // 2], other_ref[:, r * width // 2 : (r + 1) * width // 2]
        plane_ref[:, r * width : r * width + width // 2] = jnp.where(c == 0, own, other)
        plane_ref[:, r * width + width // 2 : (r + 1) * width] = jnp.where(c == 0, other, own)
        spread = jnp.where(block == (x ^ r) * (NZ * NY) + z * NY + lane, 1.0, 0.0).astype(jnp.bfloat16)
        mask_ref[:, r * width : (r + 1) * width] = jnp.dot(kept, spread, preferred_element_type=jnp.float32)


def rows_kernel(place_ref, mask_ref, plane_ref, got_ref, one_ref, two_ref, three_ref, out_ref, token_ref, held_ref, sems):
    token_ref[...] = jnp.zeros((8, LANES), jnp.float32)
    x = place_ref[0]
    width = NY * LANES
    copies = [
        pltpu.make_async_copy(got_ref.at[:, :, m], held_ref.at[m], sems.at[m]) for m in range(NZ // 2)
    ]
    for copy in copies:
        copy.start()
    for m, copy in enumerate(copies):
        copy.wait()
        mask = mask_ref[m : m + 1, :].astype(jnp.bfloat16)
        weights = plane_ref[...] * mask
        readings = jnp.concatenate([held_ref[m, :, x ^ r].reshape(width, LANES) for r in range(NX)], 0)
        out_ref[m] = jnp.dot(weights, readings, preferred_element_type=jnp.float32).T


def info_rows(place, masks, plane, received, shares):
    takers, _, steps, rows, _ = received.shape
    return pl.pallas_call(
        rows_kernel,
        name="rows",
        out_shape=[f32(steps, LANES, LANES), f32(8, LANES)],
        in_specs=[SCALARS, WHOLE, WHOLE, pl.BlockSpec(memory_space=pl.ANY)] + [WHOLE] * 3,
        out_specs=[WHOLE] * 2,
        scratch_shapes=[
            pltpu.VMEM((steps, takers, NX, rows, LANES), jnp.bfloat16),
            pltpu.SemaphoreType.DMA((steps,)),
        ],
        cost_estimate=pl.CostEstimate(flops=1 << 28, bytes_accessed=3 << 20, transcendentals=0),
        compiler_params=pltpu.CompilerParams(vmem_limit_bytes=32 << 20),
    )(place, masks, plane, received, *shares)


def tail_kernel(place_ref, a_ref, b_ref, c_ref, d_ref, decay_ref, prior_ref, add_ref, spread_ref, drive_ref, tail_ref):
    x = place_ref[0]
    rows = a_ref.shape[0]
    for r, ref in enumerate((a_ref, b_ref, c_ref, d_ref)):
        drive_ref[pl.ds(pl.multiple_of((x ^ r) * rows, rows), rows), :] = ref[...] * decay_ref[...]
    pushed = times(wide(prior_ref[...]), spread_ref[0, :, :LANES])
    drive_ref[:1] += jnp.where(place_ref[1] == 0, pushed, 0.0)
    tail = drive_ref[...]
    for step in reversed(range(LEVELS // 2)):
        n = 4**step
        terms = jnp.concatenate([wide(tail[j * n : (j + 1) * n]) for j in range(3)], 1)
        tail = times(terms, add_ref[step]) + tail[3 * n :]
    tail_ref[...] = jnp.broadcast_to(tail, (8, LANES))


def send_kernel(place_ref, tail_ref, *refs):
    rest_refs, send_ref = refs[:-1], refs[-1]
    to = lax.broadcasted_iota(jnp.int32, (NK, LANES), 0) ^ place_ref[1]
    tail = tail_ref[...]
    terms = wide(tail)
    sends = jnp.broadcast_to(tail[:1], (NK, LANES))
    for level in range(1, SCAN):
        onward = times(terms, rest_refs[level - 1][...])
        sends = jnp.where(to >= 2**level, onward[:1], sends)
    send_ref[...] = sends


def sweep_kernel(drive_ref, spread_ref, out_ref):
    swept = drive_ref[...]
    row = lax.broadcasted_iota(jnp.int32, (STEPS, LANES), 0)
    for step in range(LEVELS // 2):
        for side in range(2):
            shift = 4**step * (1 + side)
            before = jnp.where(row >= shift, pltpu.roll(swept, shift, 0), 0.0)
            swept += times(wide(before), spread_ref[step, :, side * LANES : (side + 1) * LANES])
    out_ref[...] = swept


def state_kernel(place_ref, offsets_ref, spread_ref, swept_ref, *refs):
    lead_refs, out_ref = refs[:-1], refs[-1]
    k = place_ref[1]
    index = lax.broadcasted_iota(jnp.int32, (NK, LANES), 0)
    apart = jnp.where(index < k, index ^ k, 0)
    offsets = offsets_ref[...]
    parts = []
    for level in range(SCAN):
        chosen = (apart >= 2**level) & (apart < 2 ** (level + 1))
        parts.append(jnp.sum(jnp.where(chosen, offsets, 0.0), 0, keepdims=True))
    entry = parts[0]
    for level in range(1, SCAN):
        entry += times(wide(parts[level]), lead_refs[level - 1][...])
    grown = times(wide(entry), spread_ref[0, :, :LANES])
    for step in range(LEVELS // 2):
        more = times(wide(grown), spread_ref[step])
        grown = jnp.concatenate([grown] + [more[:, j * LANES : (j + 1) * LANES] for j in range(3)], 0)
    out_ref[...] = swept_ref[...] + grown


def on_device(observations, sensor_map, noise_precision, availability, decay_rate, prior_mean):
    modes = sensor_map.shape[1]
    rows = observations.shape[0]
    z, y, c, x = (lax.axis_index(a) for a in "zycx")
    k = (z * NY + y) * NC + c
    place = jnp.stack([x, k, z, c, y]).astype(jnp.int32)
    square = f32(modes, modes)
    packet = pack(availability, noise_precision, sensor_map)
    packets = [packet] + [xor_over_x(packet, d) for d in (1, 2, 3)]
    kept, half = local(
        gather_kernel, "gather", [place], packets,
        [f32(NZ, modes), jax.ShapeDtypeStruct((modes, NX * 2 * modes), jnp.bfloat16)], 1 << 16,
    )
    sent = by_taker(observations, *packets[1:])
    received = lax.all_to_all(sent, ("y", "c", "x"), split_axis=0, concat_axis=0, tiled=True)

    for flip in (1, 2, 4):
        kept = kept + lax.ppermute(kept, "z", [(i, i ^ flip) for i in range(NZ)])
    plane, masks = local(
        mask_kernel, "masks", [place], [kept, half, lax.ppermute(half, "c", [(0, 1), (1, 0)])],
        [jax.ShapeDtypeStruct((modes, NX * NY * modes), jnp.bfloat16), f32(NZ, NX * NY * modes)], 1 << 20,
    )

    info = weigh(availability, noise_precision, sensor_map)
    infos = [info] + [xor_over_x(info, d) for d in (1, 2, 3)]

    partial, done = info_rows(place, masks, plane, received.reshape(NY * NC, NX, NZ // 2, rows, LANES), infos[1:])
    partial = lax.all_to_all(partial.reshape(NZ, -1, modes), "z", split_axis=0, concat_axis=0, tiled=True)
    piece = jnp.sum(partial, 0)
    pieces = [rows_to_block(piece, d) for d in range(NX)]

    retain = jnp.exp(-decay_rate)
    powers, total = local(
        power_kernel, "powers", [],
        infos + [decay_rate[None, :], jnp.broadcast_to(retain[:, None], (modes, modes))],
        [f32(LEVELS, modes, modes), square], 8 * 6 * 2 * modes**3, tokens=[done],
    )
    steps = LEVELS // 2
    adding, spreading = local(
        factor_kernel, "factors", [], [powers],
        [
            jax.ShapeDtypeStruct((steps, 9 * modes, modes), jnp.bfloat16),
            jax.ShapeDtypeStruct((steps, 3 * modes, 3 * modes), jnp.bfloat16),
        ],
        4 * 6 * 2 * modes**3,
    )
    drive, tail = local(
        tail_kernel, "tail", [place], pieces + [decay_rate[None, :], prior_mean[None, :], adding, spreading],
        [f32(STEPS, modes), f32(8, modes)], 8 * 6 * 2 * modes**3,
    )
    terms = jax.ShapeDtypeStruct((3 * modes, modes), jnp.bfloat16)
    got = lax.ppermute(total, "c", [(0, 1), (1, 0)])
    total, lead, rest, *pair_terms = local(
        pair_kernel, "pairs", [place], [total, got], [square] * 3 + [terms] * 2, 6 * 2 * modes**3
    )
    leads, rests = [pair_terms[0]], [pair_terms[1]]
    for axis, size, bits, tokens in (("y", NY, y, []), ("z", NZ, z, [tail])):
        got = [lax.ppermute(total, axis, [(i, i ^ d) for i in range(size)]) for d in (1, 2, 3)]
        total, lead, rest, *quad_terms = local(
            quad_kernel, "quads_" + axis, [bits.astype(jnp.int32)[None]], [total] + got + [lead, rest],
            [square] * 3 + [terms] * 4, 5 * 6 * 2 * modes**3, tokens=tokens,
        )
        leads += quad_terms[::2]
        rests += quad_terms[1::2]

    (sends,) = local(
        send_kernel, "sends", [place], [tail] + rests, [f32(NK, modes)], 5 * 6 * 2 * modes**3
    )
    offsets = lax.all_to_all(sends, ("z", "y", "c"), split_axis=0, concat_axis=0, tiled=True)
    (swept,) = local(
        sweep_kernel, "sweep", [], [drive, spreading], [f32(STEPS, modes)], 8 * 12 * 2 * modes**3
    )
    (states,) = local(
        state_kernel, "states", [place], [offsets, spreading, swept] + leads,
        [f32(STEPS, modes)], 15 * 6 * 2 * modes**3,
    )
    return states


def solution(mesh):
    fine = Mesh(mesh.devices.reshape(NZ, NY, NC, NX), ("z", "y", "c", "x"))
    return jax.shard_map(
        on_device,
        mesh=fine,
        in_specs=(
            P(("x", "z", "y", "c"), None),
            P("x", None),
            P("x", None, None),
            P(("z", "y", "c"), "x"),
            P(),
            P(),
        ),
        out_specs=P(("z", "y", "c"), None),
        check_vma=False,
    )
```

time: 670 us -> 113 us (0.17)
  the two profiles are of different devices: /device:TPU:128 before, /device:TPU:1 now
where the time goes in v2:
time: 113 us; the launch traced here: 112 us
  starting transfers between devices  61.6 us (55%)
  waiting for transfers between devices  26.8 us (24%)
  Pallas kernels  22.2 us (20%)
  local copies, waits for them, and re-layouts  1.54 us (1%)
    pallas_call x11, Pallas kernels, local(): pl.pallas_call(call, name=name, out_shape=outs, in_specs=[SCALARS] * len(...  12.3 us
    all_to_all x1, starting transfers between devices, on_device(): lax.all_to_all(sends, ('z', 'y', 'c'), split_axis=0, concat_axis=0, tiled...  12.2 us
    ppermute x3, starting transfers between devices, on_device(): kept = kept + lax.ppermute(kept, 'z', [(i, i ^ flip) for i in range(NZ)])  10.7 us
    ppermute x6, waiting for transfers between devices, xor_over_x(): return lax.ppermute(block, 'x', [(i, i ^ distance) for i in range(NX)])  10.2 us
    ppermute x6, starting transfers between devices, xor_over_x(): return lax.ppermute(block, 'x', [(i, i ^ distance) for i in range(NX)])  8.6 us
    all_to_all x1, starting transfers between devices, on_device(): lax.all_to_all(partial.reshape(NZ, -1, modes), 'z', split_axis=0, concat_...  8.2 us
    all_to_all x1, waiting for transfers between devices, on_device(): lax.all_to_all(sends, ('z', 'y', 'c'), split_axis=0, concat_axis=0, tiled...  8.06 us
    ppermute x6, starting transfers between devices, on_device(): lax.ppermute(total, axis, [(i, i ^ d) for i in range(size)])  7.58 us
  transfers between devices with their start and end apart: 24, of which 12 were waited for; matrix products, arithmetic and copies ran while one was open for 0% of the time, Pallas kernels for 10%

profile of v2, /device:TPU:1, one launch (start us, length us, event | category | flops | bytes accessed | tf_op | source)
XLA Modules:
  0.0 112.4 jit_solution(11367126147410916406)
XLA Ops:
  0.0 2.6 %pack.1.refs_1_ = bf16[144,256]{1,0:T(8,128)(2,1)} custom-call(s32[1,32]{1,0:T(1,128)} %kept_ref.3, bf16[32,128,128]{2,1,0:T(8,128)(2,1)} %noise_ref.3, bf16[4096,128]{1,0:T(8,128)(2,1)} %map_ref.3), custom_call_target="tpu_custom_call" | custom-call | flops 8388608 | bytes 262144 | tf_op jit(solution)/shard_map/pack/pallas_call | solution.py:127
  2.6 2.1 %collective-permute-start = (bf16[144,256]{1,0:T(8,128)(2,1)}, bf16[144,256]{1,0:T(8,128)(2,1)S(1)}, u32[]{:S(2)}, u32[]{:S(2)}) collective-permute-start(bf16[144,256]{1,0:T(8,128)(2,1)} %pack.1.refs_1_), channel_id=1, source_target_pairs={{0,1},{1,0},{2,3},{3,2},{4,5},{5,4},{6,7},{7,6},{8,9},{9,8},{10,11... | collective-permute-start | bytes 221192 | tf_op jit(solution)/shard_map/ppermute | solution.py:67
  4.7 2.5 %collective-permute-start.1 = (bf16[144,256]{1,0:T(8,128)(2,1)}, bf16[144,256]{1,0:T(8,128)(2,1)S(1)}, u32[]{:S(2)}, u32[]{:S(2)}) collective-permute-start(bf16[144,256]{1,0:T(8,128)(2,1)} %pack.1.refs_1_), channel_id=1, source_target_pairs={{0,2},{1,3},{2,0},{3,1},{4,6},{5,7},{6,4},{7,5},{8,10},{9,11},{10,... | collective-permute-start | bytes 221192 | tf_op jit(solution)/shard_map/ppermute | solution.py:67
  7.2 3.1 %collective-permute-done.1.refs_3_.refs_1_ = bf16[144,256]{1,0:T(8,128)(2,1)S(1)} collective-permute-done((bf16[144,256]{1,0:T(8,128)(2,1)}, bf16[144,256]{1,0:T(8,128)(2,1)S(1)}, u32[]{:S(2)}, u32[]{:S(2)}) %collective-permute-start.1) | collective-permute-done | bytes 73760 | tf_op jit(solution)/shard_map/ppermute | solution.py:67
  10.3 1.9 %collective-permute-done.2.refs_4_.refs_2_ = bf16[144,256]{1,0:T(8,128)(2,1)S(1)} collective-permute-done((bf16[144,256]{1,0:T(8,128)(2,1)}, bf16[144,256]{1,0:T(8,128)(2,1)S(1)}, u32[]{:S(2)}, u32[]{:S(2)}) %collective-permute-start.2) | collective-permute-done | bytes 73760 | tf_op jit(solution)/shard_map/ppermute | solution.py:67
  12.3 0.4 by_taker.1
  12.6 1.4 %copy-done = bf16[16,2,4,64,128]{4,3,2,1,0:T(8,128)(2,1)} copy-done((bf16[16,2,4,64,128]{4,3,2,1,0:T(8,128)(2,1)}, bf16[16,2,4,64,128]{4,3,2,1,0:T(8,128)(2,1)S(1)}, u32[]{:S(2)}) %copy-start) | copy-done | bytes 2097176
  14.0 6.7 %all-to-all-start = ((bf16[32,256,128]{2,1,0:T(8,128)(2,1)}), bf16[32,256,128]{2,1,0:T(8,128)(2,1)S(1)}, u32[]{:S(2)}, u32[]{:S(2)}) async-start(bf16[32,256,128]{2,1,0:T(8,128)(2,1)} %bitcast.15), calls=%async_computation | async-start | bytes 4194304 | tf_op jit(solution)/shard_map/all_to_all | solution.py:368
  20.8 0.6 gather.1
  21.7 4.1 %weigh.1.refs_0_ = f32[128,128]{1,0:T(8,128)} custom-call(s32[1,32]{1,0:T(1,128)} %kept_ref.3, bf16[32,128,128]{2,1,0:T(8,128)(2,1)} %noise_ref.3, bf16[4096,128]{1,0:T(8,128)(2,1)} %map_ref.3), custom_call_target="tpu_custom_call" | custom-call | flops 268435456 | bytes 2097152 | tf_op jit(solution)/shard_map/weigh/pallas_call | solution.py:176
  25.8 1.5 %collective-permute-start.7 = (f32[128,128]{1,0:T(8,128)}, f32[128,128]{1,0:T(8,128)S(1)}, u32[]{:S(2)}, u32[]{:S(2)}) collective-permute-start(f32[128,128]{1,0:T(8,128)} %weigh.1.refs_0_), channel_id=1, source_target_pairs={{0,1},{1,0},{2,3},{3,2},{4,5},{5,4},{6,7},{7,6},{8,9},{9,8},{10,11... | collective-permute-start | bytes 196616 | tf_op jit(solution)/shard_map/ppermute | solution.py:67
  27.3 2.4 %collective-permute-start.8 = (f32[128,128]{1,0:T(8,128)}, f32[128,128]{1,0:T(8,128)S(1)}, u32[]{:S(2)}, u32[]{:S(2)}) collective-permute-start(f32[128,128]{1,0:T(8,128)} %weigh.1.refs_0_), channel_id=1, source_target_pairs={{0,2},{1,3},{2,0},{3,1},{4,6},{5,7},{6,4},{7,5},{8,10},{9,11},{10,... | collective-permute-start | bytes 196616 | tf_op jit(solution)/shard_map/ppermute | solution.py:67
  29.8 1.6 %collective-permute-start.3 = (f32[8,128]{1,0:T(8,128)S(1)}, f32[8,128]{1,0:T(8,128)S(1)}, u32[]{:S(2)}, u32[]{:S(2)}) collective-permute-start(f32[8,128]{1,0:T(8,128)S(1)} %get-tuple-element.33), channel_id=1, source_target_pairs={{0,32},{32,0},{64,96},{96,64},{128,160},{160,128},{192,224},{224,1... | collective-permute-start | bytes 12296 | tf_op jit(solution)/shard_map/ppermute | solution.py:371
  31.4 1.3 %collective-permute-done.3 = f32[8,128]{1,0:T(8,128)S(1)} collective-permute-done((f32[8,128]{1,0:T(8,128)S(1)}, f32[8,128]{1,0:T(8,128)S(1)}, u32[]{:S(2)}, u32[]{:S(2)}) %collective-permute-start.3) | collective-permute-done | bytes 4128 | tf_op jit(solution)/shard_map/ppermute | solution.py:371
  32.7 3.0 %collective-permute-start.4 = (f32[8,128]{1,0:T(8,128)S(1)}, f32[8,128]{1,0:T(8,128)S(1)}, u32[]{:S(2)}, u32[]{:S(2)}) collective-permute-start(f32[8,128]{1,0:T(8,128)S(1)} %add.17), channel_id=1, source_target_pairs={{0,64},{32,96},{64,0},{96,32},{128,192},{160,224},{192,128},{224,1... | collective-permute-start | bytes 12296 | tf_op jit(solution)/shard_map/ppermute | solution.py:371
  35.7 1.3 %collective-permute-done.4 = f32[8,128]{1,0:T(8,128)S(1)} collective-permute-done((f32[8,128]{1,0:T(8,128)S(1)}, f32[8,128]{1,0:T(8,128)S(1)}, u32[]{:S(2)}, u32[]{:S(2)}) %collective-permute-start.4) | collective-permute-done | bytes 4128 | tf_op jit(solution)/shard_map/ppermute | solution.py:371
  37.0 6.1 %collective-permute-start.5 = (f32[8,128]{1,0:T(8,128)S(1)}, f32[8,128]{1,0:T(8,128)S(1)}, u32[]{:S(2)}, u32[]{:S(2)}) collective-permute-start(f32[8,128]{1,0:T(8,128)S(1)} %add.18), channel_id=1, source_target_pairs={{0,128},{32,160},{64,192},{96,224},{128,0},{160,32},{192,64},{224,... | collective-permute-start | bytes 12296 | tf_op jit(solution)/shard_map/ppermute | solution.py:371
  43.1 1.0 collective-permute-done.5
  44.1 0.8 masks.1
  44.9 1.9 %collective-permute-done.7.one_ref.refs_1_ = f32[128,128]{1,0:T(8,128)S(1)} collective-permute-done((f32[128,128]{1,0:T(8,128)}, f32[128,128]{1,0:T(8,128)S(1)}, u32[]{:S(2)}, u32[]{:S(2)}) %collective-permute-start.7) | collective-permute-done | bytes 65568 | tf_op jit(solution)/shard_map/ppermute | solution.py:67
  46.8 3.2 %collective-permute-done.8.two_ref.refs_2_ = f32[128,128]{1,0:T(8,128)S(1)} collective-permute-done((f32[128,128]{1,0:T(8,128)}, f32[128,128]{1,0:T(8,128)S(1)}, u32[]{:S(2)}, u32[]{:S(2)}) %collective-permute-start.8) | collective-permute-done | bytes 65568 | tf_op jit(solution)/shard_map/ppermute | solution.py:67
  50.1 2.9 %rows.1 = (f32[4,128,128]{2,1,0:T(8,128)}, f32[8,128]{1,0:T(8,128)S(1)}) custom-call(s32[5]{0:T(128)S(1)} %stack.23.refs_0_.place_ref, f32[8,2048]{1,0:T(8,128)S(1)} %get-tuple-element.35.mask_ref, bf16[128,2048]{1,0:T(8,128)(2,1)S(1)} %get-tuple-element.36.plane_ref, bf16[8,4,4,64,128]{4,3,2,1,0:T(8,128)(2,1)S(1)} %bitcast.14, ...), custom_call_target="tpu_custom_call" | custom-call | flops 268435456 | bytes 3145728 | tf_op jit(solution)/shard_map/rows/pallas_call | solution.py:281
  53.0 8.2 %all-to-all-start.1 = ((f32[8,64,128]{2,1,0:T(8,128)}), f32[8,64,128]{2,1,0:T(8,128)S(1)}, u32[]{:S(2)}, u32[]{:S(2)}) async-start(f32[8,64,128]{2,1,0:T(8,128)} %bitcast.7), calls=%async_computation.1 | async-start | bytes 524288 | tf_op jit(solution)/shard_map/all_to_all | solution.py:381
  61.3 1.8 %powers.1 = (f32[8,128,128]{2,1,0:T(8,128)S(1)}, f32[128,128]{1,0:T(8,128)S(1)}) custom-call(f32[128,128]{1,0:T(8,128)S(1)} %copy-done.3, f32[128,128]{1,0:T(8,128)S(1)} %collective-permute-done.7.one_ref.refs_1_, f32[128,128]{1,0:T(8,128)S(1)} %collective-permute-done.8.two_ref.refs_2_, f32[128,128]{1,0:T(8,128)S(1)} %collective-permute-done.9.three_ref.refs_3_, ...), custom_call_target="tpu_custom_call" | custom-call | flops 201326592 | bytes 1048576 | tf_op jit(solution)/shard_map/powers/pallas_call | solution.py:34
  63.1 1.2 %collective-permute-start.14 = (f32[128,128]{1,0:T(8,128)S(1)}, f32[128,128]{1,0:T(8,128)S(1)}, u32[]{:S(2)}, u32[]{:S(2)}) collective-permute-start(f32[128,128]{1,0:T(8,128)S(1)} %get-tuple-element.43.refs_1_), channel_id=1, source_target_pairs={{0,4},{4,0},{1,5},{5,1},{2,6},{6,2},{3,7},{7,3},{8,12},{12,8},{9,1... | collective-permute-start | bytes 196616 | tf_op jit(solution)/shard_map/ppermute | solution.py:405
  64.3 0.9 collective-permute-done.14.refs_2_
  65.2 0.8 pairs.1
  66.0 1.0 collective-permute-start.15
  66.9 2.5 %collective-permute-start.16 = (f32[128,128]{1,0:T(8,128)S(1)}, f32[128,128]{1,0:T(8,128)S(1)}, u32[]{:S(2)}, u32[]{:S(2)}) collective-permute-start(f32[128,128]{1,0:T(8,128)S(1)} %get-tuple-element.45.refs_1_), channel_id=1, source_target_pairs={{0,16},{8,24},{16,0},{24,8},{1,17},{9,25},{17,1},{25,9},{2,18},{10... | collective-permute-start | bytes 196616 | tf_op jit(solution)/shard_map/ppermute | solution.py:411
  69.4 0.5 collective-permute-start.17
  69.9 1.5 %all-to-all-done.1 = f32[8,64,128]{2,1,0:T(8,128)S(1)} async-done(((f32[8,64,128]{2,1,0:T(8,128)}), f32[8,64,128]{2,1,0:T(8,128)S(1)}, u32[]{:S(2)}, u32[]{:S(2)}) %all-to-all-start.1) | async-done | bytes 262176 | tf_op jit(solution)/shard_map/all_to_all | solution.py:381
  71.4 0.7 collective-permute-start.10
  72.1 3.0 %collective-permute-start.11 = (f32[64,128]{1,0:T(8,128)S(1)}, f32[64,128]{1,0:T(8,128)S(1)}, u32[]{:S(2)}, u32[]{:S(2)}) collective-permute-start(f32[64,128]{1,0:T(8,128)S(1)} %reduce_sum.9), channel_id=1, source_target_pairs={{0,1},{1,33},{2,3},{3,35},{32,0},{33,32},{34,2},{35,34},{64,65},{6... | collective-permute-start | bytes 98312 | tf_op jit(solution)/shard_map/ppermute | solution.py:76
  75.1 0.6 quads_y.1
  75.7 0.6 collective-permute-start.18
  76.3 2.1 %collective-permute-start.19 = (f32[128,128]{1,0:T(8,128)S(1)}, f32[128,128]{1,0:T(8,128)S(1)}, u32[]{:S(2)}, u32[]{:S(2)}) collective-permute-start(f32[128,128]{1,0:T(8,128)S(1)} %get-tuple-element.50.refs_1_), channel_id=1, source_target_pairs={{0,64},{32,96},{64,0},{96,32},{128,192},{160,224},{192,128},{224,1... | collective-permute-start | bytes 196616 | tf_op jit(solution)/shard_map/ppermute | solution.py:411
  78.4 0.9 collective-permute-start.20
  79.6 2.1 %collective-permute-start.13 = (f32[64,128]{1,0:T(8,128)S(1)}, f32[64,128]{1,0:T(8,128)S(1)}, u32[]{:S(2)}, u32[]{:S(2)}) collective-permute-start(f32[64,128]{1,0:T(8,128)S(1)} %reduce_sum.9), channel_id=1, source_target_pairs={{0,3},{1,35},{2,1},{3,33},{32,2},{33,34},{34,0},{35,32},{64,67},{6... | collective-permute-start | bytes 98312 | tf_op jit(solution)/shard_map/ppermute | solution.py:76
  81.7 0.5 factors.1
  82.2 1.4 %collective-permute-done.12.refs_3_ = f32[64,128]{1,0:T(8,128)S(1)} collective-permute-done((f32[64,128]{1,0:T(8,128)S(1)}, f32[64,128]{1,0:T(8,128)S(1)}, u32[]{:S(2)}, u32[]{:S(2)}) %collective-permute-start.12) | collective-permute-done | bytes 32800 | tf_op jit(solution)/shard_map/ppermute | solution.py:76
  83.6 1.3 %collective-permute-done.13.refs_4_ = f32[64,128]{1,0:T(8,128)S(1)} collective-permute-done((f32[64,128]{1,0:T(8,128)S(1)}, f32[64,128]{1,0:T(8,128)S(1)}, u32[]{:S(2)}, u32[]{:S(2)}) %collective-permute-start.13) | collective-permute-done | bytes 32800 | tf_op jit(solution)/shard_map/ppermute | solution.py:76
  84.8 1.3 %tail.1 = (f32[256,128]{1,0:T(8,128)S(1)}, f32[8,128]{1,0:T(8,128)S(1)}) custom-call(s32[5]{0:T(128)S(1)} %stack.23.refs_0_.place_ref, f32[64,128]{1,0:T(8,128)S(1)} %collective-permute-done.10.refs_1_, f32[64,128]{1,0:T(8,128)S(1)} %collective-permute-done.11.refs_2_, f32[64,128]{1,0:T(8,128)S(1)} %collective-permute-done.12.refs_3_, ...), custom_call_target="tpu_custom_call" | custom-call | flops 201326592 | bytes 1048576 | tf_op jit(solution)/shard_map/tail/pallas_call | solution.py:34
  86.2 1.3 %quads_z.1 = (f32[128,128]{1,0:T(8,128)}, f32[128,128]{1,0:T(8,128)}, f32[128,128]{1,0:T(8,128)}, bf16[384,128]{1,0:T(8,128)(2,1)S(1)}, bf16[384,128]{1,0:T(8,12...) custom-call(s32[1]{0:T(128)} %bitcast.2.refs_0_, f32[128,128]{1,0:T(8,128)S(1)} %get-tuple-element.50.refs_1_, ...), custom_call_target="tpu_custom_call" | custom-call | flops 125829120 | bytes 1048576 | tf_op jit(solution)/shard_map/quads_z/pallas_call | solution.py:34
  87.4 1.4 %sends.1 = f32[64,128]{1,0:T(8,128)} custom-call(s32[5]{0:T(128)S(1)} %stack.23.refs_0_.place_ref, f32[8,128]{1,0:T(8,128)S(1)} %get-tuple-element.42.refs_7_.refs_1_, bf16[384,128]{1,0:T(8,128)(2,1)S(1)} %get-tuple-element.44.refs_2_, bf16[384,128]{1,0:T(8,128)(2,1)S(1)} %get-tuple-element.48.refs_3_, bf16[384,128]{1,0:T(8,128)(2,1)S(1)} %get-tuple-element.49.refs_4_, ...), custom_call_target="tpu_custom_call" | custom-call | flops 125829120 | bytes 1048576 | tf_op jit(solution)/shard_map/sends/pallas_call | solution.py:34
  88.8 12.2 %all-to-all-start.2 = ((f32[64,1,128]{2,1,0:T(1,128)}), f32[64,1,128]{2,1,0:T(1,128)S(1)}, u32[]{:S(2)}, u32[]{:S(2)}) async-start(f32[64,1,128]{2,1,0:T(1,128)} %bitcast.11), calls=%async_computation.2 | async-start | bytes 65536 | tf_op jit(solution)/shard_map/all_to_all | solution.py:422
  101.0 1.2 %sweep.1.refs_3_ = f32[256,128]{1,0:T(8,128)S(1)} custom-call(f32[256,128]{1,0:T(8,128)S(1)} %get-tuple-element.55.refs_0_, bf16[4,384,384]{2,1,0:T(8,128)(2,1)S(1)} %get-tuple-element.41.refs_8_.refs_1_.refs_2_), custom_call_target="tpu_custom_call" | custom-call | flops 402653184 | bytes 1048576 | tf_op jit(solution)/shard_map/sweep/pallas_call | solution.py:34
  102.2 8.1 %all-to-all-done.2 = f32[64,1,128]{2,1,0:T(1,128)S(1)} async-done(((f32[64,1,128]{2,1,0:T(1,128)}), f32[64,1,128]{2,1,0:T(1,128)S(1)}, u32[]{:S(2)}, u32[]{:S(2)}) %all-to-all-start.2) | async-done | bytes 32800 | tf_op jit(solution)/shard_map/all_to_all | solution.py:422
  110.3 2.1 %states.1 = f32[256,128]{1,0:T(8,128)} custom-call(s32[5]{0:T(128)S(1)} %stack.23.refs_0_.place_ref, f32[64,128]{1,0:T(8,128)S(1)} %bitcast.16, bf16[4,384,384]{2,1,0:T(8,128)(2,1)S(1)} %get-tuple-element.41.refs_8_.refs_1_.refs_2_, f32[256,128]{1,0:T(8,128)S(1)} %sweep.1.refs_3_, bf16[384,128]{1,0:T(8,128)(2,1)S(1)} %get-tuple-element.56.refs_4_, ...), custom_call_target="tpu_custom_call" | custom-call | flops 377487360 | bytes 1048576 | tf_op jit(solution)/shard_map/states/pallas_call | solution.py:34
  (34 shorter events, 1.0 us)
Async XLA Ops:
  0.0 12.3 %copy-start.1 = (bf16[64,16384]{1,0:T(8,128)(2,1)S(1)}, bf16[64,16384]{1,0:T(8,128)(2,1)}, u32[]{:S(2)}) copy-start(bf16[64,16384]{1,0:T(8,128)(2,1)} %rows_ref.1) | copy-start | bytes 6291460
  2.6 4.6 %collective-permute-start = (bf16[144,256]{1,0:T(8,128)(2,1)}, bf16[144,256]{1,0:T(8,128)(2,1)S(1)}, u32[]{:S(2)}, u32[]{:S(2)}) collective-permute-start(bf16[144,256]{1,0:T(8,128)(2,1)} %pack.1.refs_1_), channel_id=1, source_target_pairs={{0,1},{1,0},{2,3},{3,2},{4,5},{5,4},{6,7},{7,6},{8,9},{9,8},{10,11... | collective-permute-start | bytes 221192 | tf_op jit(solution)/shard_map/ppermute | solution.py:67
  4.7 5.6 %collective-permute-start.1 = (bf16[144,256]{1,0:T(8,128)(2,1)}, bf16[144,256]{1,0:T(8,128)(2,1)S(1)}, u32[]{:S(2)}, u32[]{:S(2)}) collective-permute-start(bf16[144,256]{1,0:T(8,128)(2,1)} %pack.1.refs_1_), channel_id=1, source_target_pairs={{0,2},{1,3},{2,0},{3,1},{4,6},{5,7},{6,4},{7,5},{8,10},{9,11},{10,... | collective-permute-start | bytes 221192 | tf_op jit(solution)/shard_map/ppermute | solution.py:67
  7.2 5.1 %collective-permute-start.2 = (bf16[144,256]{1,0:T(8,128)(2,1)}, bf16[144,256]{1,0:T(8,128)(2,1)S(1)}, u32[]{:S(2)}, u32[]{:S(2)}) collective-permute-start(bf16[144,256]{1,0:T(8,128)(2,1)} %pack.1.refs_1_), channel_id=1, source_target_pairs={{0,3},{1,2},{2,1},{3,0},{4,7},{5,6},{6,5},{7,4},{8,11},{9,10},{10,... | collective-permute-start | bytes 221192 | tf_op jit(solution)/shard_map/ppermute | solution.py:67
  12.6 1.4 %copy-start = (bf16[16,2,4,64,128]{4,3,2,1,0:T(8,128)(2,1)}, bf16[16,2,4,64,128]{4,3,2,1,0:T(8,128)(2,1)S(1)}, u32[]{:S(2)}) copy-start(bf16[16,2,4,64,128]{4,3,2,1,0:T(8,128)(2,1)S(1)} %by_taker.1) | copy-start | bytes 6291460
  14.0 6.8 %copy-start.2 = (bf16[144,256]{1,0:T(8,128)(2,1)S(1)}, bf16[144,256]{1,0:T(8,128)(2,1)}, u32[]{:S(2)}) copy-start(bf16[144,256]{1,0:T(8,128)(2,1)} %pack.1.refs_1_) | copy-start | bytes 221188
  14.0 36.1 %all-to-all-start = ((bf16[32,256,128]{2,1,0:T(8,128)(2,1)}), bf16[32,256,128]{2,1,0:T(8,128)(2,1)S(1)}, u32[]{:S(2)}, u32[]{:S(2)}) async-start(bf16[32,256,128]{2,1,0:T(8,128)(2,1)} %bitcast.15), calls=%async_computation | async-start | bytes 4194304 | tf_op jit(solution)/shard_map/all_to_all | solution.py:368
  21.4 22.7 %collective-permute-start.6 = (bf16[128,1024]{1,0:T(8,128)(2,1)S(1)}, bf16[128,1024]{1,0:T(8,128)(2,1)S(1)}, u32[]{:S(2)}, u32[]{:S(2)}) collective-permute-start(bf16[128,1024]{1,0:T(8,128)(2,1)S(1)} %get-tuple-element.34.refs_2_), channel_id=1, source_target_pairs={{0,4},{4,0},{1,5},{5,1},{2,6},{6,2},{3,7},{7,3},{8,12},{12,8},{9,1... | collective-permute-start | bytes 786440 | tf_op jit(solution)/shard_map/ppermute | solution.py:373
  25.8 35.4 %copy-start.4 = (f32[128]{0:T(128)S(1)}, f32[128]{0:T(128)}, u32[]{:S(2)}) copy-start(f32[128]{0:T(128)} %param.10) | copy-start | bytes 1540
  25.8 35.5 %copy-start.3 = (f32[128,128]{1,0:T(8,128)S(1)}, f32[128,128]{1,0:T(8,128)}, u32[]{:S(2)}) copy-start(f32[128,128]{1,0:T(8,128)} %weigh.1.refs_0_) | copy-start | bytes 196612
  25.8 21.1 %collective-permute-start.7 = (f32[128,128]{1,0:T(8,128)}, f32[128,128]{1,0:T(8,128)S(1)}, u32[]{:S(2)}, u32[]{:S(2)}) collective-permute-start(f32[128,128]{1,0:T(8,128)} %weigh.1.refs_0_), channel_id=1, source_target_pairs={{0,1},{1,0},{2,3},{3,2},{4,5},{5,4},{6,7},{7,6},{8,9},{9,8},{10,11... | collective-permute-start | bytes 196616 | tf_op jit(solution)/shard_map/ppermute | solution.py:67
  27.3 22.8 %collective-permute-start.8 = (f32[128,128]{1,0:T(8,128)}, f32[128,128]{1,0:T(8,128)S(1)}, u32[]{:S(2)}, u32[]{:S(2)}) collective-permute-start(f32[128,128]{1,0:T(8,128)} %weigh.1.refs_0_), channel_id=1, source_target_pairs={{0,2},{1,3},{2,0},{3,1},{4,6},{5,7},{6,4},{7,5},{8,10},{9,11},{10,... | collective-permute-start | bytes 196616 | tf_op jit(solution)/shard_map/ppermute | solution.py:67
  29.7 20.4 %collective-permute-start.9 = (f32[128,128]{1,0:T(8,128)}, f32[128,128]{1,0:T(8,128)S(1)}, u32[]{:S(2)}, u32[]{:S(2)}) collective-permute-start(f32[128,128]{1,0:T(8,128)} %weigh.1.refs_0_), channel_id=1, source_target_pairs={{0,3},{1,2},{2,1},{3,0},{4,7},{5,6},{6,5},{7,4},{8,11},{9,10},{10,... | collective-permute-start | bytes 196616 | tf_op jit(solution)/shard_map/ppermute | solution.py:67
  29.8 2.9 %collective-permute-start.3 = (f32[8,128]{1,0:T(8,128)S(1)}, f32[8,128]{1,0:T(8,128)S(1)}, u32[]{:S(2)}, u32[]{:S(2)}) collective-permute-start(f32[8,128]{1,0:T(8,128)S(1)} %get-tuple-element.33), channel_id=1, source_target_pairs={{0,32},{32,0},{64,96},{96,64},{128,160},{160,128},{192,224},{224,1... | collective-permute-start | bytes 12296 | tf_op jit(solution)/shard_map/ppermute | solution.py:371
  32.7 4.3 %collective-permute-start.4 = (f32[8,128]{1,0:T(8,128)S(1)}, f32[8,128]{1,0:T(8,128)S(1)}, u32[]{:S(2)}, u32[]{:S(2)}) collective-permute-start(f32[8,128]{1,0:T(8,128)S(1)} %add.17), channel_id=1, source_target_pairs={{0,64},{32,96},{64,0},{96,32},{128,192},{160,224},{192,128},{224,1... | collective-permute-start | bytes 12296 | tf_op jit(solution)/shard_map/ppermute | solution.py:371
  37.0 7.1 %collective-permute-start.5 = (f32[8,128]{1,0:T(8,128)S(1)}, f32[8,128]{1,0:T(8,128)S(1)}, u32[]{:S(2)}, u32[]{:S(2)}) collective-permute-start(f32[8,128]{1,0:T(8,128)S(1)} %add.18), channel_id=1, source_target_pairs={{0,128},{32,160},{64,192},{96,224},{128,0},{160,32},{192,64},{224,... | collective-permute-start | bytes 12296 | tf_op jit(solution)/shard_map/ppermute | solution.py:371
  53.0 31.9 %copy-start.5 = (f32[128]{0:T(128)S(1)}, f32[128]{0:T(128)}, u32[]{:S(2)}) copy-start(f32[128]{0:T(128)} %param.11) | copy-start | bytes 1540
  53.0 18.4 %all-to-all-start.1 = ((f32[8,64,128]{2,1,0:T(8,128)}), f32[8,64,128]{2,1,0:T(8,128)S(1)}, u32[]{:S(2)}, u32[]{:S(2)}) async-start(f32[8,64,128]{2,1,0:T(8,128)} %bitcast.7), calls=%async_computation.1 | async-start | bytes 524288 | tf_op jit(solution)/shard_map/all_to_all | solution.py:381
  63.1 2.1 %collective-permute-start.14 = (f32[128,128]{1,0:T(8,128)S(1)}, f32[128,128]{1,0:T(8,128)S(1)}, u32[]{:S(2)}, u32[]{:S(2)}) collective-permute-start(f32[128,128]{1,0:T(8,128)S(1)} %get-tuple-element.43.refs_1_), channel_id=1, source_target_pairs={{0,4},{4,0},{1,5},{5,1},{2,6},{6,2},{3,7},{7,3},{8,12},{12,8},{9,1... | collective-permute-start | bytes 196616 | tf_op jit(solution)/shard_map/ppermute | solution.py:405
  66.0 9.1 %collective-permute-start.15 = (f32[128,128]{1,0:T(8,128)S(1)}, f32[128,128]{1,0:T(8,128)S(1)}, u32[]{:S(2)}, u32[]{:S(2)}) collective-permute-start(f32[128,128]{1,0:T(8,128)S(1)} %get-tuple-element.45.refs_1_), channel_id=1, source_target_pairs={{0,8},{8,0},{16,24},{24,16},{1,9},{9,1},{17,25},{25,17},{2,10},{10... | collective-permute-start | bytes 196616 | tf_op jit(solution)/shard_map/ppermute | solution.py:411
  66.9 8.1 %collective-permute-start.16 = (f32[128,128]{1,0:T(8,128)S(1)}, f32[128,128]{1,0:T(8,128)S(1)}, u32[]{:S(2)}, u32[]{:S(2)}) collective-permute-start(f32[128,128]{1,0:T(8,128)S(1)} %get-tuple-element.45.refs_1_), channel_id=1, source_target_pairs={{0,16},{8,24},{16,0},{24,8},{1,17},{9,25},{17,1},{25,9},{2,18},{10... | collective-permute-start | bytes 196616 | tf_op jit(solution)/shard_map/ppermute | solution.py:411
  69.4 5.7 %collective-permute-start.17 = (f32[128,128]{1,0:T(8,128)S(1)}, f32[128,128]{1,0:T(8,128)S(1)}, u32[]{:S(2)}, u32[]{:S(2)}) collective-permute-start(f32[128,128]{1,0:T(8,128)S(1)} %get-tuple-element.45.refs_1_), channel_id=1, source_target_pairs={{0,24},{8,16},{16,8},{24,0},{1,25},{9,17},{17,9},{25,1},{2,26},{10... | collective-permute-start | bytes 196616 | tf_op jit(solution)/shard_map/ppermute | solution.py:411
  71.4 7.9 %collective-permute-start.10 = (f32[64,128]{1,0:T(8,128)S(1)}, f32[64,128]{1,0:T(8,128)S(1)}, u32[]{:S(2)}, u32[]{:S(2)}) collective-permute-start(f32[64,128]{1,0:T(8,128)S(1)} %reduce_sum.9), channel_id=1, source_target_pairs={{0,0},{1,32},{2,2},{3,34},{32,1},{33,33},{34,3},{35,35},{64,64},{6... | collective-permute-start | bytes 98312 | tf_op jit(solution)/shard_map/ppermute | solution.py:76
  72.1 7.6 %collective-permute-start.11 = (f32[64,128]{1,0:T(8,128)S(1)}, f32[64,128]{1,0:T(8,128)S(1)}, u32[]{:S(2)}, u32[]{:S(2)}) collective-permute-start(f32[64,128]{1,0:T(8,128)S(1)} %reduce_sum.9), channel_id=1, source_target_pairs={{0,1},{1,33},{2,3},{3,35},{32,0},{33,32},{34,2},{35,34},{64,65},{6... | collective-permute-start | bytes 98312 | tf_op jit(solution)/shard_map/ppermute | solution.py:76
  75.7 10.5 %collective-permute-start.18 = (f32[128,128]{1,0:T(8,128)S(1)}, f32[128,128]{1,0:T(8,128)S(1)}, u32[]{:S(2)}, u32[]{:S(2)}) collective-permute-start(f32[128,128]{1,0:T(8,128)S(1)} %get-tuple-element.50.refs_1_), channel_id=1, source_target_pairs={{0,32},{32,0},{64,96},{96,64},{128,160},{160,128},{192,224},{224,1... | collective-permute-start | bytes 196616 | tf_op jit(solution)/shard_map/ppermute | solution.py:411
  76.3 9.9 %collective-permute-start.19 = (f32[128,128]{1,0:T(8,128)S(1)}, f32[128,128]{1,0:T(8,128)S(1)}, u32[]{:S(2)}, u32[]{:S(2)}) collective-permute-start(f32[128,128]{1,0:T(8,128)S(1)} %get-tuple-element.50.refs_1_), channel_id=1, source_target_pairs={{0,64},{32,96},{64,0},{96,32},{128,192},{160,224},{192,128},{224,1... | collective-permute-start | bytes 196616 | tf_op jit(solution)/shard_map/ppermute | solution.py:411
  78.4 7.8 %collective-permute-start.20 = (f32[128,128]{1,0:T(8,128)S(1)}, f32[128,128]{1,0:T(8,128)S(1)}, u32[]{:S(2)}, u32[]{:S(2)}) collective-permute-start(f32[128,128]{1,0:T(8,128)S(1)} %get-tuple-element.50.refs_1_), channel_id=1, source_target_pairs={{0,96},{32,64},{64,32},{96,0},{128,224},{160,192},{192,160},{224,1... | collective-permute-start | bytes 196616 | tf_op jit(solution)/shard_map/ppermute | solution.py:411
  79.3 4.3 %collective-permute-start.12 = (f32[64,128]{1,0:T(8,128)S(1)}, f32[64,128]{1,0:T(8,128)S(1)}, u32[]{:S(2)}, u32[]{:S(2)}) collective-permute-start(f32[64,128]{1,0:T(8,128)S(1)} %reduce_sum.9), channel_id=1, source_target_pairs={{0,2},{1,34},{2,0},{3,32},{32,3},{33,35},{34,1},{35,33},{64,66},{6... | collective-permute-start | bytes 98312 | tf_op jit(solution)/shard_map/ppermute | solution.py:76
  79.6 5.2 %collective-permute-start.13 = (f32[64,128]{1,0:T(8,128)S(1)}, f32[64,128]{1,0:T(8,128)S(1)}, u32[]{:S(2)}, u32[]{:S(2)}) collective-permute-start(f32[64,128]{1,0:T(8,128)S(1)} %reduce_sum.9), channel_id=1, source_target_pairs={{0,3},{1,35},{2,1},{3,33},{32,2},{33,34},{34,0},{35,32},{64,67},{6... | collective-permute-start | bytes 98312 | tf_op jit(solution)/shard_map/ppermute | solution.py:76
  88.8 21.5 %all-to-all-start.2 = ((f32[64,1,128]{2,1,0:T(1,128)}), f32[64,1,128]{2,1,0:T(1,128)S(1)}, u32[]{:S(2)}, u32[]{:S(2)}) async-start(f32[64,1,128]{2,1,0:T(1,128)} %bitcast.11), calls=%async_computation.2 | async-start | bytes 65536 | tf_op jit(solution)/shard_map/all_to_all | solution.py:422

commit v3 on v2

--- a/solution.py
+++ b/solution.py
@@ -76,8 +76,7 @@
     return lax.ppermute(piece, ("z", "x"), route)
 
 
-def order_kernel(rows_ref, *refs):
-    out_ref = refs[-1]
+def order_kernel(rows_ref, out_ref):
     for m in range(NZ // 2):
         for par in range(2):
             for j in range(TAKERS):
@@ -85,17 +84,17 @@
                 out_ref[j, par, m] = rows_ref[:, lane : lane + LANES]
 
 
-def by_taker(observations, *tokens):
+def by_taker(observations):
     rows = observations.shape[0]
     out = pl.pallas_call(
         order_kernel,
         name="by_taker",
         out_shape=jax.ShapeDtypeStruct((TAKERS, 2, NZ // 2, rows, LANES), jnp.bfloat16),
-        in_specs=[WHOLE] * (1 + len(tokens)),
+        in_specs=[WHOLE],
         out_specs=WHOLE,
         cost_estimate=pl.CostEstimate(flops=0, bytes_accessed=4 << 20, transcendentals=0),
         compiler_params=pltpu.CompilerParams(vmem_limit_bytes=32 << 20),
-    )(observations, *tokens)
+    )(observations)
     return out.reshape(TAKERS * 2, NZ // 2 * rows, LANES)
 
 
@@ -139,13 +138,35 @@
     )(availability, noise_precision, sensor_map)
 
 
-def gather_kernel(place_ref, own_ref, one_ref, two_ref, three_ref, kept_ref, half_ref):
-    refs = (own_ref, one_ref, two_ref, three_ref)
-    kept = sum(ref[LANES:, :LANES].astype(jnp.float32)[:NZ] for ref in refs)
+def gather_kernel(place_ref, own_ref, one_ref, two_ref, three_ref, kept_ref, half_ref, held_ref, sems):
+    copies = [
+        pltpu.make_async_copy(ref, held_ref.at[r], sems.at[r])
+        for r, ref in enumerate((own_ref, one_ref, two_ref, three_ref))
+    ]
+    for copy in copies:
+        copy.start()
+    for copy in copies:
+        copy.wait()
+    kept = sum(held_ref[r, LANES:, :LANES].astype(jnp.float32)[:NZ] for r in range(NX))
     at = lax.broadcasted_iota(jnp.int32, (NZ, LANES), 0)
     kept_ref[...] = jnp.where(at == place_ref[2], kept, 0.0)
-    for r, ref in enumerate(refs):
-        half_ref[:, 2 * r * LANES : 2 * (r + 1) * LANES] = ref[:LANES]
+    for r in range(NX):
+        half_ref[:, 2 * r * LANES : 2 * (r + 1) * LANES] = held_ref[r, :LANES]
+
+
+def gather(place, packets):
+    return pl.pallas_call(
+        gather_kernel,
+        name="gather",
+        out_shape=[f32(NZ, LANES), jax.ShapeDtypeStruct((LANES, NX * 2 * LANES), jnp.bfloat16)],
+        in_specs=[SCALARS] + [pl.BlockSpec(memory_space=pl.ANY)] * NX,
+        out_specs=[WHOLE] * 2,
+        scratch_shapes=[
+            pltpu.VMEM((NX,) + packets[0].shape, jnp.bfloat16),
+            pltpu.SemaphoreType.DMA((NX,)),
+        ],
+        cost_estimate=pl.CostEstimate(flops=0, bytes_accessed=1 << 20, transcendentals=0),
+    )(place, *packets)
 
 
 def weigh_kernel(kept_ref, noise_ref, map_ref, out_ref):
@@ -198,6 +219,31 @@
         out_ref[level] = power
         power = dot(power, power)
     block_ref[...] = power
+
+
+def factor_kernel(power_ref, add_ref, spread_ref):
+    for step in range(LEVELS // 2):
+        one, two = power_ref[2 * step], power_ref[2 * step + 1]
+        for j, power in enumerate((one, two, dot(one, two))):
+            terms = tall(power)
+            add_ref[step, (2 - j) * 3 * LANES : (3 - j) * 3 * LANES] = terms
+            spread_ref[step, :, j * LANES : (j + 1) * LANES] = terms
+
+
+def once_kernel(array_ref, *refs):
+    pass
+
+
+def once(array, *tokens):
+    return pl.pallas_call(
+        once_kernel,
+        name="once",
+        out_shape=jax.ShapeDtypeStruct(array.shape, array.dtype),
+        in_specs=[pl.BlockSpec(memory_space=pl.ANY)] * (1 + len(tokens)),
+        out_specs=pl.BlockSpec(memory_space=pl.ANY),
+        input_output_aliases={0: 0},
+        compiler_params=pltpu.CompilerParams(vmem_limit_bytes=60 << 20),
+    )(array, *tokens)
 
 
 def factor_kernel(power_ref, add_ref, spread_ref):
@@ -259,7 +305,7 @@
         mask_ref[:, r * width : (r + 1) * width] = jnp.dot(kept, spread, preferred_element_type=jnp.float32)
 
 
-def rows_kernel(place_ref, mask_ref, plane_ref, got_ref, one_ref, two_ref, three_ref, out_ref, token_ref, held_ref, sems):
+def rows_kernel(place_ref, mask_ref, plane_ref, got_ref, out_ref, token_ref, held_ref, sems):
     token_ref[...] = jnp.zeros((8, LANES), jnp.float32)
     x = place_ref[0]
     width = NY * LANES
@@ -276,13 +322,13 @@
         out_ref[m] = jnp.dot(weights, readings, preferred_element_type=jnp.float32).T
 
 
-def info_rows(place, masks, plane, received, shares):
+def info_rows(place, masks, plane, received):
     takers, _, steps, rows, _ = received.shape
     return pl.pallas_call(
         rows_kernel,
         name="rows",
         out_shape=[f32(steps, LANES, LANES), f32(8, LANES)],
-        in_specs=[SCALARS, WHOLE, WHOLE, pl.BlockSpec(memory_space=pl.ANY)] + [WHOLE] * 3,
+        in_specs=[SCALARS, WHOLE, WHOLE, pl.BlockSpec(memory_space=pl.ANY)],
         out_specs=[WHOLE] * 2,
         scratch_shapes=[
             pltpu.VMEM((steps, takers, NX, rows, LANES), jnp.bfloat16),
@@ -290,10 +336,11 @@
         ],
         cost_estimate=pl.CostEstimate(flops=1 << 28, bytes_accessed=3 << 20, transcendentals=0),
         compiler_params=pltpu.CompilerParams(vmem_limit_bytes=32 << 20),
-    )(place, masks, plane, received, *shares)
-
-
-def tail_kernel(place_ref, a_ref, b_ref, c_ref, d_ref, decay_ref, prior_ref, add_ref, spread_ref, drive_ref, tail_ref):
+    )(place, masks, plane, received)
+
+
+def tail_kernel(place_ref, a_ref, b_ref, c_ref, d_ref, decay_ref, prior_ref, add_ref, spread_ref, *refs):
+    rest_refs, (drive_ref, tail_ref, near_ref) = refs[:3], refs[3:]
     x = place_ref[0]
     rows = a_ref.shape[0]
     for r, ref in enumerate((a_ref, b_ref, c_ref, d_ref)):
@@ -306,18 +353,28 @@
         terms = jnp.concatenate([wide(tail[j * n : (j + 1) * n]) for j in range(3)], 1)
         tail = times(terms, add_ref[step]) + tail[3 * n :]
     tail_ref[...] = jnp.broadcast_to(tail, (8, LANES))
-
-
-def send_kernel(place_ref, tail_ref, *refs):
-    rest_refs, send_ref = refs[:-1], refs[-1]
-    to = lax.broadcasted_iota(jnp.int32, (NK, LANES), 0) ^ place_ref[1]
-    tail = tail_ref[...]
+    near_ref[...] = onward(place_ref[1], tail, jnp.broadcast_to(tail, (NK, LANES)), 1, [ref[...] for ref in rest_refs])
+
+
+def onward(k, tail, sends, level, factors):
+    to = lax.broadcasted_iota(jnp.int32, (NK, LANES), 0) ^ k
     terms = wide(tail)
-    sends = jnp.broadcast_to(tail[:1], (NK, LANES))
-    for level in range(1, SCAN):
-        onward = times(terms, rest_refs[level - 1][...])
-        sends = jnp.where(to >= 2**level, onward[:1], sends)
-    send_ref[...] = sends
+    for step, factor in enumerate(factors):
+        sends = jnp.where(to >= 2 ** (level + step), times(terms, factor), sends)
+    return sends
+
+
+def far_kernel(place_ref, total_ref, one_ref, two_ref, three_ref, lead_ref, rest_ref, tail_ref, near_ref, four_ref, five_ref, send_ref):
+    odd, upper = place_ref[2] % 2 == 1, place_ref[2] % 4 >= 2
+    two, three = two_ref[...], three_ref[...]
+    total, lead, rest = joined(odd, total_ref[...], one_ref[...], lead_ref[...], rest_ref[...])
+    four_ref[...] = tall(lead)
+    factors = [tall(rest)]
+    beside = dot(jnp.where(odd, three, two), jnp.where(odd, two, three))
+    total, lead, rest = joined(upper, total, beside, lead, rest)
+    five_ref[...] = tall(lead)
+    factors.append(tall(rest))
+    send_ref[...] = onward(place_ref[1], tail_ref[:1], near_ref[...], 4, factors)
 
 
 def sweep_kernel(drive_ref, spread_ref, out_ref):
@@ -360,11 +417,8 @@
     square = f32(modes, modes)
     packet = pack(availability, noise_precision, sensor_map)
     packets = [packet] + [xor_over_x(packet, d) for d in (1, 2, 3)]
-    kept, half = local(
-        gather_kernel, "gather", [place], packets,
-        [f32(NZ, modes), jax.ShapeDtypeStruct((modes, NX * 2 * modes), jnp.bfloat16)], 1 << 16,
-    )
-    sent = by_taker(observations, *packets[1:])
+    kept, half = gather(place, packets)
+    sent = once(by_taker(observations), *packets[1:])
     received = lax.all_to_all(sent, ("y", "c", "x"), split_axis=0, concat_axis=0, tiled=True)
 
     for flip in (1, 2, 4):
@@ -377,7 +431,7 @@
     info = weigh(availability, noise_precision, sensor_map)
     infos = [info] + [xor_over_x(info, d) for d in (1, 2, 3)]
 
-    partial, done = info_rows(place, masks, plane, received.reshape(NY * NC, NX, NZ // 2, rows, LANES), infos[1:])
+    partial, done = info_rows(place, masks, plane, received.reshape(NY * NC, NX, NZ // 2, rows, LANES))
     partial = lax.all_to_all(partial.reshape(NZ, -1, modes), "z", split_axis=0, concat_axis=0, tiled=True)
     piece = jnp.sum(partial, 0)
     pieces = [rows_to_block(piece, d) for d in range(NX)]
@@ -386,7 +440,7 @@
     powers, total = local(
         power_kernel, "powers", [],
         infos + [decay_rate[None, :], jnp.broadcast_to(retain[:, None], (modes, modes))],
-        [f32(LEVELS, modes, modes), square], 8 * 6 * 2 * modes**3, tokens=[done],
+        [f32(LEVELS, modes, modes), square], 4 * 10**10, tokens=[done],
     )
     steps = LEVELS // 2
     adding, spreading = local(
@@ -397,28 +451,32 @@
         ],
         4 * 6 * 2 * modes**3,
     )
-    drive, tail = local(
-        tail_kernel, "tail", [place], pieces + [decay_rate[None, :], prior_mean[None, :], adding, spreading],
-        [f32(STEPS, modes), f32(8, modes)], 8 * 6 * 2 * modes**3,
-    )
     terms = jax.ShapeDtypeStruct((3 * modes, modes), jnp.bfloat16)
     got = lax.ppermute(total, "c", [(0, 1), (1, 0)])
     total, lead, rest, *pair_terms = local(
         pair_kernel, "pairs", [place], [total, got], [square] * 3 + [terms] * 2, 6 * 2 * modes**3
     )
     leads, rests = [pair_terms[0]], [pair_terms[1]]
-    for axis, size, bits, tokens in (("y", NY, y, []), ("z", NZ, z, [tail])):
-        got = [lax.ppermute(total, axis, [(i, i ^ d) for i in range(size)]) for d in (1, 2, 3)]
-        total, lead, rest, *quad_terms = local(
-            quad_kernel, "quads_" + axis, [bits.astype(jnp.int32)[None]], [total] + got + [lead, rest],
-            [square] * 3 + [terms] * 4, 5 * 6 * 2 * modes**3, tokens=tokens,
-        )
-        leads += quad_terms[::2]
-        rests += quad_terms[1::2]
-
-    (sends,) = local(
-        send_kernel, "sends", [place], [tail] + rests, [f32(NK, modes)], 5 * 6 * 2 * modes**3
-    )
+    got = [lax.ppermute(total, "y", [(i, i ^ d) for i in range(NY)]) for d in (1, 2, 3)]
+    total, lead, rest, *quad_terms = local(
+        quad_kernel, "quads", [y.astype(jnp.int32)[None]], [total] + got + [lead, rest],
+        [square] * 3 + [terms] * 4, 5 * 6 * 2 * modes**3,
+    )
+    leads += quad_terms[::2]
+    rests += quad_terms[1::2]
+    got = [lax.ppermute(total, "z", [(i, i ^ d) for i in range(NZ)]) for d in (1, 2, 3)]
+
+    drive, tail, near = local(
+        tail_kernel, "tail", [place],
+        pieces + [decay_rate[None, :], prior_mean[None, :], adding, spreading] + rests,
+        [f32(STEPS, modes), f32(8, modes), f32(NK, modes)], 8 * 6 * 2 * modes**3,
+    )
+    *far_terms, sends = local(
+        far_kernel, "far", [place], [total] + got + [lead, rest, tail, near],
+        [terms] * 2 + [f32(NK, modes)], 5 * 6 * 2 * modes**3,
+    )
+    leads += far_terms
+
     offsets = lax.all_to_all(sends, ("z", "y", "c"), split_axis=0, concat_axis=0, tiled=True)
     (swept,) = local(
         sweep_kernel, "sweep", [], [drive, spreading], [f32(STEPS, modes)], 8 * 12 * 2 * modes**3

time: 113 us -> 110 us (0.973)
  waiting for transfers between devices: 26.8 us -> 21.9 us
  starting transfers between devices: 61.6 us -> 60.2 us
  Pallas kernels: 22.2 us -> 23.5 us
  local copies, waits for them, and re-layouts: 1.54 us -> 2.71 us
    ppermute x6, waiting for transfers between devices: 10.2 us -> 3.34 us  [xor_over_x(): return lax.ppermute(block, 'x', [(i, i ^ distance) for i in range(NX)])]
    all_to_all x1, starting transfers between devices: 12.2 us -> 8.46 us  [on_device(): lax.all_to_all(sends, ('z', 'y', 'c'), split_axis=0, concat_axis=0, tiled...]
    ppermute x4, starting transfers between devices: 6.04 us -> 9.15 us  [rows_to_block(): return lax.ppermute(piece, ('z', 'x'), route)]
    pallas_call x0 -> x2, Pallas kernels: none -> 2.55 us  [the longest x1 2.55 us: gather(): pl.pallas_call(gather_kernel, name='gather', out_shape=[f32(NZ, LANES), j...]
    ppermute x4, waiting for transfers between devices: 2.64 us -> 4.92 us  [rows_to_block(): return lax.ppermute(piece, ('z', 'x'), route)]
    pallas_call x11 -> x9, Pallas kernels: 12.3 us -> 11.1 us  [local(): pl.pallas_call(call, name=name, out_shape=outs, in_specs=[SCALARS] * len(...]
    ppermute x3, starting transfers between devices: 10.7 us -> 9.6 us  [on_device(): kept = kept + lax.ppermute(kept, 'z', [(i, i ^ flip) for i in range(NZ)])]
  transfers between devices with their start and end apart: 24 -> 24, of which waited for: 12 -> 10; matrix products, arithmetic and copies ran while one was open for 0% -> 1% of each run, Pallas kernels for 10% -> 16%
where the time goes in v3:
time: 110 us; the launch traced here: 109 us
  starting transfers between devices  60.2 us (55%)
  Pallas kernels  23.5 us (21%)
  waiting for transfers between devices  21.9 us (20%)
  local copies, waits for them, and re-layouts  2.71 us (2%)
    pallas_call x9, Pallas kernels, local(): pl.pallas_call(call, name=name, out_shape=outs, in_specs=[SCALARS] * len(...  11.1 us
    ppermute x3, starting transfers between devices, on_device(): kept = kept + lax.ppermute(kept, 'z', [(i, i ^ flip) for i in range(NZ)])  9.6 us
    ppermute x4, starting transfers between devices, rows_to_block(): return lax.ppermute(piece, ('z', 'x'), route)  9.15 us
    ppermute x6, starting transfers between devices, xor_over_x(): return lax.ppermute(block, 'x', [(i, i ^ distance) for i in range(NX)])  8.6 us
    all_to_all x1, starting transfers between devices, on_device(): lax.all_to_all(sends, ('z', 'y', 'c'), split_axis=0, concat_axis=0, tiled...  8.46 us
    all_to_all x1, starting transfers between devices, on_device(): lax.all_to_all(partial.reshape(NZ, -1, modes), 'z', split_axis=0, concat_...  8.2 us
    all_to_all x1, waiting for transfers between devices, on_device(): lax.all_to_all(sends, ('z', 'y', 'c'), split_axis=0, concat_axis=0, tiled...  8.05 us
    all_to_all x1, starting transfers between devices, on_device(): lax.all_to_all(sent, ('y', 'c', 'x'), split_axis=0, concat_axis=0, tiled=...  6.57 us
  transfers between devices with their start and end apart: 24, of which 10 were waited for; matrix products, arithmetic and copies ran while one was open for 1% of the time, Pallas kernels for 16%

profile of v3, /device:TPU:1, one launch (start us, length us, event | category | flops | bytes accessed | tf_op | source)
XLA Modules:
  0.0 109.3 jit_solution(15992876964162333836)
XLA Ops:
  0.0 2.6 %pack.1.own_ref = bf16[144,256]{1,0:T(8,128)(2,1)} custom-call(s32[1,32]{1,0:T(1,128)} %kept_ref.3, bf16[32,128,128]{2,1,0:T(8,128)(2,1)} %noise_ref.3, bf16[4096,128]{1,0:T(8,128)(2,1)} %map_ref.3), custom_call_target="tpu_custom_call" | custom-call | flops 8388608 | bytes 262144 | tf_op jit(solution)/shard_map/pack/pallas_call | solution.py:126
  2.6 2.1 %collective-permute-start.3 = (bf16[144,256]{1,0:T(8,128)(2,1)}, bf16[144,256]{1,0:T(8,128)(2,1)S(1)}, u32[]{:S(2)}, u32[]{:S(2)}) collective-permute-start(bf16[144,256]{1,0:T(8,128)(2,1)} %pack.1.own_ref), channel_id=1, source_target_pairs={{0,1},{1,0},{2,3},{3,2},{4,5},{5,4},{6,7},{7,6},{8,9},{9,8},{10,11... | collective-permute-start | bytes 221192 | tf_op jit(solution)/shard_map/ppermute | solution.py:67
  4.7 2.5 %collective-permute-start.4 = (bf16[144,256]{1,0:T(8,128)(2,1)}, bf16[144,256]{1,0:T(8,128)(2,1)S(1)}, u32[]{:S(2)}, u32[]{:S(2)}) collective-permute-start(bf16[144,256]{1,0:T(8,128)(2,1)} %pack.1.own_ref), channel_id=1, source_target_pairs={{0,2},{1,3},{2,0},{3,1},{4,6},{5,7},{6,4},{7,5},{8,10},{9,11},{10,... | collective-permute-start | bytes 221192 | tf_op jit(solution)/shard_map/ppermute | solution.py:67
  7.2 0.4 by_taker.1
  7.6 1.4 %copy-done = bf16[16,2,4,64,128]{4,3,2,1,0:T(8,128)(2,1)} copy-done((bf16[16,2,4,64,128]{4,3,2,1,0:T(8,128)(2,1)}, bf16[16,2,4,64,128]{4,3,2,1,0:T(8,128)(2,1)S(1)}, u32[]{:S(2)}) %copy-start) | copy-done | bytes 2097176
  8.9 1.4 %collective-permute-done.4.two_ref.refs_1_ = bf16[144,256]{1,0:T(8,128)(2,1)S(1)} collective-permute-done((bf16[144,256]{1,0:T(8,128)(2,1)}, bf16[144,256]{1,0:T(8,128)(2,1)S(1)}, u32[]{:S(2)}, u32[]{:S(2)}) %collective-permute-start.4) | collective-permute-done | bytes 73760 | tf_op jit(solution)/shard_map/ppermute | solution.py:67
  10.3 1.9 %collective-permute-done.5.three_ref.refs_2_ = bf16[144,256]{1,0:T(8,128)(2,1)S(1)} collective-permute-done((bf16[144,256]{1,0:T(8,128)(2,1)}, bf16[144,256]{1,0:T(8,128)(2,1)S(1)}, u32[]{:S(2)}, u32[]{:S(2)}) %collective-permute-start.5) | collective-permute-done | bytes 73760 | tf_op jit(solution)/shard_map/ppermute | solution.py:67
  12.3 0.6 copy-done.9
  12.9 6.6 %all-to-all-start = ((bf16[32,256,128]{2,1,0:T(8,128)(2,1)}), bf16[32,256,128]{2,1,0:T(8,128)(2,1)S(1)}, u32[]{:S(2)}, u32[]{:S(2)}) async-start(bf16[32,256,128]{2,1,0:T(8,128)(2,1)} %once.1), calls=%async_computation | async-start | bytes 4194304 | tf_op jit(solution)/shard_map/all_to_all | solution.py:422
  19.5 0.6 stack.23.place_ref.refs_0_
  20.1 2.6 %gather.1 = (f32[8,128]{1,0:T(8,128)}, bf16[128,1024]{1,0:T(8,128)(2,1)}) custom-call(s32[5]{0:T(128)} %stack.23.place_ref.refs_0_, bf16[144,256]{1,0:T(8,128)(2,1)} %pack.1.own_ref, bf16[144,256]{1,0:T(8,128)(2,1)} %copy-done.7, bf16[144,256]{1,0:T(8,128)(2,1)} %copy-done.8, bf16[144,256]{1,0:T(8,128)(2,1)} %copy-done.9), custom_call_target="tpu_custom_call" | custom-call | bytes 1048576 | tf_op jit(solution)/shard_map/gather/pallas_call | solution.py:158
  22.7 0.3 collective-permute-start.9
  23.0 1.6 %collective-permute-start.6 = (f32[8,128]{1,0:T(8,128)}, f32[8,128]{1,0:T(8,128)S(1)}, u32[]{:S(2)}, u32[]{:S(2)}) collective-permute-start(f32[8,128]{1,0:T(8,128)} %get-tuple-element.33), channel_id=1, source_target_pairs={{0,32},{32,0},{64,96},{96,64},{128,160},{160,128},{192,224},{224,1... | collective-permute-start | bytes 12296 | tf_op jit(solution)/shard_map/ppermute | solution.py:425
  24.7 1.5 %collective-permute-done.6 = f32[8,128]{1,0:T(8,128)S(1)} collective-permute-done((f32[8,128]{1,0:T(8,128)}, f32[8,128]{1,0:T(8,128)S(1)}, u32[]{:S(2)}, u32[]{:S(2)}) %collective-permute-start.6) | collective-permute-done | bytes 4128 | tf_op jit(solution)/shard_map/ppermute | solution.py:425
  26.2 0.7 add.17
  26.8 3.0 %collective-permute-start.7 = (f32[8,128]{1,0:T(8,128)S(1)}, f32[8,128]{1,0:T(8,128)S(1)}, u32[]{:S(2)}, u32[]{:S(2)}) collective-permute-start(f32[8,128]{1,0:T(8,128)S(1)} %add.17), channel_id=1, source_target_pairs={{0,64},{32,96},{64,0},{96,32},{128,192},{160,224},{192,128},{224,1... | collective-permute-start | bytes 12296 | tf_op jit(solution)/shard_map/ppermute | solution.py:425
  29.8 4.1 %weigh.1.refs_0_ = f32[128,128]{1,0:T(8,128)} custom-call(s32[1,32]{1,0:T(1,128)} %kept_ref.3, bf16[32,128,128]{2,1,0:T(8,128)(2,1)} %noise_ref.3, bf16[4096,128]{1,0:T(8,128)(2,1)} %map_ref.3), custom_call_target="tpu_custom_call" | custom-call | flops 268435456 | bytes 2097152 | tf_op jit(solution)/shard_map/weigh/pallas_call | solution.py:197
  33.9 1.5 %collective-permute-start = (f32[128,128]{1,0:T(8,128)}, f32[128,128]{1,0:T(8,128)S(1)}, u32[]{:S(2)}, u32[]{:S(2)}) collective-permute-start(f32[128,128]{1,0:T(8,128)} %weigh.1.refs_0_), channel_id=1, source_target_pairs={{0,1},{1,0},{2,3},{3,2},{4,5},{5,4},{6,7},{7,6},{8,9},{9,8},{10,11... | collective-permute-start | bytes 196616 | tf_op jit(solution)/shard_map/ppermute | solution.py:67
  35.4 2.4 %collective-permute-start.1 = (f32[128,128]{1,0:T(8,128)}, f32[128,128]{1,0:T(8,128)S(1)}, u32[]{:S(2)}, u32[]{:S(2)}) collective-permute-start(f32[128,128]{1,0:T(8,128)} %weigh.1.refs_0_), channel_id=1, source_target_pairs={{0,2},{1,3},{2,0},{3,1},{4,6},{5,7},{6,4},{7,5},{8,10},{9,11},{10,... | collective-permute-start | bytes 196616 | tf_op jit(solution)/shard_map/ppermute | solution.py:67
  37.9 5.0 %collective-permute-start.8 = (f32[8,128]{1,0:T(8,128)S(1)}, f32[8,128]{1,0:T(8,128)S(1)}, u32[]{:S(2)}, u32[]{:S(2)}) collective-permute-start(f32[8,128]{1,0:T(8,128)S(1)} %add.18), channel_id=1, source_target_pairs={{0,128},{32,160},{64,192},{96,224},{128,0},{160,32},{192,64},{224,... | collective-permute-start | bytes 12296 | tf_op jit(solution)/shard_map/ppermute | solution.py:425
  42.9 1.7 %collective-permute-done.8 = f32[8,128]{1,0:T(8,128)S(1)} collective-permute-done((f32[8,128]{1,0:T(8,128)S(1)}, f32[8,128]{1,0:T(8,128)S(1)}, u32[]{:S(2)}, u32[]{:S(2)}) %collective-permute-start.8) | collective-permute-done | bytes 4128 | tf_op jit(solution)/shard_map/ppermute | solution.py:425
  44.6 0.8 masks.1
  45.4 0.9 all-to-all-done
  46.3 2.9 %rows.1 = (f32[4,128,128]{2,1,0:T(8,128)}, f32[8,128]{1,0:T(8,128)S(1)}) custom-call(s32[5]{0:T(128)S(1)} %copy-done.4, f32[8,2048]{1,0:T(8,128)S(1)} %get-tuple-element.35.mask_ref, bf16[128,2048]{1,0:T(8,128)(2,1)S(1)} %get-tuple-element.36.plane_ref, bf16[8,4,4,64,128]{4,3,2,1,0:T(8,128)(2,1)S(1)} %bitcast.15), custom_call_target="tpu_custom_call" | custom-call | flops 268435456 | bytes 3145728 | tf_op jit(solution)/shard_map/rows/pallas_call | solution.py:327
  49.2 8.2 %all-to-all-start.1 = ((f32[8,64,128]{2,1,0:T(8,128)}), f32[8,64,128]{2,1,0:T(8,128)S(1)}, u32[]{:S(2)}, u32[]{:S(2)}) async-start(f32[8,64,128]{2,1,0:T(8,128)} %bitcast.8), calls=%async_computation.1 | async-start | bytes 524288 | tf_op jit(solution)/shard_map/all_to_all | solution.py:435
  57.6 1.8 %powers.1 = (f32[8,128,128]{2,1,0:T(8,128)S(1)}, f32[128,128]{1,0:T(8,128)S(1)}) custom-call(f32[128,128]{1,0:T(8,128)S(1)} %copy-done.3, f32[128,128]{1,0:T(8,128)S(1)} %collective-permute-done.refs_1_, f32[128,128]{1,0:T(8,128)S(1)} %collective-permute-done.1.refs_2_, f32[128,128]{1,0:T(8,128)S(1)} %collective-permute-done.2.refs_3_, ...), custom_call_target="tpu_custom_call" | custom-call | flops 40000000000 | bytes 1048576 | tf_op jit(solution)/shard_map/powers/pallas_call | solution.py:34
  59.3 1.7 %collective-permute-start.10 = (f32[128,128]{1,0:T(8,128)S(1)}, f32[128,128]{1,0:T(8,128)S(1)}, u32[]{:S(2)}, u32[]{:S(2)}) collective-permute-start(f32[128,128]{1,0:T(8,128)S(1)} %get-tuple-element.38.refs_1_), channel_id=1, source_target_pairs={{0,4},{4,0},{1,5},{5,1},{2,6},{6,2},{3,7},{7,3},{8,12},{12,8},{9,1... | collective-permute-start | bytes 196616 | tf_op jit(solution)/shard_map/ppermute | solution.py:455
  61.0 0.9 collective-permute-done.10.refs_2_
  62.0 0.8 pairs.1
  62.7 1.3 %collective-permute-start.11 = (f32[128,128]{1,0:T(8,128)S(1)}, f32[128,128]{1,0:T(8,128)S(1)}, u32[]{:S(2)}, u32[]{:S(2)}) collective-permute-start(f32[128,128]{1,0:T(8,128)S(1)} %get-tuple-element.39.refs_1_), channel_id=1, source_target_pairs={{0,8},{8,0},{16,24},{24,16},{1,9},{9,1},{17,25},{25,17},{2,10},{10... | collective-permute-start | bytes 196616 | tf_op jit(solution)/shard_map/ppermute | solution.py:460
  64.0 1.5 %collective-permute-start.12 = (f32[128,128]{1,0:T(8,128)S(1)}, f32[128,128]{1,0:T(8,128)S(1)}, u32[]{:S(2)}, u32[]{:S(2)}) collective-permute-start(f32[128,128]{1,0:T(8,128)S(1)} %get-tuple-element.39.refs_1_), channel_id=1, source_target_pairs={{0,16},{8,24},{16,0},{24,8},{1,17},{9,25},{17,1},{25,9},{2,18},{10... | collective-permute-start | bytes 196616 | tf_op jit(solution)/shard_map/ppermute | solution.py:460
  65.5 1.2 %collective-permute-start.13 = (f32[128,128]{1,0:T(8,128)S(1)}, f32[128,128]{1,0:T(8,128)S(1)}, u32[]{:S(2)}, u32[]{:S(2)}) collective-permute-start(f32[128,128]{1,0:T(8,128)S(1)} %get-tuple-element.39.refs_1_), channel_id=1, source_target_pairs={{0,24},{8,16},{16,8},{24,0},{1,25},{9,17},{17,9},{25,1},{2,26},{10... | collective-permute-start | bytes 196616 | tf_op jit(solution)/shard_map/ppermute | solution.py:460
  66.7 0.6 all-to-all-done.1
  67.3 0.7 collective-permute-start.17
  67.9 5.3 %collective-permute-start.18 = (f32[64,128]{1,0:T(8,128)S(1)}, f32[64,128]{1,0:T(8,128)S(1)}, u32[]{:S(2)}, u32[]{:S(2)}) collective-permute-start(f32[64,128]{1,0:T(8,128)S(1)} %reduce_sum.9), channel_id=1, source_target_pairs={{0,1},{1,33},{2,3},{3,35},{32,0},{33,32},{34,2},{35,34},{64,65},{6... | collective-permute-start | bytes 98312 | tf_op jit(solution)/shard_map/ppermute | solution.py:76
  73.2 0.6 quads.1
  73.8 1.3 %collective-permute-start.14 = (f32[128,128]{1,0:T(8,128)S(1)}, f32[128,128]{1,0:T(8,128)S(1)}, u32[]{:S(2)}, u32[]{:S(2)}) collective-permute-start(f32[128,128]{1,0:T(8,128)S(1)} %get-tuple-element.42.refs_1_), channel_id=1, source_target_pairs={{0,32},{32,0},{64,96},{96,64},{128,160},{160,128},{192,224},{224,1... | collective-permute-start | bytes 196616 | tf_op jit(solution)/shard_map/ppermute | solution.py:467
  75.1 2.3 %collective-permute-start.16 = (f32[128,128]{1,0:T(8,128)S(1)}, f32[128,128]{1,0:T(8,128)S(1)}, u32[]{:S(2)}, u32[]{:S(2)}) collective-permute-start(f32[128,128]{1,0:T(8,128)S(1)} %get-tuple-element.42.refs_1_), channel_id=1, source_target_pairs={{0,96},{32,64},{64,32},{96,0},{128,224},{160,192},{192,160},{224,1... | collective-permute-start | bytes 196616 | tf_op jit(solution)/shard_map/ppermute | solution.py:467
  77.5 3.1 %collective-permute-start.19 = (f32[64,128]{1,0:T(8,128)S(1)}, f32[64,128]{1,0:T(8,128)S(1)}, u32[]{:S(2)}, u32[]{:S(2)}) collective-permute-start(f32[64,128]{1,0:T(8,128)S(1)} %reduce_sum.9), channel_id=1, source_target_pairs={{0,2},{1,34},{2,0},{3,32},{32,3},{33,35},{34,1},{35,33},{64,66},{6... | collective-permute-start | bytes 98312 | tf_op jit(solution)/shard_map/ppermute | solution.py:76
  80.7 0.5 factors.1
  81.2 0.8 collective-permute-done.19.refs_3_
  82.0 4.1 %collective-permute-done.20.refs_4_ = f32[64,128]{1,0:T(8,128)S(1)} collective-permute-done((f32[64,128]{1,0:T(8,128)S(1)}, f32[64,128]{1,0:T(8,128)S(1)}, u32[]{:S(2)}, u32[]{:S(2)}) %collective-permute-start.20) | collective-permute-done | bytes 32800 | tf_op jit(solution)/shard_map/ppermute | solution.py:76
  86.1 1.5 %tail.1 = (f32[256,128]{1,0:T(8,128)S(1)}, f32[8,128]{1,0:T(8,128)S(1)}, f32[64,128]{1,0:T(8,128)S(1)}) custom-call(s32[5]{0:T(128)S(1)} %copy-done.4, f32[64,128]{1,0:T(8,128)S(1)} %collective-permute-done.17.refs_1_, f32[64,128]{1,0:T(8,128)S(1)} %collective-permute-done.18.refs_2_, f32[64,128]{1,0:T(8,128)S(1)} %collective-permute-done.19.refs_3_, ...), custom_call_target="tpu_custom_call" | custom-call | flops 201326592 | bytes 1048576 | tf_op jit(solution)/shard_map/tail/pallas_call | solution.py:34
  87.6 1.8 %far.1 = (bf16[384,128]{1,0:T(8,128)(2,1)S(1)}, bf16[384,128]{1,0:T(8,128)(2,1)S(1)}, f32[64,128]{1,0:T(8,128)}) custom-call(s32[5]{0:T(128)S(1)} %copy-done.4, f32[128,128]{1,0:T(8,128)S(1)} %get-tuple-element.42.refs_1_, f32[128,128]{1,0:T(8,128)S(1)} %collective-permute-done.14.refs_2_, f32[128,128]{1,0:T(8,128)S(1)} %collective-permute-done.15.refs_3_, ...), custom_call_target="tpu_custom_call" | custom-call | flops 125829120 | bytes 1048576 | tf_op jit(solution)/shard_map/far/pallas_call | solution.py:34
  89.4 8.5 %all-to-all-start.2 = ((f32[64,1,128]{2,1,0:T(1,128)}), f32[64,1,128]{2,1,0:T(1,128)S(1)}, u32[]{:S(2)}, u32[]{:S(2)}) async-start(f32[64,1,128]{2,1,0:T(1,128)} %bitcast.11), calls=%async_computation.2 | async-start | bytes 65536 | tf_op jit(solution)/shard_map/all_to_all | solution.py:480
  97.9 1.2 %sweep.1.refs_3_ = f32[256,128]{1,0:T(8,128)S(1)} custom-call(f32[256,128]{1,0:T(8,128)S(1)} %get-tuple-element.55.refs_0_, bf16[4,384,384]{2,1,0:T(8,128)(2,1)S(1)} %get-tuple-element.48.refs_8_.refs_1_.refs_2_), custom_call_target="tpu_custom_call" | custom-call | flops 402653184 | bytes 1048576 | tf_op jit(solution)/shard_map/sweep/pallas_call | solution.py:34
  99.1 8.1 %all-to-all-done.2 = f32[64,1,128]{2,1,0:T(1,128)S(1)} async-done(((f32[64,1,128]{2,1,0:T(1,128)}), f32[64,1,128]{2,1,0:T(1,128)S(1)}, u32[]{:S(2)}, u32[]{:S(2)}) %all-to-all-start.2) | async-done | bytes 32800 | tf_op jit(solution)/shard_map/all_to_all | solution.py:480
  107.2 2.1 %states.1 = f32[256,128]{1,0:T(8,128)} custom-call(s32[5]{0:T(128)S(1)} %copy-done.4, f32[64,128]{1,0:T(8,128)S(1)} %bitcast.16, bf16[4,384,384]{2,1,0:T(8,128)(2,1)S(1)} %get-tuple-element.48.refs_8_.refs_1_.refs_2_, f32[256,128]{1,0:T(8,128)S(1)} %sweep.1.refs_3_, bf16[384,128]{1,0:T(8,128)(2,1)S(1)} %get-tuple-element.56.refs_4_, ...), custom_call_target="tpu_custom_call" | custom-call | flops 377487360 | bytes 1048576 | tf_op jit(solution)/shard_map/states/pallas_call | solution.py:34
  (42 shorter events, 0.5 us)
Async XLA Ops:
  0.0 7.2 %copy-start.1 = (bf16[64,16384]{1,0:T(8,128)(2,1)S(1)}, bf16[64,16384]{1,0:T(8,128)(2,1)}, u32[]{:S(2)}) copy-start(bf16[64,16384]{1,0:T(8,128)(2,1)} %rows_ref.1) | copy-start | bytes 6291460
  2.6 6.4 %collective-permute-start.3 = (bf16[144,256]{1,0:T(8,128)(2,1)}, bf16[144,256]{1,0:T(8,128)(2,1)S(1)}, u32[]{:S(2)}, u32[]{:S(2)}) collective-permute-start(bf16[144,256]{1,0:T(8,128)(2,1)} %pack.1.own_ref), channel_id=1, source_target_pairs={{0,1},{1,0},{2,3},{3,2},{4,5},{5,4},{6,7},{7,6},{8,9},{9,8},{10,11... | collective-permute-start | bytes 221192 | tf_op jit(solution)/shard_map/ppermute | solution.py:67
  4.7 5.6 %collective-permute-start.4 = (bf16[144,256]{1,0:T(8,128)(2,1)}, bf16[144,256]{1,0:T(8,128)(2,1)S(1)}, u32[]{:S(2)}, u32[]{:S(2)}) collective-permute-start(bf16[144,256]{1,0:T(8,128)(2,1)} %pack.1.own_ref), channel_id=1, source_target_pairs={{0,2},{1,3},{2,0},{3,1},{4,6},{5,7},{6,4},{7,5},{8,10},{9,11},{10,... | collective-permute-start | bytes 221192 | tf_op jit(solution)/shard_map/ppermute | solution.py:67
  7.2 5.1 %collective-permute-start.5 = (bf16[144,256]{1,0:T(8,128)(2,1)}, bf16[144,256]{1,0:T(8,128)(2,1)S(1)}, u32[]{:S(2)}, u32[]{:S(2)}) collective-permute-start(bf16[144,256]{1,0:T(8,128)(2,1)} %pack.1.own_ref), channel_id=1, source_target_pairs={{0,3},{1,2},{2,1},{3,0},{4,7},{5,6},{6,5},{7,4},{8,11},{9,10},{10,... | collective-permute-start | bytes 221192 | tf_op jit(solution)/shard_map/ppermute | solution.py:67
  7.6 1.4 %copy-start = (bf16[16,2,4,64,128]{4,3,2,1,0:T(8,128)(2,1)}, bf16[16,2,4,64,128]{4,3,2,1,0:T(8,128)(2,1)S(1)}, u32[]{:S(2)}) copy-start(bf16[16,2,4,64,128]{4,3,2,1,0:T(8,128)(2,1)S(1)} %by_taker.1) | copy-start | bytes 6291460
  8.9 3.3 %copy-start.7 = (bf16[144,256]{1,0:T(8,128)(2,1)}, bf16[144,256]{1,0:T(8,128)(2,1)S(1)}, u32[]{:S(2)}) copy-start(bf16[144,256]{1,0:T(8,128)(2,1)S(1)} %collective-permute-done.3.one_ref.refs_0_) | copy-start | bytes 221188
  10.3 1.9 %copy-start.8 = (bf16[144,256]{1,0:T(8,128)(2,1)}, bf16[144,256]{1,0:T(8,128)(2,1)S(1)}, u32[]{:S(2)}) copy-start(bf16[144,256]{1,0:T(8,128)(2,1)S(1)} %collective-permute-done.4.two_ref.refs_1_) | copy-start | bytes 221188
  12.3 0.6 copy-start.9
  12.9 33.4 %all-to-all-start = ((bf16[32,256,128]{2,1,0:T(8,128)(2,1)}), bf16[32,256,128]{2,1,0:T(8,128)(2,1)S(1)}, u32[]{:S(2)}, u32[]{:S(2)}) async-start(bf16[32,256,128]{2,1,0:T(8,128)(2,1)} %once.1), calls=%async_computation | async-start | bytes 4194304 | tf_op jit(solution)/shard_map/all_to_all | solution.py:422
  19.5 23.4 %copy-start.5 = (f32[128]{0:T(128)S(1)}, f32[128]{0:T(128)}, u32[]{:S(2)}) copy-start(f32[128]{0:T(128)} %param.10) | copy-start | bytes 1540
  20.1 24.5 %copy-start.4 = (s32[5]{0:T(128)S(1)}, s32[5]{0:T(128)}, u32[]{:S(2)}) copy-start(s32[5]{0:T(128)} %stack.23.place_ref.refs_0_) | copy-start | bytes 64
  22.7 21.9 %copy-start.2 = (bf16[128,1024]{1,0:T(8,128)(2,1)S(1)}, bf16[128,1024]{1,0:T(8,128)(2,1)}, u32[]{:S(2)}) copy-start(bf16[128,1024]{1,0:T(8,128)(2,1)} %get-tuple-element.34.refs_2_) | copy-start | bytes 786436
  22.7 21.9 %collective-permute-start.9 = (bf16[128,1024]{1,0:T(8,128)(2,1)}, bf16[128,1024]{1,0:T(8,128)(2,1)S(1)}, u32[]{:S(2)}, u32[]{:S(2)}) collective-permute-start(bf16[128,1024]{1,0:T(8,128)(2,1)} %get-tuple-element.34.refs_2_), channel_id=1, source_target_pairs={{0,4},{4,0},{1,5},{5,1},{2,6},{6,2},{3,7},{7,3},{8,12},{12,8},{9,1... | collective-permute-start | bytes 786440 | tf_op jit(solution)/shard_map/ppermute | solution.py:427
  23.0 3.1 %collective-permute-start.6 = (f32[8,128]{1,0:T(8,128)}, f32[8,128]{1,0:T(8,128)S(1)}, u32[]{:S(2)}, u32[]{:S(2)}) collective-permute-start(f32[8,128]{1,0:T(8,128)} %get-tuple-element.33), channel_id=1, source_target_pairs={{0,32},{32,0},{64,96},{96,64},{128,160},{160,128},{192,224},{224,1... | collective-permute-start | bytes 12296 | tf_op jit(solution)/shard_map/ppermute | solution.py:425
  26.8 11.1 %collective-permute-start.7 = (f32[8,128]{1,0:T(8,128)S(1)}, f32[8,128]{1,0:T(8,128)S(1)}, u32[]{:S(2)}, u32[]{:S(2)}) collective-permute-start(f32[8,128]{1,0:T(8,128)S(1)} %add.17), channel_id=1, source_target_pairs={{0,64},{32,96},{64,0},{96,32},{128,192},{160,224},{192,128},{224,1... | collective-permute-start | bytes 12296 | tf_op jit(solution)/shard_map/ppermute | solution.py:425
  33.9 23.6 %copy-start.3 = (f32[128,128]{1,0:T(8,128)S(1)}, f32[128,128]{1,0:T(8,128)}, u32[]{:S(2)}) copy-start(f32[128,128]{1,0:T(8,128)} %weigh.1.refs_0_) | copy-start | bytes 196612
  33.9 23.5 %collective-permute-start = (f32[128,128]{1,0:T(8,128)}, f32[128,128]{1,0:T(8,128)S(1)}, u32[]{:S(2)}, u32[]{:S(2)}) collective-permute-start(f32[128,128]{1,0:T(8,128)} %weigh.1.refs_0_), channel_id=1, source_target_pairs={{0,1},{1,0},{2,3},{3,2},{4,5},{5,4},{6,7},{7,6},{8,9},{9,8},{10,11... | collective-permute-start | bytes 196616 | tf_op jit(solution)/shard_map/ppermute | solution.py:67
  35.4 22.0 %collective-permute-start.1 = (f32[128,128]{1,0:T(8,128)}, f32[128,128]{1,0:T(8,128)S(1)}, u32[]{:S(2)}, u32[]{:S(2)}) collective-permute-start(f32[128,128]{1,0:T(8,128)} %weigh.1.refs_0_), channel_id=1, source_target_pairs={{0,2},{1,3},{2,0},{3,1},{4,6},{5,7},{6,4},{7,5},{8,10},{9,11},{10,... | collective-permute-start | bytes 196616 | tf_op jit(solution)/shard_map/ppermute | solution.py:67
  37.8 19.6 %collective-permute-start.2 = (f32[128,128]{1,0:T(8,128)}, f32[128,128]{1,0:T(8,128)S(1)}, u32[]{:S(2)}, u32[]{:S(2)}) collective-permute-start(f32[128,128]{1,0:T(8,128)} %weigh.1.refs_0_), channel_id=1, source_target_pairs={{0,3},{1,2},{2,1},{3,0},{4,7},{5,6},{6,5},{7,4},{8,11},{9,10},{10,... | collective-permute-start | bytes 196616 | tf_op jit(solution)/shard_map/ppermute | solution.py:67
  37.9 6.7 %collective-permute-start.8 = (f32[8,128]{1,0:T(8,128)S(1)}, f32[8,128]{1,0:T(8,128)S(1)}, u32[]{:S(2)}, u32[]{:S(2)}) collective-permute-start(f32[8,128]{1,0:T(8,128)S(1)} %add.18), channel_id=1, source_target_pairs={{0,128},{32,160},{64,192},{96,224},{128,0},{160,32},{192,64},{224,... | collective-permute-start | bytes 12296 | tf_op jit(solution)/shard_map/ppermute | solution.py:425
  49.2 18.0 %all-to-all-start.1 = ((f32[8,64,128]{2,1,0:T(8,128)}), f32[8,64,128]{2,1,0:T(8,128)S(1)}, u32[]{:S(2)}, u32[]{:S(2)}) async-start(f32[8,64,128]{2,1,0:T(8,128)} %bitcast.8), calls=%async_computation.1 | async-start | bytes 524288 | tf_op jit(solution)/shard_map/all_to_all | solution.py:435
  57.6 28.5 %copy-start.6 = (f32[128]{0:T(128)S(1)}, f32[128]{0:T(128)}, u32[]{:S(2)}) copy-start(f32[128]{0:T(128)} %param.11) | copy-start | bytes 1540
  59.3 2.6 %collective-permute-start.10 = (f32[128,128]{1,0:T(8,128)S(1)}, f32[128,128]{1,0:T(8,128)S(1)}, u32[]{:S(2)}, u32[]{:S(2)}) collective-permute-start(f32[128,128]{1,0:T(8,128)S(1)} %get-tuple-element.38.refs_1_), channel_id=1, source_target_pairs={{0,4},{4,0},{1,5},{5,1},{2,6},{6,2},{3,7},{7,3},{8,12},{12,8},{9,1... | collective-permute-start | bytes 196616 | tf_op jit(solution)/shard_map/ppermute | solution.py:455
  62.7 10.5 %collective-permute-start.11 = (f32[128,128]{1,0:T(8,128)S(1)}, f32[128,128]{1,0:T(8,128)S(1)}, u32[]{:S(2)}, u32[]{:S(2)}) collective-permute-start(f32[128,128]{1,0:T(8,128)S(1)} %get-tuple-element.39.refs_1_), channel_id=1, source_target_pairs={{0,8},{8,0},{16,24},{24,16},{1,9},{9,1},{17,25},{25,17},{2,10},{10... | collective-permute-start | bytes 196616 | tf_op jit(solution)/shard_map/ppermute | solution.py:460
  64.0 9.2 %collective-permute-start.12 = (f32[128,128]{1,0:T(8,128)S(1)}, f32[128,128]{1,0:T(8,128)S(1)}, u32[]{:S(2)}, u32[]{:S(2)}) collective-permute-start(f32[128,128]{1,0:T(8,128)S(1)} %get-tuple-element.39.refs_1_), channel_id=1, source_target_pairs={{0,16},{8,24},{16,0},{24,8},{1,17},{9,25},{17,1},{25,9},{2,18},{10... | collective-permute-start | bytes 196616 | tf_op jit(solution)/shard_map/ppermute | solution.py:460
  65.5 7.7 %collective-permute-start.13 = (f32[128,128]{1,0:T(8,128)S(1)}, f32[128,128]{1,0:T(8,128)S(1)}, u32[]{:S(2)}, u32[]{:S(2)}) collective-permute-start(f32[128,128]{1,0:T(8,128)S(1)} %get-tuple-element.39.refs_1_), channel_id=1, source_target_pairs={{0,24},{8,16},{16,8},{24,0},{1,25},{9,17},{17,9},{25,1},{2,26},{10... | collective-permute-start | bytes 196616 | tf_op jit(solution)/shard_map/ppermute | solution.py:460
  67.3 10.2 %collective-permute-start.17 = (f32[64,128]{1,0:T(8,128)S(1)}, f32[64,128]{1,0:T(8,128)S(1)}, u32[]{:S(2)}, u32[]{:S(2)}) collective-permute-start(f32[64,128]{1,0:T(8,128)S(1)} %reduce_sum.9), channel_id=1, source_target_pairs={{0,0},{1,32},{2,2},{3,34},{32,1},{33,33},{34,3},{35,35},{64,64},{6... | collective-permute-start | bytes 98312 | tf_op jit(solution)/shard_map/ppermute | solution.py:76
  67.9 12.6 %collective-permute-start.18 = (f32[64,128]{1,0:T(8,128)S(1)}, f32[64,128]{1,0:T(8,128)S(1)}, u32[]{:S(2)}, u32[]{:S(2)}) collective-permute-start(f32[64,128]{1,0:T(8,128)S(1)} %reduce_sum.9), channel_id=1, source_target_pairs={{0,1},{1,33},{2,3},{3,35},{32,0},{33,32},{34,2},{35,34},{64,65},{6... | collective-permute-start | bytes 98312 | tf_op jit(solution)/shard_map/ppermute | solution.py:76
  73.8 13.8 %collective-permute-start.14 = (f32[128,128]{1,0:T(8,128)S(1)}, f32[128,128]{1,0:T(8,128)S(1)}, u32[]{:S(2)}, u32[]{:S(2)}) collective-permute-start(f32[128,128]{1,0:T(8,128)S(1)} %get-tuple-element.42.refs_1_), channel_id=1, source_target_pairs={{0,32},{32,0},{64,96},{96,64},{128,160},{160,128},{192,224},{224,1... | collective-permute-start | bytes 196616 | tf_op jit(solution)/shard_map/ppermute | solution.py:467
  75.1 12.5 %collective-permute-start.15 = (f32[128,128]{1,0:T(8,128)S(1)}, f32[128,128]{1,0:T(8,128)S(1)}, u32[]{:S(2)}, u32[]{:S(2)}) collective-permute-start(f32[128,128]{1,0:T(8,128)S(1)} %get-tuple-element.42.refs_1_), channel_id=1, source_target_pairs={{0,64},{32,96},{64,0},{96,32},{128,192},{160,224},{192,128},{224,1... | collective-permute-start | bytes 196616 | tf_op jit(solution)/shard_map/ppermute | solution.py:467
  75.1 12.5 %collective-permute-start.16 = (f32[128,128]{1,0:T(8,128)S(1)}, f32[128,128]{1,0:T(8,128)S(1)}, u32[]{:S(2)}, u32[]{:S(2)}) collective-permute-start(f32[128,128]{1,0:T(8,128)S(1)} %get-tuple-element.42.refs_1_), channel_id=1, source_target_pairs={{0,96},{32,64},{64,32},{96,0},{128,224},{160,192},{192,160},{224,1... | collective-permute-start | bytes 196616 | tf_op jit(solution)/shard_map/ppermute | solution.py:467
  77.5 4.5 %collective-permute-start.19 = (f32[64,128]{1,0:T(8,128)S(1)}, f32[64,128]{1,0:T(8,128)S(1)}, u32[]{:S(2)}, u32[]{:S(2)}) collective-permute-start(f32[64,128]{1,0:T(8,128)S(1)} %reduce_sum.9), channel_id=1, source_target_pairs={{0,2},{1,34},{2,0},{3,32},{32,3},{33,35},{34,1},{35,33},{64,66},{6... | collective-permute-start | bytes 98312 | tf_op jit(solution)/shard_map/ppermute | solution.py:76
  80.5 5.6 %collective-permute-start.20 = (f32[64,128]{1,0:T(8,128)S(1)}, f32[64,128]{1,0:T(8,128)S(1)}, u32[]{:S(2)}, u32[]{:S(2)}) collective-permute-start(f32[64,128]{1,0:T(8,128)S(1)} %reduce_sum.9), channel_id=1, source_target_pairs={{0,3},{1,35},{2,1},{3,33},{32,2},{33,34},{34,0},{35,32},{64,67},{6... | collective-permute-start | bytes 98312 | tf_op jit(solution)/shard_map/ppermute | solution.py:76
  89.4 17.8 %all-to-all-start.2 = ((f32[64,1,128]{2,1,0:T(1,128)}), f32[64,1,128]{2,1,0:T(1,128)S(1)}, u32[]{:S(2)}, u32[]{:S(2)}) async-start(f32[64,1,128]{2,1,0:T(1,128)} %bitcast.11), calls=%async_computation.2 | async-start | bytes 65536 | tf_op jit(solution)/shard_map/all_to_all | solution.py:480

commit v4 on v3

--- a/solution.py
+++ b/solution.py
@@ -11,7 +11,6 @@
 LEVELS = 8
 SCAN = 6
 LANES = 128
-TAKERS = NY * NC * 2
 HIGHEST = lax.Precision.HIGHEST
 WHOLE = pl.BlockSpec(memory_space=pltpu.VMEM)
 SCALARS = pl.BlockSpec(memory_space=pltpu.SMEM)
@@ -67,35 +66,30 @@
     return lax.ppermute(block, "x", [(i, i ^ distance) for i in range(NX)])
 
 
-def rows_to_block(piece, distance):
-    route = []
-    for z in range(NZ):
-        for x in range(NX):
-            part = 2 * (x // 2) + z % 2
-            route.append((z * NX + x, (z // 2 * 2 + x % 2) * NX + (part ^ distance)))
-    return lax.ppermute(piece, ("z", "x"), route)
-
-
 def order_kernel(rows_ref, out_ref):
-    for m in range(NZ // 2):
-        for par in range(2):
-            for j in range(TAKERS):
-                lane = ((m * 2 + par) * TAKERS + j) * LANES
-                out_ref[j, par, m] = rows_ref[:, lane : lane + LANES]
+    half, side = rows_ref.shape[0] // 2, LANES // 2
+    for k in range(NZ):
+        for j in range(NY * NC):
+            for pair in range(2):
+                lane = ((k * NY * NC + j) * 2 + pair) * LANES
+                upper = rows_ref[:half, lane : lane + LANES]
+                lower = rows_ref[half:, lane : lane + LANES]
+                out_ref[j, 2 * pair, k] = jnp.concatenate([upper[:, :side], lower[:, :side]], 1)
+                out_ref[j, 2 * pair + 1, k] = jnp.concatenate([upper[:, side:], lower[:, side:]], 1)
 
 
 def by_taker(observations):
-    rows = observations.shape[0]
+    half = observations.shape[0] // 2
     out = pl.pallas_call(
         order_kernel,
         name="by_taker",
-        out_shape=jax.ShapeDtypeStruct((TAKERS, 2, NZ // 2, rows, LANES), jnp.bfloat16),
+        out_shape=jax.ShapeDtypeStruct((NY * NC, NX, NZ, half, LANES), jnp.bfloat16),
         in_specs=[WHOLE],
         out_specs=WHOLE,
         cost_estimate=pl.CostEstimate(flops=0, bytes_accessed=4 << 20, transcendentals=0),
         compiler_params=pltpu.CompilerParams(vmem_limit_bytes=32 << 20),
     )(observations)
-    return out.reshape(TAKERS * 2, NZ // 2 * rows, LANES)
+    return out.reshape(NY * NC * NX, NZ * half, LANES)
 
 
 def pack_kernel(kept_ref, noise_ref, map_ref, out_ref, noise_held, map_held, sems):
@@ -286,54 +280,54 @@
 
 def mask_kernel(place_ref, kept_ref, own_ref, other_ref, plane_ref, mask_ref):
     x, z, c = place_ref[0], place_ref[2], place_ref[3]
-    half = NZ // 2
-    zs = lax.broadcasted_iota(jnp.int32, (NZ, NZ), 1)
-    pick = lax.broadcasted_iota(jnp.int32, (NZ, NZ), 0) * 2 + x % 2
-    kept = jnp.dot(
-        jnp.where(zs == pick, 1.0, 0.0).astype(jnp.bfloat16),
-        kept_ref[...].astype(jnp.bfloat16),
-        preferred_element_type=jnp.float32,
-    ).astype(jnp.bfloat16)
     width = NY * LANES
-    block = lax.broadcasted_iota(jnp.int32, (LANES, width), 0)
-    lane = lax.broadcasted_iota(jnp.int32, (LANES, width), 1) // LANES
+    kept = kept_ref[...].astype(jnp.bfloat16)
+    block = lax.broadcasted_iota(jnp.int32, (LANES, width // 2), 0)
+    lane = lax.broadcasted_iota(jnp.int32, (LANES, width // 2), 1) // (LANES // 2)
+    source = lax.broadcasted_iota(jnp.int32, (width, width // 2), 0)
+    target = lax.broadcasted_iota(jnp.int32, (width, width // 2), 1)
+    picks = [
+        jnp.where(source == target // 32 * 64 + target % 32 + 32 * side, 1.0, 0.0).astype(jnp.bfloat16)
+        for side in range(2)
+    ]
     for r in range(NX):
-        own, other = own_ref[:, r * width // 2 : (r + 1) * width // 2], other_ref[:, r * width // 2 : (r + 1) * width // 2]
-        plane_ref[:, r * width : r * width + width // 2] = jnp.where(c == 0, own, other)
-        plane_ref[:, r * width + width // 2 : (r + 1) * width] = jnp.where(c == 0, other, own)
+        lanes = slice(r * width // 2, (r + 1) * width // 2)
+        own, other = own_ref[:, lanes], other_ref[:, lanes]
+        whole = jnp.concatenate([jnp.where(c == 0, own, other), jnp.where(c == 0, other, own)], 1)
+        for side in range(2):
+            plane_ref[side * LANES : (side + 1) * LANES, lanes] = jnp.dot(
+                whole, picks[side], preferred_element_type=jnp.float32
+            ).astype(jnp.bfloat16)
         spread = jnp.where(block == (x ^ r) * (NZ * NY) + z * NY + lane, 1.0, 0.0).astype(jnp.bfloat16)
-        mask_ref[:, r * width : (r + 1) * width] = jnp.dot(kept, spread, preferred_element_type=jnp.float32)
-
-
-def rows_kernel(place_ref, mask_ref, plane_ref, got_ref, out_ref, token_ref, held_ref, sems):
+        mask_ref[:, lanes] = jnp.dot(kept, spread, preferred_element_type=jnp.float32)
+
+
+def rows_kernel(place_ref, mask_ref, plane_ref, got_ref, out_ref, token_ref):
+    x = place_ref[0]
     token_ref[...] = jnp.zeros((8, LANES), jnp.float32)
-    x = place_ref[0]
-    width = NY * LANES
-    copies = [
-        pltpu.make_async_copy(got_ref.at[:, :, m], held_ref.at[m], sems.at[m]) for m in range(NZ // 2)
-    ]
-    for copy in copies:
-        copy.start()
-    for m, copy in enumerate(copies):
-        copy.wait()
-        mask = mask_ref[m : m + 1, :].astype(jnp.bfloat16)
-        weights = plane_ref[...] * mask
-        readings = jnp.concatenate([held_ref[m, :, x ^ r].reshape(width, LANES) for r in range(NX)], 0)
-        out_ref[m] = jnp.dot(weights, readings, preferred_element_type=jnp.float32).T
+    rows = plane_ref.shape[1] // NX
+    side = LANES // 2
+    left = lax.broadcasted_iota(jnp.int32, (LANES, LANES), 1) < side
+    for k in range(NZ):
+        weights = plane_ref[...] * mask_ref[k : k + 1, :].astype(jnp.bfloat16)
+        readings = jnp.concatenate([got_ref[:, x ^ r, k].reshape(rows, LANES) for r in range(NX)], 0)
+        both = jnp.dot(weights, readings, preferred_element_type=jnp.float32)
+        upper, lower = both[:LANES], both[LANES:]
+        if k % 2 == 0:
+            first = upper + pltpu.roll(lower, side, 1)
+        else:
+            second = lower + pltpu.roll(upper, side, 1)
+            pair = jnp.where(left, first, second).T
+            out_ref[k - 1], out_ref[k] = pair[:side], pair[side:]
 
 
 def info_rows(place, masks, plane, received):
-    takers, _, steps, rows, _ = received.shape
     return pl.pallas_call(
         rows_kernel,
         name="rows",
-        out_shape=[f32(steps, LANES, LANES), f32(8, LANES)],
-        in_specs=[SCALARS, WHOLE, WHOLE, pl.BlockSpec(memory_space=pl.ANY)],
+        out_shape=[f32(NZ, LANES // 2, LANES), f32(8, LANES)],
+        in_specs=[SCALARS, WHOLE, WHOLE, WHOLE],
         out_specs=[WHOLE] * 2,
-        scratch_shapes=[
-            pltpu.VMEM((steps, takers, NX, rows, LANES), jnp.bfloat16),
-            pltpu.SemaphoreType.DMA((steps,)),
-        ],
         cost_estimate=pl.CostEstimate(flops=1 << 28, bytes_accessed=3 << 20, transcendentals=0),
         compiler_params=pltpu.CompilerParams(vmem_limit_bytes=32 << 20),
     )(place, masks, plane, received)
@@ -425,16 +419,16 @@
         kept = kept + lax.ppermute(kept, "z", [(i, i ^ flip) for i in range(NZ)])
     plane, masks = local(
         mask_kernel, "masks", [place], [kept, half, lax.ppermute(half, "c", [(0, 1), (1, 0)])],
-        [jax.ShapeDtypeStruct((modes, NX * NY * modes), jnp.bfloat16), f32(NZ, NX * NY * modes)], 1 << 20,
+        [jax.ShapeDtypeStruct((2 * modes, NX * NY * modes // 2), jnp.bfloat16), f32(NZ, NX * NY * modes // 2)], 1 << 20,
     )
 
     info = weigh(availability, noise_precision, sensor_map)
     infos = [info] + [xor_over_x(info, d) for d in (1, 2, 3)]
 
-    partial, done = info_rows(place, masks, plane, received.reshape(NY * NC, NX, NZ // 2, rows, LANES))
-    partial = lax.all_to_all(partial.reshape(NZ, -1, modes), "z", split_axis=0, concat_axis=0, tiled=True)
+    partial, done = info_rows(place, masks, plane, received.reshape(NY * NC, NX, NZ, rows // 2, LANES))
+    partial = lax.all_to_all(partial, "z", split_axis=0, concat_axis=0, tiled=True)
     piece = jnp.sum(partial, 0)
-    pieces = [rows_to_block(piece, d) for d in range(NX)]
+    pieces = [piece] + [xor_over_x(piece, d) for d in (1, 2, 3)]
 
     retain = jnp.exp(-decay_rate)
     powers, total = local(

time: 110 us -> 107 us (0.973)
  waiting for transfers between devices: 21.9 us -> 20.2 us
    ppermute x4 -> x0, starting transfers between devices: 9.15 us -> none  [rows_to_block(): return lax.ppermute(piece, ('z', 'x'), route)]
    ppermute x6 -> x9, starting transfers between devices: 8.6 us -> 15.5 us  [xor_over_x(): return lax.ppermute(block, 'x', [(i, i ^ distance) for i in range(NX)])]
    ppermute x4 -> x0, waiting for transfers between devices: 4.92 us -> none  [rows_to_block(): return lax.ppermute(piece, ('z', 'x'), route)]
    ppermute x6 -> x9, waiting for transfers between devices: 3.34 us -> 6.86 us  [xor_over_x(): return lax.ppermute(block, 'x', [(i, i ^ distance) for i in range(NX)])]
    all_to_all x1, starting transfers between devices: 8.46 us -> 9.94 us  [on_device(): lax.all_to_all(sends, ('z', 'y', 'c'), split_axis=0, concat_axis=0, tiled...]
  transfers between devices with their start and end apart: 24 -> 23, of which waited for: 10 -> 10; matrix products, arithmetic and copies ran while one was open for 1% -> 1% of each run, Pallas kernels for 16% -> 16%
where the time goes in v4:
time: 107 us
  starting transfers between devices  59.4 us (56%)
  Pallas kernels  23.7 us (22%)
  waiting for transfers between devices  20.2 us (19%)
  local copies, waits for them, and re-layouts  2.76 us (3%)
    ppermute x9, starting transfers between devices, xor_over_x(): return lax.ppermute(block, 'x', [(i, i ^ distance) for i in range(NX)])  15.5 us
    pallas_call x9, Pallas kernels, local(): pl.pallas_call(call, name=name, out_shape=outs, in_specs=[SCALARS] * len(...  11.3 us
    all_to_all x1, starting transfers between devices, on_device(): lax.all_to_all(sends, ('z', 'y', 'c'), split_axis=0, concat_axis=0, tiled...  9.94 us
    ppermute x3, starting transfers between devices, on_device(): kept = kept + lax.ppermute(kept, 'z', [(i, i ^ flip) for i in range(NZ)])  9.6 us
    all_to_all x1, starting transfers between devices, on_device(): lax.all_to_all(partial, 'z', split_axis=0, concat_axis=0, tiled=True)  8.19 us
    all_to_all x1, waiting for transfers between devices, on_device(): lax.all_to_all(sends, ('z', 'y', 'c'), split_axis=0, concat_axis=0, tiled...  8.06 us
    ppermute x9, waiting for transfers between devices, xor_over_x(): return lax.ppermute(block, 'x', [(i, i ^ distance) for i in range(NX)])  6.86 us
    all_to_all x1, starting transfers between devices, on_device(): lax.all_to_all(sent, ('y', 'c', 'x'), split_axis=0, concat_axis=0, tiled=...  6.57 us
  transfers between devices with their start and end apart: 23, of which 10 were waited for; matrix products, arithmetic and copies ran while one was open for 1% of the time, Pallas kernels for 16%

profile of v4, /device:TPU:1, one launch (start us, length us, event | category | flops | bytes accessed | tf_op | source)
XLA Modules:
  0.0 107.0 jit_solution(17965450738311725256)
XLA Ops:
  0.0 2.6 %pack.1.own_ref = bf16[144,256]{1,0:T(8,128)(2,1)} custom-call(s32[1,32]{1,0:T(1,128)} %kept_ref.3, bf16[32,128,128]{2,1,0:T(8,128)(2,1)} %noise_ref.3, bf16[4096,128]{1,0:T(8,128)(2,1)} %map_ref.3), custom_call_target="tpu_custom_call" | custom-call | flops 8388608 | bytes 262144 | tf_op jit(solution)/shard_map/pack/pallas_call | solution.py:120
  2.6 2.1 %collective-permute-start.3 = (bf16[144,256]{1,0:T(8,128)(2,1)}, bf16[144,256]{1,0:T(8,128)(2,1)S(1)}, u32[]{:S(2)}, u32[]{:S(2)}) collective-permute-start(bf16[144,256]{1,0:T(8,128)(2,1)} %pack.1.own_ref), channel_id=1, source_target_pairs={{0,1},{1,0},{2,3},{3,2},{4,5},{5,4},{6,7},{7,6},{8,9},{9,8},{10,11... | collective-permute-start | bytes 221192 | tf_op jit(solution)/shard_map/ppermute | solution.py:66
  4.7 2.5 %collective-permute-start.4 = (bf16[144,256]{1,0:T(8,128)(2,1)}, bf16[144,256]{1,0:T(8,128)(2,1)S(1)}, u32[]{:S(2)}, u32[]{:S(2)}) collective-permute-start(bf16[144,256]{1,0:T(8,128)(2,1)} %pack.1.own_ref), channel_id=1, source_target_pairs={{0,2},{1,3},{2,0},{3,1},{4,6},{5,7},{6,4},{7,5},{8,10},{9,11},{10,... | collective-permute-start | bytes 221192 | tf_op jit(solution)/shard_map/ppermute | solution.py:66
  7.2 0.6 by_taker.1
  7.8 1.4 %copy-done = bf16[8,4,8,32,128]{4,3,2,1,0:T(8,128)(2,1)} copy-done((bf16[8,4,8,32,128]{4,3,2,1,0:T(8,128)(2,1)}, bf16[8,4,8,32,128]{4,3,2,1,0:T(8,128)(2,1)S(1)}, u32[]{:S(2)}) %copy-start) | copy-done | bytes 2097176
  9.2 1.1 %collective-permute-done.4.two_ref.refs_1_ = bf16[144,256]{1,0:T(8,128)(2,1)S(1)} collective-permute-done((bf16[144,256]{1,0:T(8,128)(2,1)}, bf16[144,256]{1,0:T(8,128)(2,1)S(1)}, u32[]{:S(2)}, u32[]{:S(2)}) %collective-permute-start.4) | collective-permute-done | bytes 73760 | tf_op jit(solution)/shard_map/ppermute | solution.py:66
  10.3 1.9 %collective-permute-done.5.three_ref.refs_2_ = bf16[144,256]{1,0:T(8,128)(2,1)S(1)} collective-permute-done((bf16[144,256]{1,0:T(8,128)(2,1)}, bf16[144,256]{1,0:T(8,128)(2,1)S(1)}, u32[]{:S(2)}, u32[]{:S(2)}) %collective-permute-start.5) | collective-permute-done | bytes 73760 | tf_op jit(solution)/shard_map/ppermute | solution.py:66
  12.3 0.6 copy-done.9
  12.9 6.6 %all-to-all-start = ((bf16[32,256,128]{2,1,0:T(8,128)(2,1)}), bf16[32,256,128]{2,1,0:T(8,128)(2,1)S(1)}, u32[]{:S(2)}, u32[]{:S(2)}) async-start(bf16[32,256,128]{2,1,0:T(8,128)(2,1)} %once.1), calls=%async_computation | async-start | bytes 4194304 | tf_op jit(solution)/shard_map/all_to_all | solution.py:416
  19.5 0.7 stack.23.place_ref.refs_0_
  20.2 2.5 %gather.1 = (f32[8,128]{1,0:T(8,128)}, bf16[128,1024]{1,0:T(8,128)(2,1)}) custom-call(s32[5]{0:T(128)} %stack.23.place_ref.refs_0_, bf16[144,256]{1,0:T(8,128)(2,1)} %pack.1.own_ref, bf16[144,256]{1,0:T(8,128)(2,1)} %copy-done.7, bf16[144,256]{1,0:T(8,128)(2,1)} %copy-done.8, bf16[144,256]{1,0:T(8,128)(2,1)} %copy-done.9), custom_call_target="tpu_custom_call" | custom-call | bytes 1048576 | tf_op jit(solution)/shard_map/gather/pallas_call | solution.py:152
  22.7 0.3 collective-permute-start.9
  23.1 1.6 %collective-permute-start.6 = (f32[8,128]{1,0:T(8,128)}, f32[8,128]{1,0:T(8,128)S(1)}, u32[]{:S(2)}, u32[]{:S(2)}) collective-permute-start(f32[8,128]{1,0:T(8,128)} %get-tuple-element.33), channel_id=1, source_target_pairs={{0,32},{32,0},{64,96},{96,64},{128,160},{160,128},{192,224},{224,1... | collective-permute-start | bytes 12296 | tf_op jit(solution)/shard_map/ppermute | solution.py:419
  24.7 1.5 %collective-permute-done.6 = f32[8,128]{1,0:T(8,128)S(1)} collective-permute-done((f32[8,128]{1,0:T(8,128)}, f32[8,128]{1,0:T(8,128)S(1)}, u32[]{:S(2)}, u32[]{:S(2)}) %collective-permute-start.6) | collective-permute-done | bytes 4128 | tf_op jit(solution)/shard_map/ppermute | solution.py:419
  26.2 0.7 add.17
  26.9 3.0 %collective-permute-start.7 = (f32[8,128]{1,0:T(8,128)S(1)}, f32[8,128]{1,0:T(8,128)S(1)}, u32[]{:S(2)}, u32[]{:S(2)}) collective-permute-start(f32[8,128]{1,0:T(8,128)S(1)} %add.17), channel_id=1, source_target_pairs={{0,64},{32,96},{64,0},{96,32},{128,192},{160,224},{192,128},{224,1... | collective-permute-start | bytes 12296 | tf_op jit(solution)/shard_map/ppermute | solution.py:419
  29.9 4.1 %weigh.1.refs_0_ = f32[128,128]{1,0:T(8,128)} custom-call(s32[1,32]{1,0:T(1,128)} %kept_ref.3, bf16[32,128,128]{2,1,0:T(8,128)(2,1)} %noise_ref.3, bf16[4096,128]{1,0:T(8,128)(2,1)} %map_ref.3), custom_call_target="tpu_custom_call" | custom-call | flops 268435456 | bytes 2097152 | tf_op jit(solution)/shard_map/weigh/pallas_call | solution.py:191
  33.9 1.5 %collective-permute-start = (f32[128,128]{1,0:T(8,128)}, f32[128,128]{1,0:T(8,128)S(1)}, u32[]{:S(2)}, u32[]{:S(2)}) collective-permute-start(f32[128,128]{1,0:T(8,128)} %weigh.1.refs_0_), channel_id=1, source_target_pairs={{0,1},{1,0},{2,3},{3,2},{4,5},{5,4},{6,7},{7,6},{8,9},{9,8},{10,11... | collective-permute-start | bytes 196616 | tf_op jit(solution)/shard_map/ppermute | solution.py:66
  35.5 2.4 %collective-permute-start.1 = (f32[128,128]{1,0:T(8,128)}, f32[128,128]{1,0:T(8,128)S(1)}, u32[]{:S(2)}, u32[]{:S(2)}) collective-permute-start(f32[128,128]{1,0:T(8,128)} %weigh.1.refs_0_), channel_id=1, source_target_pairs={{0,2},{1,3},{2,0},{3,1},{4,6},{5,7},{6,4},{7,5},{8,10},{9,11},{10,... | collective-permute-start | bytes 196616 | tf_op jit(solution)/shard_map/ppermute | solution.py:66
  37.9 5.0 %collective-permute-start.8 = (f32[8,128]{1,0:T(8,128)S(1)}, f32[8,128]{1,0:T(8,128)S(1)}, u32[]{:S(2)}, u32[]{:S(2)}) collective-permute-start(f32[8,128]{1,0:T(8,128)S(1)} %add.18), channel_id=1, source_target_pairs={{0,128},{32,160},{64,192},{96,224},{128,0},{160,32},{192,64},{224,... | collective-permute-start | bytes 12296 | tf_op jit(solution)/shard_map/ppermute | solution.py:419
  42.9 1.7 %collective-permute-done.8 = f32[8,128]{1,0:T(8,128)S(1)} collective-permute-done((f32[8,128]{1,0:T(8,128)S(1)}, f32[8,128]{1,0:T(8,128)S(1)}, u32[]{:S(2)}, u32[]{:S(2)}) %collective-permute-start.8) | collective-permute-done | bytes 4128 | tf_op jit(solution)/shard_map/ppermute | solution.py:419
  44.6 1.1 %masks.1 = (bf16[256,1024]{1,0:T(8,128)(2,1)S(1)}, f32[8,1024]{1,0:T(8,128)S(1)}) custom-call(s32[5]{0:T(128)S(1)} %copy-done.4, f32[8,128]{1,0:T(8,128)S(1)} %add.19.refs_1_, bf16[128,1024]{1,0:T(8,128)(2,1)S(1)} %copy-done.2, bf16[128,1024]{1,0:T(8,128)(2,1)S(1)} %collective-permute-done.9.refs_3_), custom_call_target="tpu_custom_call" | custom-call | flops 1048576 | bytes 1048576 | tf_op jit(solution)/shard_map/masks/pallas_call | solution.py:33
  45.7 0.6 all-to-all-done
  46.3 2.6 %rows.1 = (f32[8,64,128]{2,1,0:T(8,128)}, f32[8,128]{1,0:T(8,128)S(1)}) custom-call(s32[5]{0:T(128)S(1)} %copy-done.4, f32[8,1024]{1,0:T(8,128)S(1)} %get-tuple-element.35.mask_ref, bf16[256,1024]{1,0:T(8,128)(2,1)S(1)} %get-tuple-element.36.plane_ref, bf16[8,4,8,32,128]{4,3,2,1,0:T(8,128)(2,1)S(1)} %bitcast.14), custom_call_target="tpu_custom_call" | custom-call | flops 268435456 | bytes 3145728 | tf_op jit(solution)/shard_map/rows/pallas_call | solution.py:325
  48.9 8.2 %all-to-all-start.1 = ((f32[8,64,128]{2,1,0:T(8,128)}), f32[8,64,128]{2,1,0:T(8,128)S(1)}, u32[]{:S(2)}, u32[]{:S(2)}) async-start(f32[8,64,128]{2,1,0:T(8,128)} %get-tuple-element.45), calls=%async_computation.1 | async-start | bytes 524288 | tf_op jit(solution)/shard_map/all_to_all | solution.py:429
  57.2 1.8 %powers.1 = (f32[8,128,128]{2,1,0:T(8,128)S(1)}, f32[128,128]{1,0:T(8,128)S(1)}) custom-call(f32[128,128]{1,0:T(8,128)S(1)} %copy-done.3, f32[128,128]{1,0:T(8,128)S(1)} %collective-permute-done.refs_1_, f32[128,128]{1,0:T(8,128)S(1)} %collective-permute-done.1.refs_2_, f32[128,128]{1,0:T(8,128)S(1)} %collective-permute-done.2.refs_3_, ...), custom_call_target="tpu_custom_call" | custom-call | flops 40000000000 | bytes 1048576 | tf_op jit(solution)/shard_map/powers/pallas_call | solution.py:33
  59.0 1.7 %collective-permute-start.10 = (f32[128,128]{1,0:T(8,128)S(1)}, f32[128,128]{1,0:T(8,128)S(1)}, u32[]{:S(2)}, u32[]{:S(2)}) collective-permute-start(f32[128,128]{1,0:T(8,128)S(1)} %get-tuple-element.38.refs_1_), channel_id=1, source_target_pairs={{0,4},{4,0},{1,5},{5,1},{2,6},{6,2},{3,7},{7,3},{8,12},{12,8},{9,1... | collective-permute-start | bytes 196616 | tf_op jit(solution)/shard_map/ppermute | solution.py:449
  60.7 0.9 collective-permute-done.10.refs_2_
  61.6 0.8 pairs.1
  62.4 1.3 %collective-permute-start.11 = (f32[128,128]{1,0:T(8,128)S(1)}, f32[128,128]{1,0:T(8,128)S(1)}, u32[]{:S(2)}, u32[]{:S(2)}) collective-permute-start(f32[128,128]{1,0:T(8,128)S(1)} %get-tuple-element.39.refs_1_), channel_id=1, source_target_pairs={{0,8},{8,0},{16,24},{24,16},{1,9},{9,1},{17,25},{25,17},{2,10},{10... | collective-permute-start | bytes 196616 | tf_op jit(solution)/shard_map/ppermute | solution.py:454
  63.7 1.7 %collective-permute-start.12 = (f32[128,128]{1,0:T(8,128)S(1)}, f32[128,128]{1,0:T(8,128)S(1)}, u32[]{:S(2)}, u32[]{:S(2)}) collective-permute-start(f32[128,128]{1,0:T(8,128)S(1)} %get-tuple-element.39.refs_1_), channel_id=1, source_target_pairs={{0,16},{8,24},{16,0},{24,8},{1,17},{9,25},{17,1},{25,9},{2,18},{10... | collective-permute-start | bytes 196616 | tf_op jit(solution)/shard_map/ppermute | solution.py:454
  65.4 1.0 collective-permute-start.13
  66.3 0.6 all-to-all-done.1
  66.9 3.8 %collective-permute-start.17 = (f32[64,128]{1,0:T(8,128)S(1)}, f32[64,128]{1,0:T(8,128)S(1)}, u32[]{:S(2)}, u32[]{:S(2)}) collective-permute-start(f32[64,128]{1,0:T(8,128)S(1)} %reduce_sum.9.refs_1_), channel_id=1, source_target_pairs={{0,1},{1,0},{2,3},{3,2},{4,5},{5,4},{6,7},{7,6},{8,9},{9,8},{10,11... | collective-permute-start | bytes 98312 | tf_op jit(solution)/shard_map/ppermute | solution.py:66
  70.8 0.6 quads.1
  71.4 1.1 %collective-permute-start.14 = (f32[128,128]{1,0:T(8,128)S(1)}, f32[128,128]{1,0:T(8,128)S(1)}, u32[]{:S(2)}, u32[]{:S(2)}) collective-permute-start(f32[128,128]{1,0:T(8,128)S(1)} %get-tuple-element.42.refs_1_), channel_id=1, source_target_pairs={{0,32},{32,0},{64,96},{96,64},{128,160},{160,128},{192,224},{224,1... | collective-permute-start | bytes 196616 | tf_op jit(solution)/shard_map/ppermute | solution.py:461
  72.5 2.1 %collective-permute-start.15 = (f32[128,128]{1,0:T(8,128)S(1)}, f32[128,128]{1,0:T(8,128)S(1)}, u32[]{:S(2)}, u32[]{:S(2)}) collective-permute-start(f32[128,128]{1,0:T(8,128)S(1)} %get-tuple-element.42.refs_1_), channel_id=1, source_target_pairs={{0,64},{32,96},{64,0},{96,32},{128,192},{160,224},{192,128},{224,1... | collective-permute-start | bytes 196616 | tf_op jit(solution)/shard_map/ppermute | solution.py:461
  74.6 0.4 collective-permute-start.16
  75.0 3.0 %collective-permute-start.18 = (f32[64,128]{1,0:T(8,128)S(1)}, f32[64,128]{1,0:T(8,128)S(1)}, u32[]{:S(2)}, u32[]{:S(2)}) collective-permute-start(f32[64,128]{1,0:T(8,128)S(1)} %reduce_sum.9.refs_1_), channel_id=1, source_target_pairs={{0,2},{1,3},{2,0},{3,1},{4,6},{5,7},{6,4},{7,5},{8,10},{9,11},{10,... | collective-permute-start | bytes 98312 | tf_op jit(solution)/shard_map/ppermute | solution.py:66
  78.1 0.5 factors.1
  78.6 0.8 collective-permute-done.18.refs_3_
  79.4 3.0 %collective-permute-done.19.refs_4_ = f32[64,128]{1,0:T(8,128)S(1)} collective-permute-done((f32[64,128]{1,0:T(8,128)S(1)}, f32[64,128]{1,0:T(8,128)S(1)}, u32[]{:S(2)}, u32[]{:S(2)}) %collective-permute-start.19) | collective-permute-done | bytes 32800 | tf_op jit(solution)/shard_map/ppermute | solution.py:66
  82.3 1.5 %tail.1 = (f32[256,128]{1,0:T(8,128)S(1)}, f32[8,128]{1,0:T(8,128)S(1)}, f32[64,128]{1,0:T(8,128)S(1)}) custom-call(s32[5]{0:T(128)S(1)} %copy-done.4, f32[64,128]{1,0:T(8,128)S(1)} %reduce_sum.9.refs_1_, f32[64,128]{1,0:T(8,128)S(1)} %collective-permute-done.17.refs_2_, f32[64,128]{1,0:T(8,128)S(1)} %collective-permute-done.18.refs_3_, ...), custom_call_target="tpu_custom_call" | custom-call | flops 201326592 | bytes 1048576 | tf_op jit(solution)/shard_map/tail/pallas_call | solution.py:33
  83.8 1.8 %far.1 = (bf16[384,128]{1,0:T(8,128)(2,1)S(1)}, bf16[384,128]{1,0:T(8,128)(2,1)S(1)}, f32[64,128]{1,0:T(8,128)}) custom-call(s32[5]{0:T(128)S(1)} %copy-done.4, f32[128,128]{1,0:T(8,128)S(1)} %get-tuple-element.42.refs_1_, f32[128,128]{1,0:T(8,128)S(1)} %collective-permute-done.14.refs_2_, f32[128,128]{1,0:T(8,128)S(1)} %collective-permute-done.15.refs_3_, ...), custom_call_target="tpu_custom_call" | custom-call | flops 125829120 | bytes 1048576 | tf_op jit(solution)/shard_map/far/pallas_call | solution.py:33
  85.6 9.9 %all-to-all-start.2 = ((f32[64,1,128]{2,1,0:T(1,128)}), f32[64,1,128]{2,1,0:T(1,128)S(1)}, u32[]{:S(2)}, u32[]{:S(2)}) async-start(f32[64,1,128]{2,1,0:T(1,128)} %bitcast.10), calls=%async_computation.2 | async-start | bytes 65536 | tf_op jit(solution)/shard_map/all_to_all | solution.py:474
  95.6 1.2 %sweep.1.refs_3_ = f32[256,128]{1,0:T(8,128)S(1)} custom-call(f32[256,128]{1,0:T(8,128)S(1)} %get-tuple-element.55.refs_0_, bf16[4,384,384]{2,1,0:T(8,128)(2,1)S(1)} %get-tuple-element.48.refs_8_.refs_1_.refs_2_), custom_call_target="tpu_custom_call" | custom-call | flops 402653184 | bytes 1048576 | tf_op jit(solution)/shard_map/sweep/pallas_call | solution.py:33
  96.8 8.1 %all-to-all-done.2 = f32[64,1,128]{2,1,0:T(1,128)S(1)} async-done(((f32[64,1,128]{2,1,0:T(1,128)}), f32[64,1,128]{2,1,0:T(1,128)S(1)}, u32[]{:S(2)}, u32[]{:S(2)}) %all-to-all-start.2) | async-done | bytes 32800 | tf_op jit(solution)/shard_map/all_to_all | solution.py:474
  104.9 2.1 %states.1 = f32[256,128]{1,0:T(8,128)} custom-call(s32[5]{0:T(128)S(1)} %copy-done.4, f32[64,128]{1,0:T(8,128)S(1)} %bitcast.15, bf16[4,384,384]{2,1,0:T(8,128)(2,1)S(1)} %get-tuple-element.48.refs_8_.refs_1_.refs_2_, f32[256,128]{1,0:T(8,128)S(1)} %sweep.1.refs_3_, bf16[384,128]{1,0:T(8,128)(2,1)S(1)} %get-tuple-element.56.refs_4_, ...), custom_call_target="tpu_custom_call" | custom-call | flops 377487360 | bytes 1048576 | tf_op jit(solution)/shard_map/states/pallas_call | solution.py:33
  (40 shorter events, 0.3 us)
Async XLA Ops:
  0.0 7.2 %copy-start.1 = (bf16[64,16384]{1,0:T(8,128)(2,1)S(1)}, bf16[64,16384]{1,0:T(8,128)(2,1)}, u32[]{:S(2)}) copy-start(bf16[64,16384]{1,0:T(8,128)(2,1)} %rows_ref.1) | copy-start | bytes 6291460
  2.6 6.6 %collective-permute-start.3 = (bf16[144,256]{1,0:T(8,128)(2,1)}, bf16[144,256]{1,0:T(8,128)(2,1)S(1)}, u32[]{:S(2)}, u32[]{:S(2)}) collective-permute-start(bf16[144,256]{1,0:T(8,128)(2,1)} %pack.1.own_ref), channel_id=1, source_target_pairs={{0,1},{1,0},{2,3},{3,2},{4,5},{5,4},{6,7},{7,6},{8,9},{9,8},{10,11... | collective-permute-start | bytes 221192 | tf_op jit(solution)/shard_map/ppermute | solution.py:66
  4.7 5.6 %collective-permute-start.4 = (bf16[144,256]{1,0:T(8,128)(2,1)}, bf16[144,256]{1,0:T(8,128)(2,1)S(1)}, u32[]{:S(2)}, u32[]{:S(2)}) collective-permute-start(bf16[144,256]{1,0:T(8,128)(2,1)} %pack.1.own_ref), channel_id=1, source_target_pairs={{0,2},{1,3},{2,0},{3,1},{4,6},{5,7},{6,4},{7,5},{8,10},{9,11},{10,... | collective-permute-start | bytes 221192 | tf_op jit(solution)/shard_map/ppermute | solution.py:66
  7.2 5.1 %collective-permute-start.5 = (bf16[144,256]{1,0:T(8,128)(2,1)}, bf16[144,256]{1,0:T(8,128)(2,1)S(1)}, u32[]{:S(2)}, u32[]{:S(2)}) collective-permute-start(bf16[144,256]{1,0:T(8,128)(2,1)} %pack.1.own_ref), channel_id=1, source_target_pairs={{0,3},{1,2},{2,1},{3,0},{4,7},{5,6},{6,5},{7,4},{8,11},{9,10},{10,... | collective-permute-start | bytes 221192 | tf_op jit(solution)/shard_map/ppermute | solution.py:66
  7.8 1.4 %copy-start = (bf16[8,4,8,32,128]{4,3,2,1,0:T(8,128)(2,1)}, bf16[8,4,8,32,128]{4,3,2,1,0:T(8,128)(2,1)S(1)}, u32[]{:S(2)}) copy-start(bf16[8,4,8,32,128]{4,3,2,1,0:T(8,128)(2,1)S(1)} %by_taker.1) | copy-start | bytes 6291460
  9.2 3.1 %copy-start.7 = (bf16[144,256]{1,0:T(8,128)(2,1)}, bf16[144,256]{1,0:T(8,128)(2,1)S(1)}, u32[]{:S(2)}) copy-start(bf16[144,256]{1,0:T(8,128)(2,1)S(1)} %collective-permute-done.3.one_ref.refs_0_) | copy-start | bytes 221188
  10.3 1.9 %copy-start.8 = (bf16[144,256]{1,0:T(8,128)(2,1)}, bf16[144,256]{1,0:T(8,128)(2,1)S(1)}, u32[]{:S(2)}) copy-start(bf16[144,256]{1,0:T(8,128)(2,1)S(1)} %collective-permute-done.4.two_ref.refs_1_) | copy-start | bytes 221188
  12.3 0.6 copy-start.9
  12.9 33.4 %all-to-all-start = ((bf16[32,256,128]{2,1,0:T(8,128)(2,1)}), bf16[32,256,128]{2,1,0:T(8,128)(2,1)S(1)}, u32[]{:S(2)}, u32[]{:S(2)}) async-start(bf16[32,256,128]{2,1,0:T(8,128)(2,1)} %once.1), calls=%async_computation | async-start | bytes 4194304 | tf_op jit(solution)/shard_map/all_to_all | solution.py:416
  19.5 23.4 %copy-start.5 = (f32[128]{0:T(128)S(1)}, f32[128]{0:T(128)}, u32[]{:S(2)}) copy-start(f32[128]{0:T(128)} %param.10) | copy-start | bytes 1540
  20.2 24.5 %copy-start.4 = (s32[5]{0:T(128)S(1)}, s32[5]{0:T(128)}, u32[]{:S(2)}) copy-start(s32[5]{0:T(128)} %stack.23.place_ref.refs_0_) | copy-start | bytes 64
  22.7 21.9 %copy-start.2 = (bf16[128,1024]{1,0:T(8,128)(2,1)S(1)}, bf16[128,1024]{1,0:T(8,128)(2,1)}, u32[]{:S(2)}) copy-start(bf16[128,1024]{1,0:T(8,128)(2,1)} %get-tuple-element.34.refs_2_) | copy-start | bytes 786436
  22.7 21.9 %collective-permute-start.9 = (bf16[128,1024]{1,0:T(8,128)(2,1)}, bf16[128,1024]{1,0:T(8,128)(2,1)S(1)}, u32[]{:S(2)}, u32[]{:S(2)}) collective-permute-start(bf16[128,1024]{1,0:T(8,128)(2,1)} %get-tuple-element.34.refs_2_), channel_id=1, source_target_pairs={{0,4},{4,0},{1,5},{5,1},{2,6},{6,2},{3,7},{7,3},{8,12},{12,8},{9,1... | collective-permute-start | bytes 786440 | tf_op jit(solution)/shard_map/ppermute | solution.py:421
  23.1 3.1 %collective-permute-start.6 = (f32[8,128]{1,0:T(8,128)}, f32[8,128]{1,0:T(8,128)S(1)}, u32[]{:S(2)}, u32[]{:S(2)}) collective-permute-start(f32[8,128]{1,0:T(8,128)} %get-tuple-element.33), channel_id=1, source_target_pairs={{0,32},{32,0},{64,96},{96,64},{128,160},{160,128},{192,224},{224,1... | collective-permute-start | bytes 12296 | tf_op jit(solution)/shard_map/ppermute | solution.py:419
  26.9 11.1 %collective-permute-start.7 = (f32[8,128]{1,0:T(8,128)S(1)}, f32[8,128]{1,0:T(8,128)S(1)}, u32[]{:S(2)}, u32[]{:S(2)}) collective-permute-start(f32[8,128]{1,0:T(8,128)S(1)} %add.17), channel_id=1, source_target_pairs={{0,64},{32,96},{64,0},{96,32},{128,192},{160,224},{192,128},{224,1... | collective-permute-start | bytes 12296 | tf_op jit(solution)/shard_map/ppermute | solution.py:419
  33.9 23.3 %copy-start.3 = (f32[128,128]{1,0:T(8,128)S(1)}, f32[128,128]{1,0:T(8,128)}, u32[]{:S(2)}) copy-start(f32[128,128]{1,0:T(8,128)} %weigh.1.refs_0_) | copy-start | bytes 196612
  33.9 23.2 %collective-permute-start = (f32[128,128]{1,0:T(8,128)}, f32[128,128]{1,0:T(8,128)S(1)}, u32[]{:S(2)}, u32[]{:S(2)}) collective-permute-start(f32[128,128]{1,0:T(8,128)} %weigh.1.refs_0_), channel_id=1, source_target_pairs={{0,1},{1,0},{2,3},{3,2},{4,5},{5,4},{6,7},{7,6},{8,9},{9,8},{10,11... | collective-permute-start | bytes 196616 | tf_op jit(solution)/shard_map/ppermute | solution.py:66
  35.5 21.7 %collective-permute-start.1 = (f32[128,128]{1,0:T(8,128)}, f32[128,128]{1,0:T(8,128)S(1)}, u32[]{:S(2)}, u32[]{:S(2)}) collective-permute-start(f32[128,128]{1,0:T(8,128)} %weigh.1.refs_0_), channel_id=1, source_target_pairs={{0,2},{1,3},{2,0},{3,1},{4,6},{5,7},{6,4},{7,5},{8,10},{9,11},{10,... | collective-permute-start | bytes 196616 | tf_op jit(solution)/shard_map/ppermute | solution.py:66
  37.8 19.3 %collective-permute-start.2 = (f32[128,128]{1,0:T(8,128)}, f32[128,128]{1,0:T(8,128)S(1)}, u32[]{:S(2)}, u32[]{:S(2)}) collective-permute-start(f32[128,128]{1,0:T(8,128)} %weigh.1.refs_0_), channel_id=1, source_target_pairs={{0,3},{1,2},{2,1},{3,0},{4,7},{5,6},{6,5},{7,4},{8,11},{9,10},{10,... | collective-permute-start | bytes 196616 | tf_op jit(solution)/shard_map/ppermute | solution.py:66
  37.9 6.7 %collective-permute-start.8 = (f32[8,128]{1,0:T(8,128)S(1)}, f32[8,128]{1,0:T(8,128)S(1)}, u32[]{:S(2)}, u32[]{:S(2)}) collective-permute-start(f32[8,128]{1,0:T(8,128)S(1)} %add.18), channel_id=1, source_target_pairs={{0,128},{32,160},{64,192},{96,224},{128,0},{160,32},{192,64},{224,... | collective-permute-start | bytes 12296 | tf_op jit(solution)/shard_map/ppermute | solution.py:419
  48.9 18.0 %all-to-all-start.1 = ((f32[8,64,128]{2,1,0:T(8,128)}), f32[8,64,128]{2,1,0:T(8,128)S(1)}, u32[]{:S(2)}, u32[]{:S(2)}) async-start(f32[8,64,128]{2,1,0:T(8,128)} %get-tuple-element.45), calls=%async_computation.1 | async-start | bytes 524288 | tf_op jit(solution)/shard_map/all_to_all | solution.py:429
  57.2 25.1 %copy-start.6 = (f32[128]{0:T(128)S(1)}, f32[128]{0:T(128)}, u32[]{:S(2)}) copy-start(f32[128]{0:T(128)} %param.11) | copy-start | bytes 1540
  59.0 2.6 %collective-permute-start.10 = (f32[128,128]{1,0:T(8,128)S(1)}, f32[128,128]{1,0:T(8,128)S(1)}, u32[]{:S(2)}, u32[]{:S(2)}) collective-permute-start(f32[128,128]{1,0:T(8,128)S(1)} %get-tuple-element.38.refs_1_), channel_id=1, source_target_pairs={{0,4},{4,0},{1,5},{5,1},{2,6},{6,2},{3,7},{7,3},{8,12},{12,8},{9,1... | collective-permute-start | bytes 196616 | tf_op jit(solution)/shard_map/ppermute | solution.py:449
  62.4 8.4 %collective-permute-start.11 = (f32[128,128]{1,0:T(8,128)S(1)}, f32[128,128]{1,0:T(8,128)S(1)}, u32[]{:S(2)}, u32[]{:S(2)}) collective-permute-start(f32[128,128]{1,0:T(8,128)S(1)} %get-tuple-element.39.refs_1_), channel_id=1, source_target_pairs={{0,8},{8,0},{16,24},{24,16},{1,9},{9,1},{17,25},{25,17},{2,10},{10... | collective-permute-start | bytes 196616 | tf_op jit(solution)/shard_map/ppermute | solution.py:454
  63.7 7.1 %collective-permute-start.12 = (f32[128,128]{1,0:T(8,128)S(1)}, f32[128,128]{1,0:T(8,128)S(1)}, u32[]{:S(2)}, u32[]{:S(2)}) collective-permute-start(f32[128,128]{1,0:T(8,128)S(1)} %get-tuple-element.39.refs_1_), channel_id=1, source_target_pairs={{0,16},{8,24},{16,0},{24,8},{1,17},{9,25},{17,1},{25,9},{2,18},{10... | collective-permute-start | bytes 196616 | tf_op jit(solution)/shard_map/ppermute | solution.py:454
  65.4 5.4 %collective-permute-start.13 = (f32[128,128]{1,0:T(8,128)S(1)}, f32[128,128]{1,0:T(8,128)S(1)}, u32[]{:S(2)}, u32[]{:S(2)}) collective-permute-start(f32[128,128]{1,0:T(8,128)S(1)} %get-tuple-element.39.refs_1_), channel_id=1, source_target_pairs={{0,24},{8,16},{16,8},{24,0},{1,25},{9,17},{17,9},{25,1},{2,26},{10... | collective-permute-start | bytes 196616 | tf_op jit(solution)/shard_map/ppermute | solution.py:454
  66.9 11.1 %collective-permute-start.17 = (f32[64,128]{1,0:T(8,128)S(1)}, f32[64,128]{1,0:T(8,128)S(1)}, u32[]{:S(2)}, u32[]{:S(2)}) collective-permute-start(f32[64,128]{1,0:T(8,128)S(1)} %reduce_sum.9.refs_1_), channel_id=1, source_target_pairs={{0,1},{1,0},{2,3},{3,2},{4,5},{5,4},{6,7},{7,6},{8,9},{9,8},{10,11... | collective-permute-start | bytes 98312 | tf_op jit(solution)/shard_map/ppermute | solution.py:66
  71.4 12.4 %collective-permute-start.14 = (f32[128,128]{1,0:T(8,128)S(1)}, f32[128,128]{1,0:T(8,128)S(1)}, u32[]{:S(2)}, u32[]{:S(2)}) collective-permute-start(f32[128,128]{1,0:T(8,128)S(1)} %get-tuple-element.42.refs_1_), channel_id=1, source_target_pairs={{0,32},{32,0},{64,96},{96,64},{128,160},{160,128},{192,224},{224,1... | collective-permute-start | bytes 196616 | tf_op jit(solution)/shard_map/ppermute | solution.py:461
  72.5 11.3 %collective-permute-start.15 = (f32[128,128]{1,0:T(8,128)S(1)}, f32[128,128]{1,0:T(8,128)S(1)}, u32[]{:S(2)}, u32[]{:S(2)}) collective-permute-start(f32[128,128]{1,0:T(8,128)S(1)} %get-tuple-element.42.refs_1_), channel_id=1, source_target_pairs={{0,64},{32,96},{64,0},{96,32},{128,192},{160,224},{192,128},{224,1... | collective-permute-start | bytes 196616 | tf_op jit(solution)/shard_map/ppermute | solution.py:461
  74.6 9.2 %collective-permute-start.16 = (f32[128,128]{1,0:T(8,128)S(1)}, f32[128,128]{1,0:T(8,128)S(1)}, u32[]{:S(2)}, u32[]{:S(2)}) collective-permute-start(f32[128,128]{1,0:T(8,128)S(1)} %get-tuple-element.42.refs_1_), channel_id=1, source_target_pairs={{0,96},{32,64},{64,32},{96,0},{128,224},{160,192},{192,160},{224,1... | collective-permute-start | bytes 196616 | tf_op jit(solution)/shard_map/ppermute | solution.py:461
  75.0 4.3 %collective-permute-start.18 = (f32[64,128]{1,0:T(8,128)S(1)}, f32[64,128]{1,0:T(8,128)S(1)}, u32[]{:S(2)}, u32[]{:S(2)}) collective-permute-start(f32[64,128]{1,0:T(8,128)S(1)} %reduce_sum.9.refs_1_), channel_id=1, source_target_pairs={{0,2},{1,3},{2,0},{3,1},{4,6},{5,7},{6,4},{7,5},{8,10},{9,11},{10,... | collective-permute-start | bytes 98312 | tf_op jit(solution)/shard_map/ppermute | solution.py:66
  78.1 4.3 %collective-permute-start.19 = (f32[64,128]{1,0:T(8,128)S(1)}, f32[64,128]{1,0:T(8,128)S(1)}, u32[]{:S(2)}, u32[]{:S(2)}) collective-permute-start(f32[64,128]{1,0:T(8,128)S(1)} %reduce_sum.9.refs_1_), channel_id=1, source_target_pairs={{0,3},{1,2},{2,1},{3,0},{4,7},{5,6},{6,5},{7,4},{8,11},{9,10},{10,... | collective-permute-start | bytes 98312 | tf_op jit(solution)/shard_map/ppermute | solution.py:66
  85.6 19.2 %all-to-all-start.2 = ((f32[64,1,128]{2,1,0:T(1,128)}), f32[64,1,128]{2,1,0:T(1,128)S(1)}, u32[]{:S(2)}, u32[]{:S(2)}) async-start(f32[64,1,128]{2,1,0:T(1,128)} %bitcast.10), calls=%async_computation.2 | async-start | bytes 65536 | tf_op jit(solution)/shard_map/all_to_all | solution.py:474

commit v5 on v4

--- a/solution.py
+++ b/solution.py
@@ -215,7 +215,8 @@
     block_ref[...] = power
 
 
-def factor_kernel(power_ref, add_ref, spread_ref):
+def factor_kernel(power_ref, add_ref, spread_ref, token_ref):
+    token_ref[...] = jnp.zeros((8, LANES), jnp.float32)
     for step in range(LEVELS // 2):
         one, two = power_ref[2 * step], power_ref[2 * step + 1]
         for j, power in enumerate((one, two, dot(one, two))):
@@ -240,7 +241,8 @@
     )(array, *tokens)
 
 
-def factor_kernel(power_ref, add_ref, spread_ref):
+def factor_kernel(power_ref, add_ref, spread_ref, token_ref):
+    token_ref[...] = jnp.zeros((8, LANES), jnp.float32)
     for step in range(LEVELS // 2):
         one, two = power_ref[2 * step], power_ref[2 * step + 1]
         for j, power in enumerate((one, two, dot(one, two))):
@@ -358,16 +360,18 @@
     return sends
 
 
-def far_kernel(place_ref, total_ref, one_ref, two_ref, three_ref, lead_ref, rest_ref, tail_ref, near_ref, four_ref, five_ref, send_ref):
+def far_kernel(place_ref, one_ref, two_ref, three_ref, lead_ref, rest_ref, tail_ref, near_ref, four_ref, five_ref, send_ref):
     odd, upper = place_ref[2] % 2 == 1, place_ref[2] % 4 >= 2
-    two, three = two_ref[...], three_ref[...]
-    total, lead, rest = joined(odd, total_ref[...], one_ref[...], lead_ref[...], rest_ref[...])
+    one, two, three = one_ref[...], two_ref[...], three_ref[...]
+    lead, rest = lead_ref[...], rest_ref[...]
+    beside = times(wide(jnp.where(odd, three, two)), tall(jnp.where(odd, two, three)))
+    new = times(wide(jnp.where(odd, one, rest)), tall(jnp.where(odd, lead, one)))
+    lead, rest = jnp.where(odd, new, lead), jnp.where(odd, rest, new)
     four_ref[...] = tall(lead)
     factors = [tall(rest)]
-    beside = dot(jnp.where(odd, three, two), jnp.where(odd, two, three))
-    total, lead, rest = joined(upper, total, beside, lead, rest)
-    five_ref[...] = tall(lead)
-    factors.append(tall(rest))
+    new = times(wide(jnp.where(upper, beside, rest)), tall(jnp.where(upper, lead, beside)))
+    five_ref[...] = tall(jnp.where(upper, new, lead))
+    factors.append(tall(jnp.where(upper, rest, new)))
     send_ref[...] = onward(place_ref[1], tail_ref[:1], near_ref[...], 4, factors)
 
 
@@ -380,6 +384,13 @@
             before = jnp.where(row >= shift, pltpu.roll(swept, shift, 0), 0.0)
             swept += times(wide(before), spread_ref[step, :, side * LANES : (side + 1) * LANES])
     out_ref[...] = swept
+
+
+def step_kernel(power_ref, *refs):
+    step = power_ref[...]
+    for lead_ref, out_ref in zip(refs[: SCAN - 1], refs[SCAN - 1 :]):
+        lead = lead_ref[:LANES].astype(jnp.float32) + lead_ref[2 * LANES :].astype(jnp.float32)
+        out_ref[...] = tall(dot(lead, step))
 
 
 def state_kernel(place_ref, offsets_ref, spread_ref, swept_ref, *refs):
@@ -392,10 +403,9 @@
     for level in range(SCAN):
         chosen = (apart >= 2**level) & (apart < 2 ** (level + 1))
         parts.append(jnp.sum(jnp.where(chosen, offsets, 0.0), 0, keepdims=True))
-    entry = parts[0]
+    grown = times(wide(parts[0]), spread_ref[0, :, :LANES])
     for level in range(1, SCAN):
-        entry += times(wide(parts[level]), lead_refs[level - 1][...])
-    grown = times(wide(entry), spread_ref[0, :, :LANES])
+        grown += times(wide(parts[level]), lead_refs[level - 1][...])
     for step in range(LEVELS // 2):
         more = times(wide(grown), spread_ref[step])
         grown = jnp.concatenate([grown] + [more[:, j * LANES : (j + 1) * LANES] for j in range(3)], 0)
@@ -437,11 +447,12 @@
         [f32(LEVELS, modes, modes), square], 4 * 10**10, tokens=[done],
     )
     steps = LEVELS // 2
-    adding, spreading = local(
+    adding, spreading, ready = local(
         factor_kernel, "factors", [], [powers],
         [
             jax.ShapeDtypeStruct((steps, 9 * modes, modes), jnp.bfloat16),
             jax.ShapeDtypeStruct((steps, 3 * modes, 3 * modes), jnp.bfloat16),
+            f32(8, modes),
         ],
         4 * 6 * 2 * modes**3,
     )
@@ -454,7 +465,7 @@
     got = [lax.ppermute(total, "y", [(i, i ^ d) for i in range(NY)]) for d in (1, 2, 3)]
     total, lead, rest, *quad_terms = local(
         quad_kernel, "quads", [y.astype(jnp.int32)[None]], [total] + got + [lead, rest],
-        [square] * 3 + [terms] * 4, 5 * 6 * 2 * modes**3,
+        [square] * 3 + [terms] * 4, 5 * 6 * 2 * modes**3, tokens=[ready],
     )
     leads += quad_terms[::2]
     rests += quad_terms[1::2]
@@ -466,7 +477,7 @@
         [f32(STEPS, modes), f32(8, modes), f32(NK, modes)], 8 * 6 * 2 * modes**3,
     )
     *far_terms, sends = local(
-        far_kernel, "far", [place], [total] + got + [lead, rest, tail, near],
+        far_kernel, "far", [place], got + [lead, rest, tail, near],
         [terms] * 2 + [f32(NK, modes)], 5 * 6 * 2 * modes**3,
     )
     leads += far_terms
@@ -475,6 +486,9 @@
     (swept,) = local(
         sweep_kernel, "sweep", [], [drive, spreading], [f32(STEPS, modes)], 8 * 12 * 2 * modes**3
     )
+    leads = list(local(
+        step_kernel, "steps", [], [powers[0]] + leads, [terms] * (SCAN - 1), 5 * 6 * 2 * modes**3, tokens=[swept]
+    ))
     (states,) = local(
         state_kernel, "states", [place], [offsets, spreading, swept] + leads,
         [f32(STEPS, modes)], 15 * 6 * 2 * modes**3,

time: 107 us -> 107 us (level)
    pallas_call x9 -> x10, Pallas kernels: 11.3 us -> 11.5 us  [local(): pl.pallas_call(call, name=name, out_shape=outs, in_specs=[SCALARS] * len(...]
  transfers between devices with their start and end apart: 23 -> 23, of which waited for: 10 -> 10; matrix products, arithmetic and copies ran while one was open for 1% -> 1% of each run, Pallas kernels for 16% -> 17%
where the time goes in v5:
time: 107 us
  starting transfers between devices  59.2 us (55%)
  Pallas kernels  23.9 us (22%)
  waiting for transfers between devices  20 us (19%)
  local copies, waits for them, and re-layouts  2.72 us (3%)
    ppermute x9, starting transfers between devices, xor_over_x(): return lax.ppermute(block, 'x', [(i, i ^ distance) for i in range(NX)])  15.5 us
    pallas_call x10, Pallas kernels, local(): pl.pallas_call(call, name=name, out_shape=outs, in_specs=[SCALARS] * len(...  11.5 us
    all_to_all x1, starting transfers between devices, on_device(): lax.all_to_all(sends, ('z', 'y', 'c'), split_axis=0, concat_axis=0, tiled...  9.73 us
    ppermute x3, starting transfers between devices, on_device(): kept = kept + lax.ppermute(kept, 'z', [(i, i ^ flip) for i in range(NZ)])  9.58 us
    all_to_all x1, starting transfers between devices, on_device(): lax.all_to_all(partial, 'z', split_axis=0, concat_axis=0, tiled=True)  8.19 us
    all_to_all x1, waiting for transfers between devices, on_device(): lax.all_to_all(sends, ('z', 'y', 'c'), split_axis=0, concat_axis=0, tiled...  7.62 us
    ppermute x9, waiting for transfers between devices, xor_over_x(): return lax.ppermute(block, 'x', [(i, i ^ distance) for i in range(NX)])  7.06 us
    all_to_all x1, starting transfers between devices, on_device(): lax.all_to_all(sent, ('y', 'c', 'x'), split_axis=0, concat_axis=0, tiled=...  6.57 us
  transfers between devices with their start and end apart: 23, of which 10 were waited for; matrix products, arithmetic and copies ran while one was open for 1% of the time, Pallas kernels for 17%

profile of v5, /device:TPU:1, one launch (start us, length us, event | category | flops | bytes accessed | tf_op | source)
XLA Modules:
  0.0 106.7 jit_solution(5071520527030100520)
XLA Ops:
  0.0 2.6 %pack.1.own_ref = bf16[144,256]{1,0:T(8,128)(2,1)} custom-call(s32[1,32]{1,0:T(1,128)} %kept_ref.3, bf16[32,128,128]{2,1,0:T(8,128)(2,1)} %noise_ref.3, bf16[4096,128]{1,0:T(8,128)(2,1)} %map_ref.3), custom_call_target="tpu_custom_call" | custom-call | flops 8388608 | bytes 262144 | tf_op jit(solution)/shard_map/pack/pallas_call | solution.py:120
  2.6 2.1 %collective-permute-start.3 = (bf16[144,256]{1,0:T(8,128)(2,1)}, bf16[144,256]{1,0:T(8,128)(2,1)S(1)}, u32[]{:S(2)}, u32[]{:S(2)}) collective-permute-start(bf16[144,256]{1,0:T(8,128)(2,1)} %pack.1.own_ref), channel_id=1, source_target_pairs={{0,1},{1,0},{2,3},{3,2},{4,5},{5,4},{6,7},{7,6},{8,9},{9,8},{10,11... | collective-permute-start | bytes 221192 | tf_op jit(solution)/shard_map/ppermute | solution.py:66
  4.7 2.5 %collective-permute-start.4 = (bf16[144,256]{1,0:T(8,128)(2,1)}, bf16[144,256]{1,0:T(8,128)(2,1)S(1)}, u32[]{:S(2)}, u32[]{:S(2)}) collective-permute-start(bf16[144,256]{1,0:T(8,128)(2,1)} %pack.1.own_ref), channel_id=1, source_target_pairs={{0,2},{1,3},{2,0},{3,1},{4,6},{5,7},{6,4},{7,5},{8,10},{9,11},{10,... | collective-permute-start | bytes 221192 | tf_op jit(solution)/shard_map/ppermute | solution.py:66
  7.2 0.6 by_taker.1
  7.8 1.4 %copy-done = bf16[8,4,8,32,128]{4,3,2,1,0:T(8,128)(2,1)} copy-done((bf16[8,4,8,32,128]{4,3,2,1,0:T(8,128)(2,1)}, bf16[8,4,8,32,128]{4,3,2,1,0:T(8,128)(2,1)S(1)}, u32[]{:S(2)}) %copy-start) | copy-done | bytes 2097176
  9.2 1.1 %collective-permute-done.4.two_ref.refs_1_ = bf16[144,256]{1,0:T(8,128)(2,1)S(1)} collective-permute-done((bf16[144,256]{1,0:T(8,128)(2,1)}, bf16[144,256]{1,0:T(8,128)(2,1)S(1)}, u32[]{:S(2)}, u32[]{:S(2)}) %collective-permute-start.4) | collective-permute-done | bytes 73760 | tf_op jit(solution)/shard_map/ppermute | solution.py:66
  10.3 1.9 %collective-permute-done.5.three_ref.refs_2_ = bf16[144,256]{1,0:T(8,128)(2,1)S(1)} collective-permute-done((bf16[144,256]{1,0:T(8,128)(2,1)}, bf16[144,256]{1,0:T(8,128)(2,1)S(1)}, u32[]{:S(2)}, u32[]{:S(2)}) %collective-permute-start.5) | collective-permute-done | bytes 73760 | tf_op jit(solution)/shard_map/ppermute | solution.py:66
  12.3 0.6 copy-done.9
  12.9 6.6 %all-to-all-start = ((bf16[32,256,128]{2,1,0:T(8,128)(2,1)}), bf16[32,256,128]{2,1,0:T(8,128)(2,1)S(1)}, u32[]{:S(2)}, u32[]{:S(2)}) async-start(bf16[32,256,128]{2,1,0:T(8,128)(2,1)} %once.1), calls=%async_computation | async-start | bytes 4194304 | tf_op jit(solution)/shard_map/all_to_all | solution.py:426
  19.5 0.6 stack.23.place_ref.refs_0_
  20.1 2.6 %gather.1 = (f32[8,128]{1,0:T(8,128)}, bf16[128,1024]{1,0:T(8,128)(2,1)}) custom-call(s32[5]{0:T(128)} %stack.23.place_ref.refs_0_, bf16[144,256]{1,0:T(8,128)(2,1)} %pack.1.own_ref, bf16[144,256]{1,0:T(8,128)(2,1)} %copy-done.7, bf16[144,256]{1,0:T(8,128)(2,1)} %copy-done.8, bf16[144,256]{1,0:T(8,128)(2,1)} %copy-done.9), custom_call_target="tpu_custom_call" | custom-call | bytes 1048576 | tf_op jit(solution)/shard_map/gather/pallas_call | solution.py:152
  23.0 1.6 %collective-permute-start.6 = (f32[8,128]{1,0:T(8,128)}, f32[8,128]{1,0:T(8,128)S(1)}, u32[]{:S(2)}, u32[]{:S(2)}) collective-permute-start(f32[8,128]{1,0:T(8,128)} %get-tuple-element.39), channel_id=1, source_target_pairs={{0,32},{32,0},{64,96},{96,64},{128,160},{160,128},{192,224},{224,1... | collective-permute-start | bytes 12296 | tf_op jit(solution)/shard_map/ppermute | solution.py:429
  24.7 1.5 %collective-permute-done.6 = f32[8,128]{1,0:T(8,128)S(1)} collective-permute-done((f32[8,128]{1,0:T(8,128)}, f32[8,128]{1,0:T(8,128)S(1)}, u32[]{:S(2)}, u32[]{:S(2)}) %collective-permute-start.6) | collective-permute-done | bytes 4128 | tf_op jit(solution)/shard_map/ppermute | solution.py:429
  26.2 0.7 add.17
  26.8 3.0 %collective-permute-start.7 = (f32[8,128]{1,0:T(8,128)S(1)}, f32[8,128]{1,0:T(8,128)S(1)}, u32[]{:S(2)}, u32[]{:S(2)}) collective-permute-start(f32[8,128]{1,0:T(8,128)S(1)} %add.17), channel_id=1, source_target_pairs={{0,64},{32,96},{64,0},{96,32},{128,192},{160,224},{192,128},{224,1... | collective-permute-start | bytes 12296 | tf_op jit(solution)/shard_map/ppermute | solution.py:429
  29.8 4.1 %weigh.1.refs_0_ = f32[128,128]{1,0:T(8,128)} custom-call(s32[1,32]{1,0:T(1,128)} %kept_ref.3, bf16[32,128,128]{2,1,0:T(8,128)(2,1)} %noise_ref.3, bf16[4096,128]{1,0:T(8,128)(2,1)} %map_ref.3), custom_call_target="tpu_custom_call" | custom-call | flops 268435456 | bytes 2097152 | tf_op jit(solution)/shard_map/weigh/pallas_call | solution.py:191
  33.9 1.5 %collective-permute-start = (f32[128,128]{1,0:T(8,128)}, f32[128,128]{1,0:T(8,128)S(1)}, u32[]{:S(2)}, u32[]{:S(2)}) collective-permute-start(f32[128,128]{1,0:T(8,128)} %weigh.1.refs_0_), channel_id=1, source_target_pairs={{0,1},{1,0},{2,3},{3,2},{4,5},{5,4},{6,7},{7,6},{8,9},{9,8},{10,11... | collective-permute-start | bytes 196616 | tf_op jit(solution)/shard_map/ppermute | solution.py:66
  35.4 2.4 %collective-permute-start.1 = (f32[128,128]{1,0:T(8,128)}, f32[128,128]{1,0:T(8,128)S(1)}, u32[]{:S(2)}, u32[]{:S(2)}) collective-permute-start(f32[128,128]{1,0:T(8,128)} %weigh.1.refs_0_), channel_id=1, source_target_pairs={{0,2},{1,3},{2,0},{3,1},{4,6},{5,7},{6,4},{7,5},{8,10},{9,11},{10,... | collective-permute-start | bytes 196616 | tf_op jit(solution)/shard_map/ppermute | solution.py:66
  37.9 5.0 %collective-permute-start.8 = (f32[8,128]{1,0:T(8,128)S(1)}, f32[8,128]{1,0:T(8,128)S(1)}, u32[]{:S(2)}, u32[]{:S(2)}) collective-permute-start(f32[8,128]{1,0:T(8,128)S(1)} %add.18), channel_id=1, source_target_pairs={{0,128},{32,160},{64,192},{96,224},{128,0},{160,32},{192,64},{224,... | collective-permute-start | bytes 12296 | tf_op jit(solution)/shard_map/ppermute | solution.py:429
  42.9 1.7 %collective-permute-done.8 = f32[8,128]{1,0:T(8,128)S(1)} collective-permute-done((f32[8,128]{1,0:T(8,128)S(1)}, f32[8,128]{1,0:T(8,128)S(1)}, u32[]{:S(2)}, u32[]{:S(2)}) %collective-permute-start.8) | collective-permute-done | bytes 4128 | tf_op jit(solution)/shard_map/ppermute | solution.py:429
  44.6 1.1 %masks.1 = (bf16[256,1024]{1,0:T(8,128)(2,1)S(1)}, f32[8,1024]{1,0:T(8,128)S(1)}) custom-call(s32[5]{0:T(128)S(1)} %copy-done.4, f32[8,128]{1,0:T(8,128)S(1)} %add.19.refs_1_, bf16[128,1024]{1,0:T(8,128)(2,1)S(1)} %copy-done.2, bf16[128,1024]{1,0:T(8,128)(2,1)S(1)} %collective-permute-done.9.refs_3_), custom_call_target="tpu_custom_call" | custom-call | flops 1048576 | bytes 1048576 | tf_op jit(solution)/shard_map/masks/pallas_call | solution.py:33
  45.7 0.6 all-to-all-done
  46.3 2.6 %rows.1 = (f32[8,64,128]{2,1,0:T(8,128)}, f32[8,128]{1,0:T(8,128)S(1)}) custom-call(s32[5]{0:T(128)S(1)} %copy-done.4, f32[8,1024]{1,0:T(8,128)S(1)} %get-tuple-element.41.mask_ref, bf16[256,1024]{1,0:T(8,128)(2,1)S(1)} %get-tuple-element.42.plane_ref, bf16[8,4,8,32,128]{4,3,2,1,0:T(8,128)(2,1)S(1)} %bitcast.16), custom_call_target="tpu_custom_call" | custom-call | flops 268435456 | bytes 3145728 | tf_op jit(solution)/shard_map/rows/pallas_call | solution.py:327
  48.9 8.2 %all-to-all-start.1 = ((f32[8,64,128]{2,1,0:T(8,128)}), f32[8,64,128]{2,1,0:T(8,128)S(1)}, u32[]{:S(2)}, u32[]{:S(2)}) async-start(f32[8,64,128]{2,1,0:T(8,128)} %get-tuple-element.53), calls=%async_computation.1 | async-start | bytes 524288 | tf_op jit(solution)/shard_map/all_to_all | solution.py:439
  57.2 1.8 %powers.1 = (f32[8,128,128]{2,1,0:T(8,128)S(1)}, f32[128,128]{1,0:T(8,128)S(1)}) custom-call(f32[128,128]{1,0:T(8,128)S(1)} %copy-done.3, f32[128,128]{1,0:T(8,128)S(1)} %collective-permute-done.refs_1_, f32[128,128]{1,0:T(8,128)S(1)} %collective-permute-done.1.refs_2_, f32[128,128]{1,0:T(8,128)S(1)} %collective-permute-done.2.refs_3_, ...), custom_call_target="tpu_custom_call" | custom-call | flops 40000000000 | bytes 1048576 | tf_op jit(solution)/shard_map/powers/pallas_call | solution.py:33
  59.0 1.7 %collective-permute-start.10 = (f32[128,128]{1,0:T(8,128)S(1)}, f32[128,128]{1,0:T(8,128)S(1)}, u32[]{:S(2)}, u32[]{:S(2)}) collective-permute-start(f32[128,128]{1,0:T(8,128)S(1)} %get-tuple-element.44.refs_1_), channel_id=1, source_target_pairs={{0,4},{4,0},{1,5},{5,1},{2,6},{6,2},{3,7},{7,3},{8,12},{12,8},{9,1... | collective-permute-start | bytes 196616 | tf_op jit(solution)/shard_map/ppermute | solution.py:460
  60.7 0.9 collective-permute-done.10.refs_2_
  61.6 0.8 pairs.1
  62.4 1.3 %collective-permute-start.11 = (f32[128,128]{1,0:T(8,128)S(1)}, f32[128,128]{1,0:T(8,128)S(1)}, u32[]{:S(2)}, u32[]{:S(2)}) collective-permute-start(f32[128,128]{1,0:T(8,128)S(1)} %get-tuple-element.45.refs_1_), channel_id=1, source_target_pairs={{0,8},{8,0},{16,24},{24,16},{1,9},{9,1},{17,25},{25,17},{2,10},{10... | collective-permute-start | bytes 196616 | tf_op jit(solution)/shard_map/ppermute | solution.py:465
  63.7 1.7 %collective-permute-start.12 = (f32[128,128]{1,0:T(8,128)S(1)}, f32[128,128]{1,0:T(8,128)S(1)}, u32[]{:S(2)}, u32[]{:S(2)}) collective-permute-start(f32[128,128]{1,0:T(8,128)S(1)} %get-tuple-element.45.refs_1_), channel_id=1, source_target_pairs={{0,16},{8,24},{16,0},{24,8},{1,17},{9,25},{17,1},{25,9},{2,18},{10... | collective-permute-start | bytes 196616 | tf_op jit(solution)/shard_map/ppermute | solution.py:465
  65.3 1.0 collective-permute-start.13
  66.3 0.6 all-to-all-done.1
  66.9 3.8 %collective-permute-start.17 = (f32[64,128]{1,0:T(8,128)S(1)}, f32[64,128]{1,0:T(8,128)S(1)}, u32[]{:S(2)}, u32[]{:S(2)}) collective-permute-start(f32[64,128]{1,0:T(8,128)S(1)} %reduce_sum.9.refs_1_), channel_id=1, source_target_pairs={{0,1},{1,0},{2,3},{3,2},{4,5},{5,4},{6,7},{7,6},{8,9},{9,8},{10,11... | collective-permute-start | bytes 98312 | tf_op jit(solution)/shard_map/ppermute | solution.py:66
  70.7 0.5 factors.1
  71.3 0.6 quads.1
  71.9 0.6 collective-permute-start.14
  72.5 2.1 %collective-permute-start.15 = (f32[128,128]{1,0:T(8,128)S(1)}, f32[128,128]{1,0:T(8,128)S(1)}, u32[]{:S(2)}, u32[]{:S(2)}) collective-permute-start(f32[128,128]{1,0:T(8,128)S(1)} %get-tuple-element.50), channel_id=1, source_target_pairs={{0,64},{32,96},{64,0},{96,32},{128,192},{160,224},{192,128},{224,1... | collective-permute-start | bytes 196616 | tf_op jit(solution)/shard_map/ppermute | solution.py:472
  74.6 0.9 collective-permute-start.16
  75.5 3.0 %collective-permute-start.18 = (f32[64,128]{1,0:T(8,128)S(1)}, f32[64,128]{1,0:T(8,128)S(1)}, u32[]{:S(2)}, u32[]{:S(2)}) collective-permute-start(f32[64,128]{1,0:T(8,128)S(1)} %reduce_sum.9.refs_1_), channel_id=1, source_target_pairs={{0,2},{1,3},{2,0},{3,1},{4,6},{5,7},{6,4},{7,5},{8,10},{9,11},{10,... | collective-permute-start | bytes 98312 | tf_op jit(solution)/shard_map/ppermute | solution.py:66
  78.6 1.3 %collective-permute-done.18.refs_3_ = f32[64,128]{1,0:T(8,128)S(1)} collective-permute-done((f32[64,128]{1,0:T(8,128)S(1)}, f32[64,128]{1,0:T(8,128)S(1)}, u32[]{:S(2)}, u32[]{:S(2)}) %collective-permute-start.18) | collective-permute-done | bytes 32800 | tf_op jit(solution)/shard_map/ppermute | solution.py:66
  79.9 2.7 %collective-permute-done.19.refs_4_ = f32[64,128]{1,0:T(8,128)S(1)} collective-permute-done((f32[64,128]{1,0:T(8,128)S(1)}, f32[64,128]{1,0:T(8,128)S(1)}, u32[]{:S(2)}, u32[]{:S(2)}) %collective-permute-start.19) | collective-permute-done | bytes 32800 | tf_op jit(solution)/shard_map/ppermute | solution.py:66
  82.5 1.5 %tail.1 = (f32[256,128]{1,0:T(8,128)S(1)}, f32[8,128]{1,0:T(8,128)S(1)}, f32[64,128]{1,0:T(8,128)S(1)}) custom-call(s32[5]{0:T(128)S(1)} %copy-done.4, f32[64,128]{1,0:T(8,128)S(1)} %reduce_sum.9.refs_1_, f32[64,128]{1,0:T(8,128)S(1)} %collective-permute-done.17.refs_2_, f32[64,128]{1,0:T(8,128)S(1)} %collective-permute-done.18.refs_3_, ...), custom_call_target="tpu_custom_call" | custom-call | flops 201326592 | bytes 1048576 | tf_op jit(solution)/shard_map/tail/pallas_call | solution.py:33
  84.0 1.7 %far.1 = (bf16[384,128]{1,0:T(8,128)(2,1)S(1)}, bf16[384,128]{1,0:T(8,128)(2,1)S(1)}, f32[64,128]{1,0:T(8,128)}) custom-call(s32[5]{0:T(128)S(1)} %copy-done.4, f32[128,128]{1,0:T(8,128)S(1)} %collective-permute-done.14.refs_1_, f32[128,128]{1,0:T(8,128)S(1)} %collective-permute-done.15.refs_2_, f32[128,128]{1,0:T(8,128)S(1)} %collective-permute-done.16.refs_3_, ...), custom_call_target="tpu_custom_call" | custom-call | flops 125829120 | bytes 1048576 | tf_op jit(solution)/shard_map/far/pallas_call | solution.py:33
  85.7 9.7 %all-to-all-start.2 = ((f32[64,1,128]{2,1,0:T(1,128)}), f32[64,1,128]{2,1,0:T(1,128)S(1)}, u32[]{:S(2)}, u32[]{:S(2)}) async-start(f32[64,1,128]{2,1,0:T(1,128)} %bitcast.10), calls=%async_computation.2 | async-start | bytes 65536 | tf_op jit(solution)/shard_map/all_to_all | solution.py:485
  95.5 1.2 %sweep.1.refs_6_.refs_3_ = f32[256,128]{1,0:T(8,128)S(1)} custom-call(f32[256,128]{1,0:T(8,128)S(1)} %get-tuple-element.62.refs_0_, bf16[4,384,384]{2,1,0:T(8,128)(2,1)S(1)} %get-tuple-element.55.refs_8_.refs_1_.refs_2_), custom_call_target="tpu_custom_call" | custom-call | flops 402653184 | bytes 1048576 | tf_op jit(solution)/shard_map/sweep/pallas_call | solution.py:33
  96.7 0.4 steps.1
  97.1 7.6 %all-to-all-done.2 = f32[64,1,128]{2,1,0:T(1,128)S(1)} async-done(((f32[64,1,128]{2,1,0:T(1,128)}), f32[64,1,128]{2,1,0:T(1,128)S(1)}, u32[]{:S(2)}, u32[]{:S(2)}) %all-to-all-start.2) | async-done | bytes 32800 | tf_op jit(solution)/shard_map/all_to_all | solution.py:485
  104.7 2.0 %states.1 = f32[256,128]{1,0:T(8,128)} custom-call(s32[5]{0:T(128)S(1)} %copy-done.4, f32[64,128]{1,0:T(8,128)S(1)} %bitcast.17, bf16[4,384,384]{2,1,0:T(8,128)(2,1)S(1)} %get-tuple-element.55.refs_8_.refs_1_.refs_2_, f32[256,128]{1,0:T(8,128)S(1)} %sweep.1.refs_6_.refs_3_, bf16[384,128]{1,0:T(8,128)(2,1)S(1)} %get-tuple-element.68.refs_4_, ...), custom_call_target="tpu_custom_call" | custom-call | flops 377487360 | bytes 1048576 | tf_op jit(solution)/shard_map/states/pallas_call | solution.py:33
  (42 shorter events, 0.6 us)
Async XLA Ops:
  0.0 7.2 %copy-start.1 = (bf16[64,16384]{1,0:T(8,128)(2,1)S(1)}, bf16[64,16384]{1,0:T(8,128)(2,1)}, u32[]{:S(2)}) copy-start(bf16[64,16384]{1,0:T(8,128)(2,1)} %rows_ref.1) | copy-start | bytes 6291460
  2.6 6.6 %collective-permute-start.3 = (bf16[144,256]{1,0:T(8,128)(2,1)}, bf16[144,256]{1,0:T(8,128)(2,1)S(1)}, u32[]{:S(2)}, u32[]{:S(2)}) collective-permute-start(bf16[144,256]{1,0:T(8,128)(2,1)} %pack.1.own_ref), channel_id=1, source_target_pairs={{0,1},{1,0},{2,3},{3,2},{4,5},{5,4},{6,7},{7,6},{8,9},{9,8},{10,11... | collective-permute-start | bytes 221192 | tf_op jit(solution)/shard_map/ppermute | solution.py:66
  4.7 5.6 %collective-permute-start.4 = (bf16[144,256]{1,0:T(8,128)(2,1)}, bf16[144,256]{1,0:T(8,128)(2,1)S(1)}, u32[]{:S(2)}, u32[]{:S(2)}) collective-permute-start(bf16[144,256]{1,0:T(8,128)(2,1)} %pack.1.own_ref), channel_id=1, source_target_pairs={{0,2},{1,3},{2,0},{3,1},{4,6},{5,7},{6,4},{7,5},{8,10},{9,11},{10,... | collective-permute-start | bytes 221192 | tf_op jit(solution)/shard_map/ppermute | solution.py:66
  7.2 5.1 %collective-permute-start.5 = (bf16[144,256]{1,0:T(8,128)(2,1)}, bf16[144,256]{1,0:T(8,128)(2,1)S(1)}, u32[]{:S(2)}, u32[]{:S(2)}) collective-permute-start(bf16[144,256]{1,0:T(8,128)(2,1)} %pack.1.own_ref), channel_id=1, source_target_pairs={{0,3},{1,2},{2,1},{3,0},{4,7},{5,6},{6,5},{7,4},{8,11},{9,10},{10,... | collective-permute-start | bytes 221192 | tf_op jit(solution)/shard_map/ppermute | solution.py:66
  7.8 1.4 %copy-start = (bf16[8,4,8,32,128]{4,3,2,1,0:T(8,128)(2,1)}, bf16[8,4,8,32,128]{4,3,2,1,0:T(8,128)(2,1)S(1)}, u32[]{:S(2)}) copy-start(bf16[8,4,8,32,128]{4,3,2,1,0:T(8,128)(2,1)S(1)} %by_taker.1) | copy-start | bytes 6291460
  9.2 3.1 %copy-start.7 = (bf16[144,256]{1,0:T(8,128)(2,1)}, bf16[144,256]{1,0:T(8,128)(2,1)S(1)}, u32[]{:S(2)}) copy-start(bf16[144,256]{1,0:T(8,128)(2,1)S(1)} %collective-permute-done.3.one_ref.refs_0_) | copy-start | bytes 221188
  10.3 1.9 %copy-start.8 = (bf16[144,256]{1,0:T(8,128)(2,1)}, bf16[144,256]{1,0:T(8,128)(2,1)S(1)}, u32[]{:S(2)}) copy-start(bf16[144,256]{1,0:T(8,128)(2,1)S(1)} %collective-permute-done.4.two_ref.refs_1_) | copy-start | bytes 221188
  12.3 0.6 copy-start.9
  12.9 33.4 %all-to-all-start = ((bf16[32,256,128]{2,1,0:T(8,128)(2,1)}), bf16[32,256,128]{2,1,0:T(8,128)(2,1)S(1)}, u32[]{:S(2)}, u32[]{:S(2)}) async-start(bf16[32,256,128]{2,1,0:T(8,128)(2,1)} %once.1), calls=%async_computation | async-start | bytes 4194304 | tf_op jit(solution)/shard_map/all_to_all | solution.py:426
  19.5 23.4 %copy-start.5 = (f32[128]{0:T(128)S(1)}, f32[128]{0:T(128)}, u32[]{:S(2)}) copy-start(f32[128]{0:T(128)} %param.10) | copy-start | bytes 1540
  20.1 24.5 %copy-start.4 = (s32[5]{0:T(128)S(1)}, s32[5]{0:T(128)}, u32[]{:S(2)}) copy-start(s32[5]{0:T(128)} %stack.23.place_ref.refs_0_) | copy-start | bytes 64
  22.7 21.9 %copy-start.2 = (bf16[128,1024]{1,0:T(8,128)(2,1)S(1)}, bf16[128,1024]{1,0:T(8,128)(2,1)}, u32[]{:S(2)}) copy-start(bf16[128,1024]{1,0:T(8,128)(2,1)} %get-tuple-element.40.refs_2_) | copy-start | bytes 786436
  22.7 21.9 %collective-permute-start.9 = (bf16[128,1024]{1,0:T(8,128)(2,1)}, bf16[128,1024]{1,0:T(8,128)(2,1)S(1)}, u32[]{:S(2)}, u32[]{:S(2)}) collective-permute-start(bf16[128,1024]{1,0:T(8,128)(2,1)} %get-tuple-element.40.refs_2_), channel_id=1, source_target_pairs={{0,4},{4,0},{1,5},{5,1},{2,6},{6,2},{3,7},{7,3},{8,12},{12,8},{9,1... | collective-permute-start | bytes 786440 | tf_op jit(solution)/shard_map/ppermute | solution.py:431
  23.0 3.1 %collective-permute-start.6 = (f32[8,128]{1,0:T(8,128)}, f32[8,128]{1,0:T(8,128)S(1)}, u32[]{:S(2)}, u32[]{:S(2)}) collective-permute-start(f32[8,128]{1,0:T(8,128)} %get-tuple-element.39), channel_id=1, source_target_pairs={{0,32},{32,0},{64,96},{96,64},{128,160},{160,128},{192,224},{224,1... | collective-permute-start | bytes 12296 | tf_op jit(solution)/shard_map/ppermute | solution.py:429
  26.8 11.1 %collective-permute-start.7 = (f32[8,128]{1,0:T(8,128)S(1)}, f32[8,128]{1,0:T(8,128)S(1)}, u32[]{:S(2)}, u32[]{:S(2)}) collective-permute-start(f32[8,128]{1,0:T(8,128)S(1)} %add.17), channel_id=1, source_target_pairs={{0,64},{32,96},{64,0},{96,32},{128,192},{160,224},{192,128},{224,1... | collective-permute-start | bytes 12296 | tf_op jit(solution)/shard_map/ppermute | solution.py:429
  33.9 23.3 %copy-start.3 = (f32[128,128]{1,0:T(8,128)S(1)}, f32[128,128]{1,0:T(8,128)}, u32[]{:S(2)}) copy-start(f32[128,128]{1,0:T(8,128)} %weigh.1.refs_0_) | copy-start | bytes 196612
  33.9 23.2 %collective-permute-start = (f32[128,128]{1,0:T(8,128)}, f32[128,128]{1,0:T(8,128)S(1)}, u32[]{:S(2)}, u32[]{:S(2)}) collective-permute-start(f32[128,128]{1,0:T(8,128)} %weigh.1.refs_0_), channel_id=1, source_target_pairs={{0,1},{1,0},{2,3},{3,2},{4,5},{5,4},{6,7},{7,6},{8,9},{9,8},{10,11... | collective-permute-start | bytes 196616 | tf_op jit(solution)/shard_map/ppermute | solution.py:66
  35.4 21.7 %collective-permute-start.1 = (f32[128,128]{1,0:T(8,128)}, f32[128,128]{1,0:T(8,128)S(1)}, u32[]{:S(2)}, u32[]{:S(2)}) collective-permute-start(f32[128,128]{1,0:T(8,128)} %weigh.1.refs_0_), channel_id=1, source_target_pairs={{0,2},{1,3},{2,0},{3,1},{4,6},{5,7},{6,4},{7,5},{8,10},{9,11},{10,... | collective-permute-start | bytes 196616 | tf_op jit(solution)/shard_map/ppermute | solution.py:66
  37.8 19.3 %collective-permute-start.2 = (f32[128,128]{1,0:T(8,128)}, f32[128,128]{1,0:T(8,128)S(1)}, u32[]{:S(2)}, u32[]{:S(2)}) collective-permute-start(f32[128,128]{1,0:T(8,128)} %weigh.1.refs_0_), channel_id=1, source_target_pairs={{0,3},{1,2},{2,1},{3,0},{4,7},{5,6},{6,5},{7,4},{8,11},{9,10},{10,... | collective-permute-start | bytes 196616 | tf_op jit(solution)/shard_map/ppermute | solution.py:66
  37.9 6.7 %collective-permute-start.8 = (f32[8,128]{1,0:T(8,128)S(1)}, f32[8,128]{1,0:T(8,128)S(1)}, u32[]{:S(2)}, u32[]{:S(2)}) collective-permute-start(f32[8,128]{1,0:T(8,128)S(1)} %add.18), channel_id=1, source_target_pairs={{0,128},{32,160},{64,192},{96,224},{128,0},{160,32},{192,64},{224,... | collective-permute-start | bytes 12296 | tf_op jit(solution)/shard_map/ppermute | solution.py:429
  48.9 18.0 %all-to-all-start.1 = ((f32[8,64,128]{2,1,0:T(8,128)}), f32[8,64,128]{2,1,0:T(8,128)S(1)}, u32[]{:S(2)}, u32[]{:S(2)}) async-start(f32[8,64,128]{2,1,0:T(8,128)} %get-tuple-element.53), calls=%async_computation.1 | async-start | bytes 524288 | tf_op jit(solution)/shard_map/all_to_all | solution.py:439
  57.2 25.3 %copy-start.6 = (f32[128]{0:T(128)S(1)}, f32[128]{0:T(128)}, u32[]{:S(2)}) copy-start(f32[128]{0:T(128)} %param.11) | copy-start | bytes 1540
  59.0 2.6 %collective-permute-start.10 = (f32[128,128]{1,0:T(8,128)S(1)}, f32[128,128]{1,0:T(8,128)S(1)}, u32[]{:S(2)}, u32[]{:S(2)}) collective-permute-start(f32[128,128]{1,0:T(8,128)S(1)} %get-tuple-element.44.refs_1_), channel_id=1, source_target_pairs={{0,4},{4,0},{1,5},{5,1},{2,6},{6,2},{3,7},{7,3},{8,12},{12,8},{9,1... | collective-permute-start | bytes 196616 | tf_op jit(solution)/shard_map/ppermute | solution.py:460
  62.4 8.9 %collective-permute-start.11 = (f32[128,128]{1,0:T(8,128)S(1)}, f32[128,128]{1,0:T(8,128)S(1)}, u32[]{:S(2)}, u32[]{:S(2)}) collective-permute-start(f32[128,128]{1,0:T(8,128)S(1)} %get-tuple-element.45.refs_1_), channel_id=1, source_target_pairs={{0,8},{8,0},{16,24},{24,16},{1,9},{9,1},{17,25},{25,17},{2,10},{10... | collective-permute-start | bytes 196616 | tf_op jit(solution)/shard_map/ppermute | solution.py:465
  63.7 7.6 %collective-permute-start.12 = (f32[128,128]{1,0:T(8,128)S(1)}, f32[128,128]{1,0:T(8,128)S(1)}, u32[]{:S(2)}, u32[]{:S(2)}) collective-permute-start(f32[128,128]{1,0:T(8,128)S(1)} %get-tuple-element.45.refs_1_), channel_id=1, source_target_pairs={{0,16},{8,24},{16,0},{24,8},{1,17},{9,25},{17,1},{25,9},{2,18},{10... | collective-permute-start | bytes 196616 | tf_op jit(solution)/shard_map/ppermute | solution.py:465
  65.3 5.9 %collective-permute-start.13 = (f32[128,128]{1,0:T(8,128)S(1)}, f32[128,128]{1,0:T(8,128)S(1)}, u32[]{:S(2)}, u32[]{:S(2)}) collective-permute-start(f32[128,128]{1,0:T(8,128)S(1)} %get-tuple-element.45.refs_1_), channel_id=1, source_target_pairs={{0,24},{8,16},{16,8},{24,0},{1,25},{9,17},{17,9},{25,1},{2,26},{10... | collective-permute-start | bytes 196616 | tf_op jit(solution)/shard_map/ppermute | solution.py:465
  66.9 11.6 %collective-permute-start.17 = (f32[64,128]{1,0:T(8,128)S(1)}, f32[64,128]{1,0:T(8,128)S(1)}, u32[]{:S(2)}, u32[]{:S(2)}) collective-permute-start(f32[64,128]{1,0:T(8,128)S(1)} %reduce_sum.9.refs_1_), channel_id=1, source_target_pairs={{0,1},{1,0},{2,3},{3,2},{4,5},{5,4},{6,7},{7,6},{8,9},{9,8},{10,11... | collective-permute-start | bytes 98312 | tf_op jit(solution)/shard_map/ppermute | solution.py:66
  71.9 12.1 %collective-permute-start.14 = (f32[128,128]{1,0:T(8,128)S(1)}, f32[128,128]{1,0:T(8,128)S(1)}, u32[]{:S(2)}, u32[]{:S(2)}) collective-permute-start(f32[128,128]{1,0:T(8,128)S(1)} %get-tuple-element.50), channel_id=1, source_target_pairs={{0,32},{32,0},{64,96},{96,64},{128,160},{160,128},{192,224},{224,1... | collective-permute-start | bytes 196616 | tf_op jit(solution)/shard_map/ppermute | solution.py:472
  72.5 11.5 %collective-permute-start.15 = (f32[128,128]{1,0:T(8,128)S(1)}, f32[128,128]{1,0:T(8,128)S(1)}, u32[]{:S(2)}, u32[]{:S(2)}) collective-permute-start(f32[128,128]{1,0:T(8,128)S(1)} %get-tuple-element.50), channel_id=1, source_target_pairs={{0,64},{32,96},{64,0},{96,32},{128,192},{160,224},{192,128},{224,1... | collective-permute-start | bytes 196616 | tf_op jit(solution)/shard_map/ppermute | solution.py:472
  74.6 9.4 %collective-permute-start.16 = (f32[128,128]{1,0:T(8,128)S(1)}, f32[128,128]{1,0:T(8,128)S(1)}, u32[]{:S(2)}, u32[]{:S(2)}) collective-permute-start(f32[128,128]{1,0:T(8,128)S(1)} %get-tuple-element.50), channel_id=1, source_target_pairs={{0,96},{32,64},{64,32},{96,0},{128,224},{160,192},{192,160},{224,1... | collective-permute-start | bytes 196616 | tf_op jit(solution)/shard_map/ppermute | solution.py:472
  75.5 4.3 %collective-permute-start.18 = (f32[64,128]{1,0:T(8,128)S(1)}, f32[64,128]{1,0:T(8,128)S(1)}, u32[]{:S(2)}, u32[]{:S(2)}) collective-permute-start(f32[64,128]{1,0:T(8,128)S(1)} %reduce_sum.9.refs_1_), channel_id=1, source_target_pairs={{0,2},{1,3},{2,0},{3,1},{4,6},{5,7},{6,4},{7,5},{8,10},{9,11},{10,... | collective-permute-start | bytes 98312 | tf_op jit(solution)/shard_map/ppermute | solution.py:66
  78.6 4.0 %collective-permute-start.19 = (f32[64,128]{1,0:T(8,128)S(1)}, f32[64,128]{1,0:T(8,128)S(1)}, u32[]{:S(2)}, u32[]{:S(2)}) collective-permute-start(f32[64,128]{1,0:T(8,128)S(1)} %reduce_sum.9.refs_1_), channel_id=1, source_target_pairs={{0,3},{1,2},{2,1},{3,0},{4,7},{5,6},{6,5},{7,4},{8,11},{9,10},{10,... | collective-permute-start | bytes 98312 | tf_op jit(solution)/shard_map/ppermute | solution.py:66
  85.7 19.0 %all-to-all-start.2 = ((f32[64,1,128]{2,1,0:T(1,128)}), f32[64,1,128]{2,1,0:T(1,128)S(1)}, u32[]{:S(2)}, u32[]{:S(2)}) async-start(f32[64,1,128]{2,1,0:T(1,128)} %bitcast.10), calls=%async_computation.2 | async-start | bytes 65536 | tf_op jit(solution)/shard_map/all_to_all | solution.py:485

commit v6 on v5

--- a/solution.py
+++ b/solution.py
@@ -237,7 +237,6 @@
         in_specs=[pl.BlockSpec(memory_space=pl.ANY)] * (1 + len(tokens)),
         out_specs=pl.BlockSpec(memory_space=pl.ANY),
         input_output_aliases={0: 0},
-        compiler_params=pltpu.CompilerParams(vmem_limit_bytes=60 << 20),
     )(array, *tokens)
 
 

time: 107 us -> 107 us (level)
  no operation moved by 1% of the time
where the time goes in v6:
time: 107 us
  starting transfers between devices  59.2 us (55%)
  Pallas kernels  23.9 us (22%)
  waiting for transfers between devices  20 us (19%)
  local copies, waits for them, and re-layouts  2.72 us (3%)
    ppermute x9, starting transfers between devices, xor_over_x(): return lax.ppermute(block, 'x', [(i, i ^ distance) for i in range(NX)])  15.5 us
    pallas_call x10, Pallas kernels, local(): pl.pallas_call(call, name=name, out_shape=outs, in_specs=[SCALARS] * len(...  11.5 us
    all_to_all x1, starting transfers between devices, on_device(): lax.all_to_all(sends, ('z', 'y', 'c'), split_axis=0, concat_axis=0, tiled...  9.73 us
    ppermute x3, starting transfers between devices, on_device(): kept = kept + lax.ppermute(kept, 'z', [(i, i ^ flip) for i in range(NZ)])  9.58 us
    all_to_all x1, starting transfers between devices, on_device(): lax.all_to_all(partial, 'z', split_axis=0, concat_axis=0, tiled=True)  8.19 us
    all_to_all x1, waiting for transfers between devices, on_device(): lax.all_to_all(sends, ('z', 'y', 'c'), split_axis=0, concat_axis=0, tiled...  7.62 us
    ppermute x9, waiting for transfers between devices, xor_over_x(): return lax.ppermute(block, 'x', [(i, i ^ distance) for i in range(NX)])  7.06 us
    all_to_all x1, starting transfers between devices, on_device(): lax.all_to_all(sent, ('y', 'c', 'x'), split_axis=0, concat_axis=0, tiled=...  6.57 us
  transfers between devices with their start and end apart: 23, of which 10 were waited for; matrix products, arithmetic and copies ran while one was open for 1% of the time, Pallas kernels for 17%

profile of v6, /device:TPU:1, one launch (start us, length us, event | category | flops | bytes accessed | tf_op | source)
XLA Modules:
  0.0 106.7 jit_solution(5071520527030100520)
XLA Ops:
  0.0 2.6 %pack.1.own_ref = bf16[144,256]{1,0:T(8,128)(2,1)} custom-call(s32[1,32]{1,0:T(1,128)} %kept_ref.3, bf16[32,128,128]{2,1,0:T(8,128)(2,1)} %noise_ref.3, bf16[4096,128]{1,0:T(8,128)(2,1)} %map_ref.3), custom_call_target="tpu_custom_call" | custom-call | flops 8388608 | bytes 262144 | tf_op jit(solution)/shard_map/pack/pallas_call | solution.py:120
  2.6 2.1 %collective-permute-start.3 = (bf16[144,256]{1,0:T(8,128)(2,1)}, bf16[144,256]{1,0:T(8,128)(2,1)S(1)}, u32[]{:S(2)}, u32[]{:S(2)}) collective-permute-start(bf16[144,256]{1,0:T(8,128)(2,1)} %pack.1.own_ref), channel_id=1, source_target_pairs={{0,1},{1,0},{2,3},{3,2},{4,5},{5,4},{6,7},{7,6},{8,9},{9,8},{10,11... | collective-permute-start | bytes 221192 | tf_op jit(solution)/shard_map/ppermute | solution.py:66
  4.7 2.5 %collective-permute-start.4 = (bf16[144,256]{1,0:T(8,128)(2,1)}, bf16[144,256]{1,0:T(8,128)(2,1)S(1)}, u32[]{:S(2)}, u32[]{:S(2)}) collective-permute-start(bf16[144,256]{1,0:T(8,128)(2,1)} %pack.1.own_ref), channel_id=1, source_target_pairs={{0,2},{1,3},{2,0},{3,1},{4,6},{5,7},{6,4},{7,5},{8,10},{9,11},{10,... | collective-permute-start | bytes 221192 | tf_op jit(solution)/shard_map/ppermute | solution.py:66
  7.2 0.6 by_taker.1
  7.8 1.4 %copy-done = bf16[8,4,8,32,128]{4,3,2,1,0:T(8,128)(2,1)} copy-done((bf16[8,4,8,32,128]{4,3,2,1,0:T(8,128)(2,1)}, bf16[8,4,8,32,128]{4,3,2,1,0:T(8,128)(2,1)S(1)}, u32[]{:S(2)}) %copy-start) | copy-done | bytes 2097176
  9.2 1.1 %collective-permute-done.4.two_ref.refs_1_ = bf16[144,256]{1,0:T(8,128)(2,1)S(1)} collective-permute-done((bf16[144,256]{1,0:T(8,128)(2,1)}, bf16[144,256]{1,0:T(8,128)(2,1)S(1)}, u32[]{:S(2)}, u32[]{:S(2)}) %collective-permute-start.4) | collective-permute-done | bytes 73760 | tf_op jit(solution)/shard_map/ppermute | solution.py:66
  10.3 1.9 %collective-permute-done.5.three_ref.refs_2_ = bf16[144,256]{1,0:T(8,128)(2,1)S(1)} collective-permute-done((bf16[144,256]{1,0:T(8,128)(2,1)}, bf16[144,256]{1,0:T(8,128)(2,1)S(1)}, u32[]{:S(2)}, u32[]{:S(2)}) %collective-permute-start.5) | collective-permute-done | bytes 73760 | tf_op jit(solution)/shard_map/ppermute | solution.py:66
  12.3 0.6 copy-done.9
  12.9 6.6 %all-to-all-start = ((bf16[32,256,128]{2,1,0:T(8,128)(2,1)}), bf16[32,256,128]{2,1,0:T(8,128)(2,1)S(1)}, u32[]{:S(2)}, u32[]{:S(2)}) async-start(bf16[32,256,128]{2,1,0:T(8,128)(2,1)} %once.1), calls=%async_computation | async-start | bytes 4194304 | tf_op jit(solution)/shard_map/all_to_all | solution.py:425
  19.5 0.6 stack.23.place_ref.refs_0_
  20.1 2.6 %gather.1 = (f32[8,128]{1,0:T(8,128)}, bf16[128,1024]{1,0:T(8,128)(2,1)}) custom-call(s32[5]{0:T(128)} %stack.23.place_ref.refs_0_, bf16[144,256]{1,0:T(8,128)(2,1)} %pack.1.own_ref, bf16[144,256]{1,0:T(8,128)(2,1)} %copy-done.7, bf16[144,256]{1,0:T(8,128)(2,1)} %copy-done.8, bf16[144,256]{1,0:T(8,128)(2,1)} %copy-done.9), custom_call_target="tpu_custom_call" | custom-call | bytes 1048576 | tf_op jit(solution)/shard_map/gather/pallas_call | solution.py:152
  23.0 1.6 %collective-permute-start.6 = (f32[8,128]{1,0:T(8,128)}, f32[8,128]{1,0:T(8,128)S(1)}, u32[]{:S(2)}, u32[]{:S(2)}) collective-permute-start(f32[8,128]{1,0:T(8,128)} %get-tuple-element.39), channel_id=1, source_target_pairs={{0,32},{32,0},{64,96},{96,64},{128,160},{160,128},{192,224},{224,1... | collective-permute-start | bytes 12296 | tf_op jit(solution)/shard_map/ppermute | solution.py:428
  24.7 1.5 %collective-permute-done.6 = f32[8,128]{1,0:T(8,128)S(1)} collective-permute-done((f32[8,128]{1,0:T(8,128)}, f32[8,128]{1,0:T(8,128)S(1)}, u32[]{:S(2)}, u32[]{:S(2)}) %collective-permute-start.6) | collective-permute-done | bytes 4128 | tf_op jit(solution)/shard_map/ppermute | solution.py:428
  26.2 0.7 add.17
  26.8 3.0 %collective-permute-start.7 = (f32[8,128]{1,0:T(8,128)S(1)}, f32[8,128]{1,0:T(8,128)S(1)}, u32[]{:S(2)}, u32[]{:S(2)}) collective-permute-start(f32[8,128]{1,0:T(8,128)S(1)} %add.17), channel_id=1, source_target_pairs={{0,64},{32,96},{64,0},{96,32},{128,192},{160,224},{192,128},{224,1... | collective-permute-start | bytes 12296 | tf_op jit(solution)/shard_map/ppermute | solution.py:428
  29.8 4.1 %weigh.1.refs_0_ = f32[128,128]{1,0:T(8,128)} custom-call(s32[1,32]{1,0:T(1,128)} %kept_ref.3, bf16[32,128,128]{2,1,0:T(8,128)(2,1)} %noise_ref.3, bf16[4096,128]{1,0:T(8,128)(2,1)} %map_ref.3), custom_call_target="tpu_custom_call" | custom-call | flops 268435456 | bytes 2097152 | tf_op jit(solution)/shard_map/weigh/pallas_call | solution.py:191
  33.9 1.5 %collective-permute-start = (f32[128,128]{1,0:T(8,128)}, f32[128,128]{1,0:T(8,128)S(1)}, u32[]{:S(2)}, u32[]{:S(2)}) collective-permute-start(f32[128,128]{1,0:T(8,128)} %weigh.1.refs_0_), channel_id=1, source_target_pairs={{0,1},{1,0},{2,3},{3,2},{4,5},{5,4},{6,7},{7,6},{8,9},{9,8},{10,11... | collective-permute-start | bytes 196616 | tf_op jit(solution)/shard_map/ppermute | solution.py:66
  35.4 2.4 %collective-permute-start.1 = (f32[128,128]{1,0:T(8,128)}, f32[128,128]{1,0:T(8,128)S(1)}, u32[]{:S(2)}, u32[]{:S(2)}) collective-permute-start(f32[128,128]{1,0:T(8,128)} %weigh.1.refs_0_), channel_id=1, source_target_pairs={{0,2},{1,3},{2,0},{3,1},{4,6},{5,7},{6,4},{7,5},{8,10},{9,11},{10,... | collective-permute-start | bytes 196616 | tf_op jit(solution)/shard_map/ppermute | solution.py:66
  37.9 5.0 %collective-permute-start.8 = (f32[8,128]{1,0:T(8,128)S(1)}, f32[8,128]{1,0:T(8,128)S(1)}, u32[]{:S(2)}, u32[]{:S(2)}) collective-permute-start(f32[8,128]{1,0:T(8,128)S(1)} %add.18), channel_id=1, source_target_pairs={{0,128},{32,160},{64,192},{96,224},{128,0},{160,32},{192,64},{224,... | collective-permute-start | bytes 12296 | tf_op jit(solution)/shard_map/ppermute | solution.py:428
  42.9 1.7 %collective-permute-done.8 = f32[8,128]{1,0:T(8,128)S(1)} collective-permute-done((f32[8,128]{1,0:T(8,128)S(1)}, f32[8,128]{1,0:T(8,128)S(1)}, u32[]{:S(2)}, u32[]{:S(2)}) %collective-permute-start.8) | collective-permute-done | bytes 4128 | tf_op jit(solution)/shard_map/ppermute | solution.py:428
  44.6 1.1 %masks.1 = (bf16[256,1024]{1,0:T(8,128)(2,1)S(1)}, f32[8,1024]{1,0:T(8,128)S(1)}) custom-call(s32[5]{0:T(128)S(1)} %copy-done.4, f32[8,128]{1,0:T(8,128)S(1)} %add.19.refs_1_, bf16[128,1024]{1,0:T(8,128)(2,1)S(1)} %copy-done.2, bf16[128,1024]{1,0:T(8,128)(2,1)S(1)} %collective-permute-done.9.refs_3_), custom_call_target="tpu_custom_call" | custom-call | flops 1048576 | bytes 1048576 | tf_op jit(solution)/shard_map/masks/pallas_call | solution.py:33
  45.7 0.6 all-to-all-done
  46.3 2.6 %rows.1 = (f32[8,64,128]{2,1,0:T(8,128)}, f32[8,128]{1,0:T(8,128)S(1)}) custom-call(s32[5]{0:T(128)S(1)} %copy-done.4, f32[8,1024]{1,0:T(8,128)S(1)} %get-tuple-element.41.mask_ref, bf16[256,1024]{1,0:T(8,128)(2,1)S(1)} %get-tuple-element.42.plane_ref, bf16[8,4,8,32,128]{4,3,2,1,0:T(8,128)(2,1)S(1)} %bitcast.16), custom_call_target="tpu_custom_call" | custom-call | flops 268435456 | bytes 3145728 | tf_op jit(solution)/shard_map/rows/pallas_call | solution.py:326
  48.9 8.2 %all-to-all-start.1 = ((f32[8,64,128]{2,1,0:T(8,128)}), f32[8,64,128]{2,1,0:T(8,128)S(1)}, u32[]{:S(2)}, u32[]{:S(2)}) async-start(f32[8,64,128]{2,1,0:T(8,128)} %get-tuple-element.53), calls=%async_computation.1 | async-start | bytes 524288 | tf_op jit(solution)/shard_map/all_to_all | solution.py:438
  57.2 1.8 %powers.1 = (f32[8,128,128]{2,1,0:T(8,128)S(1)}, f32[128,128]{1,0:T(8,128)S(1)}) custom-call(f32[128,128]{1,0:T(8,128)S(1)} %copy-done.3, f32[128,128]{1,0:T(8,128)S(1)} %collective-permute-done.refs_1_, f32[128,128]{1,0:T(8,128)S(1)} %collective-permute-done.1.refs_2_, f32[128,128]{1,0:T(8,128)S(1)} %collective-permute-done.2.refs_3_, ...), custom_call_target="tpu_custom_call" | custom-call | flops 40000000000 | bytes 1048576 | tf_op jit(solution)/shard_map/powers/pallas_call | solution.py:33
  59.0 1.7 %collective-permute-start.10 = (f32[128,128]{1,0:T(8,128)S(1)}, f32[128,128]{1,0:T(8,128)S(1)}, u32[]{:S(2)}, u32[]{:S(2)}) collective-permute-start(f32[128,128]{1,0:T(8,128)S(1)} %get-tuple-element.44.refs_1_), channel_id=1, source_target_pairs={{0,4},{4,0},{1,5},{5,1},{2,6},{6,2},{3,7},{7,3},{8,12},{12,8},{9,1... | collective-permute-start | bytes 196616 | tf_op jit(solution)/shard_map/ppermute | solution.py:459
  60.7 0.9 collective-permute-done.10.refs_2_
  61.6 0.8 pairs.1
  62.4 1.3 %collective-permute-start.11 = (f32[128,128]{1,0:T(8,128)S(1)}, f32[128,128]{1,0:T(8,128)S(1)}, u32[]{:S(2)}, u32[]{:S(2)}) collective-permute-start(f32[128,128]{1,0:T(8,128)S(1)} %get-tuple-element.45.refs_1_), channel_id=1, source_target_pairs={{0,8},{8,0},{16,24},{24,16},{1,9},{9,1},{17,25},{25,17},{2,10},{10... | collective-permute-start | bytes 196616 | tf_op jit(solution)/shard_map/ppermute | solution.py:464
  63.7 1.7 %collective-permute-start.12 = (f32[128,128]{1,0:T(8,128)S(1)}, f32[128,128]{1,0:T(8,128)S(1)}, u32[]{:S(2)}, u32[]{:S(2)}) collective-permute-start(f32[128,128]{1,0:T(8,128)S(1)} %get-tuple-element.45.refs_1_), channel_id=1, source_target_pairs={{0,16},{8,24},{16,0},{24,8},{1,17},{9,25},{17,1},{25,9},{2,18},{10... | collective-permute-start | bytes 196616 | tf_op jit(solution)/shard_map/ppermute | solution.py:464
  65.3 1.0 collective-permute-start.13
  66.3 0.6 all-to-all-done.1
  66.9 3.8 %collective-permute-start.17 = (f32[64,128]{1,0:T(8,128)S(1)}, f32[64,128]{1,0:T(8,128)S(1)}, u32[]{:S(2)}, u32[]{:S(2)}) collective-permute-start(f32[64,128]{1,0:T(8,128)S(1)} %reduce_sum.9.refs_1_), channel_id=1, source_target_pairs={{0,1},{1,0},{2,3},{3,2},{4,5},{5,4},{6,7},{7,6},{8,9},{9,8},{10,11... | collective-permute-start | bytes 98312 | tf_op jit(solution)/shard_map/ppermute | solution.py:66
  70.7 0.5 factors.1
  71.3 0.6 quads.1
  71.9 0.6 collective-permute-start.14
  72.5 2.1 %collective-permute-start.15 = (f32[128,128]{1,0:T(8,128)S(1)}, f32[128,128]{1,0:T(8,128)S(1)}, u32[]{:S(2)}, u32[]{:S(2)}) collective-permute-start(f32[128,128]{1,0:T(8,128)S(1)} %get-tuple-element.50), channel_id=1, source_target_pairs={{0,64},{32,96},{64,0},{96,32},{128,192},{160,224},{192,128},{224,1... | collective-permute-start | bytes 196616 | tf_op jit(solution)/shard_map/ppermute | solution.py:471
  74.6 0.9 collective-permute-start.16
  75.5 3.0 %collective-permute-start.18 = (f32[64,128]{1,0:T(8,128)S(1)}, f32[64,128]{1,0:T(8,128)S(1)}, u32[]{:S(2)}, u32[]{:S(2)}) collective-permute-start(f32[64,128]{1,0:T(8,128)S(1)} %reduce_sum.9.refs_1_), channel_id=1, source_target_pairs={{0,2},{1,3},{2,0},{3,1},{4,6},{5,7},{6,4},{7,5},{8,10},{9,11},{10,... | collective-permute-start | bytes 98312 | tf_op jit(solution)/shard_map/ppermute | solution.py:66
  78.6 1.3 %collective-permute-done.18.refs_3_ = f32[64,128]{1,0:T(8,128)S(1)} collective-permute-done((f32[64,128]{1,0:T(8,128)S(1)}, f32[64,128]{1,0:T(8,128)S(1)}, u32[]{:S(2)}, u32[]{:S(2)}) %collective-permute-start.18) | collective-permute-done | bytes 32800 | tf_op jit(solution)/shard_map/ppermute | solution.py:66
  79.9 2.7 %collective-permute-done.19.refs_4_ = f32[64,128]{1,0:T(8,128)S(1)} collective-permute-done((f32[64,128]{1,0:T(8,128)S(1)}, f32[64,128]{1,0:T(8,128)S(1)}, u32[]{:S(2)}, u32[]{:S(2)}) %collective-permute-start.19) | collective-permute-done | bytes 32800 | tf_op jit(solution)/shard_map/ppermute | solution.py:66
  82.5 1.5 %tail.1 = (f32[256,128]{1,0:T(8,128)S(1)}, f32[8,128]{1,0:T(8,128)S(1)}, f32[64,128]{1,0:T(8,128)S(1)}) custom-call(s32[5]{0:T(128)S(1)} %copy-done.4, f32[64,128]{1,0:T(8,128)S(1)} %reduce_sum.9.refs_1_, f32[64,128]{1,0:T(8,128)S(1)} %collective-permute-done.17.refs_2_, f32[64,128]{1,0:T(8,128)S(1)} %collective-permute-done.18.refs_3_, ...), custom_call_target="tpu_custom_call" | custom-call | flops 201326592 | bytes 1048576 | tf_op jit(solution)/shard_map/tail/pallas_call | solution.py:33
  84.0 1.7 %far.1 = (bf16[384,128]{1,0:T(8,128)(2,1)S(1)}, bf16[384,128]{1,0:T(8,128)(2,1)S(1)}, f32[64,128]{1,0:T(8,128)}) custom-call(s32[5]{0:T(128)S(1)} %copy-done.4, f32[128,128]{1,0:T(8,128)S(1)} %collective-permute-done.14.refs_1_, f32[128,128]{1,0:T(8,128)S(1)} %collective-permute-done.15.refs_2_, f32[128,128]{1,0:T(8,128)S(1)} %collective-permute-done.16.refs_3_, ...), custom_call_target="tpu_custom_call" | custom-call | flops 125829120 | bytes 1048576 | tf_op jit(solution)/shard_map/far/pallas_call | solution.py:33
  85.7 9.7 %all-to-all-start.2 = ((f32[64,1,128]{2,1,0:T(1,128)}), f32[64,1,128]{2,1,0:T(1,128)S(1)}, u32[]{:S(2)}, u32[]{:S(2)}) async-start(f32[64,1,128]{2,1,0:T(1,128)} %bitcast.10), calls=%async_computation.2 | async-start | bytes 65536 | tf_op jit(solution)/shard_map/all_to_all | solution.py:484
  95.5 1.2 %sweep.1.refs_6_.refs_3_ = f32[256,128]{1,0:T(8,128)S(1)} custom-call(f32[256,128]{1,0:T(8,128)S(1)} %get-tuple-element.62.refs_0_, bf16[4,384,384]{2,1,0:T(8,128)(2,1)S(1)} %get-tuple-element.55.refs_8_.refs_1_.refs_2_), custom_call_target="tpu_custom_call" | custom-call | flops 402653184 | bytes 1048576 | tf_op jit(solution)/shard_map/sweep/pallas_call | solution.py:33
  96.7 0.4 steps.1
  97.1 7.6 %all-to-all-done.2 = f32[64,1,128]{2,1,0:T(1,128)S(1)} async-done(((f32[64,1,128]{2,1,0:T(1,128)}), f32[64,1,128]{2,1,0:T(1,128)S(1)}, u32[]{:S(2)}, u32[]{:S(2)}) %all-to-all-start.2) | async-done | bytes 32800 | tf_op jit(solution)/shard_map/all_to_all | solution.py:484
  104.7 2.0 %states.1 = f32[256,128]{1,0:T(8,128)} custom-call(s32[5]{0:T(128)S(1)} %copy-done.4, f32[64,128]{1,0:T(8,128)S(1)} %bitcast.17, bf16[4,384,384]{2,1,0:T(8,128)(2,1)S(1)} %get-tuple-element.55.refs_8_.refs_1_.refs_2_, f32[256,128]{1,0:T(8,128)S(1)} %sweep.1.refs_6_.refs_3_, bf16[384,128]{1,0:T(8,128)(2,1)S(1)} %get-tuple-element.68.refs_4_, ...), custom_call_target="tpu_custom_call" | custom-call | flops 377487360 | bytes 1048576 | tf_op jit(solution)/shard_map/states/pallas_call | solution.py:33
  (42 shorter events, 0.6 us)
Async XLA Ops:
  0.0 7.2 %copy-start.1 = (bf16[64,16384]{1,0:T(8,128)(2,1)S(1)}, bf16[64,16384]{1,0:T(8,128)(2,1)}, u32[]{:S(2)}) copy-start(bf16[64,16384]{1,0:T(8,128)(2,1)} %rows_ref.1) | copy-start | bytes 6291460
  2.6 6.6 %collective-permute-start.3 = (bf16[144,256]{1,0:T(8,128)(2,1)}, bf16[144,256]{1,0:T(8,128)(2,1)S(1)}, u32[]{:S(2)}, u32[]{:S(2)}) collective-permute-start(bf16[144,256]{1,0:T(8,128)(2,1)} %pack.1.own_ref), channel_id=1, source_target_pairs={{0,1},{1,0},{2,3},{3,2},{4,5},{5,4},{6,7},{7,6},{8,9},{9,8},{10,11... | collective-permute-start | bytes 221192 | tf_op jit(solution)/shard_map/ppermute | solution.py:66
  4.7 5.6 %collective-permute-start.4 = (bf16[144,256]{1,0:T(8,128)(2,1)}, bf16[144,256]{1,0:T(8,128)(2,1)S(1)}, u32[]{:S(2)}, u32[]{:S(2)}) collective-permute-start(bf16[144,256]{1,0:T(8,128)(2,1)} %pack.1.own_ref), channel_id=1, source_target_pairs={{0,2},{1,3},{2,0},{3,1},{4,6},{5,7},{6,4},{7,5},{8,10},{9,11},{10,... | collective-permute-start | bytes 221192 | tf_op jit(solution)/shard_map/ppermute | solution.py:66
  7.2 5.1 %collective-permute-start.5 = (bf16[144,256]{1,0:T(8,128)(2,1)}, bf16[144,256]{1,0:T(8,128)(2,1)S(1)}, u32[]{:S(2)}, u32[]{:S(2)}) collective-permute-start(bf16[144,256]{1,0:T(8,128)(2,1)} %pack.1.own_ref), channel_id=1, source_target_pairs={{0,3},{1,2},{2,1},{3,0},{4,7},{5,6},{6,5},{7,4},{8,11},{9,10},{10,... | collective-permute-start | bytes 221192 | tf_op jit(solution)/shard_map/ppermute | solution.py:66
  7.8 1.4 %copy-start = (bf16[8,4,8,32,128]{4,3,2,1,0:T(8,128)(2,1)}, bf16[8,4,8,32,128]{4,3,2,1,0:T(8,128)(2,1)S(1)}, u32[]{:S(2)}) copy-start(bf16[8,4,8,32,128]{4,3,2,1,0:T(8,128)(2,1)S(1)} %by_taker.1) | copy-start | bytes 6291460
  9.2 3.1 %copy-start.7 = (bf16[144,256]{1,0:T(8,128)(2,1)}, bf16[144,256]{1,0:T(8,128)(2,1)S(1)}, u32[]{:S(2)}) copy-start(bf16[144,256]{1,0:T(8,128)(2,1)S(1)} %collective-permute-done.3.one_ref.refs_0_) | copy-start | bytes 221188
  10.3 1.9 %copy-start.8 = (bf16[144,256]{1,0:T(8,128)(2,1)}, bf16[144,256]{1,0:T(8,128)(2,1)S(1)}, u32[]{:S(2)}) copy-start(bf16[144,256]{1,0:T(8,128)(2,1)S(1)} %collective-permute-done.4.two_ref.refs_1_) | copy-start | bytes 221188
  12.3 0.6 copy-start.9
  12.9 33.4 %all-to-all-start = ((bf16[32,256,128]{2,1,0:T(8,128)(2,1)}), bf16[32,256,128]{2,1,0:T(8,128)(2,1)S(1)}, u32[]{:S(2)}, u32[]{:S(2)}) async-start(bf16[32,256,128]{2,1,0:T(8,128)(2,1)} %once.1), calls=%async_computation | async-start | bytes 4194304 | tf_op jit(solution)/shard_map/all_to_all | solution.py:425
  19.5 23.4 %copy-start.5 = (f32[128]{0:T(128)S(1)}, f32[128]{0:T(128)}, u32[]{:S(2)}) copy-start(f32[128]{0:T(128)} %param.10) | copy-start | bytes 1540
  20.1 24.5 %copy-start.4 = (s32[5]{0:T(128)S(1)}, s32[5]{0:T(128)}, u32[]{:S(2)}) copy-start(s32[5]{0:T(128)} %stack.23.place_ref.refs_0_) | copy-start | bytes 64
  22.7 21.9 %copy-start.2 = (bf16[128,1024]{1,0:T(8,128)(2,1)S(1)}, bf16[128,1024]{1,0:T(8,128)(2,1)}, u32[]{:S(2)}) copy-start(bf16[128,1024]{1,0:T(8,128)(2,1)} %get-tuple-element.40.refs_2_) | copy-start | bytes 786436
  22.7 21.9 %collective-permute-start.9 = (bf16[128,1024]{1,0:T(8,128)(2,1)}, bf16[128,1024]{1,0:T(8,128)(2,1)S(1)}, u32[]{:S(2)}, u32[]{:S(2)}) collective-permute-start(bf16[128,1024]{1,0:T(8,128)(2,1)} %get-tuple-element.40.refs_2_), channel_id=1, source_target_pairs={{0,4},{4,0},{1,5},{5,1},{2,6},{6,2},{3,7},{7,3},{8,12},{12,8},{9,1... | collective-permute-start | bytes 786440 | tf_op jit(solution)/shard_map/ppermute | solution.py:430
  23.0 3.1 %collective-permute-start.6 = (f32[8,128]{1,0:T(8,128)}, f32[8,128]{1,0:T(8,128)S(1)}, u32[]{:S(2)}, u32[]{:S(2)}) collective-permute-start(f32[8,128]{1,0:T(8,128)} %get-tuple-element.39), channel_id=1, source_target_pairs={{0,32},{32,0},{64,96},{96,64},{128,160},{160,128},{192,224},{224,1... | collective-permute-start | bytes 12296 | tf_op jit(solution)/shard_map/ppermute | solution.py:428
  26.8 11.1 %collective-permute-start.7 = (f32[8,128]{1,0:T(8,128)S(1)}, f32[8,128]{1,0:T(8,128)S(1)}, u32[]{:S(2)}, u32[]{:S(2)}) collective-permute-start(f32[8,128]{1,0:T(8,128)S(1)} %add.17), channel_id=1, source_target_pairs={{0,64},{32,96},{64,0},{96,32},{128,192},{160,224},{192,128},{224,1... | collective-permute-start | bytes 12296 | tf_op jit(solution)/shard_map/ppermute | solution.py:428
  33.9 23.3 %copy-start.3 = (f32[128,128]{1,0:T(8,128)S(1)}, f32[128,128]{1,0:T(8,128)}, u32[]{:S(2)}) copy-start(f32[128,128]{1,0:T(8,128)} %weigh.1.refs_0_) | copy-start | bytes 196612
  33.9 23.2 %collective-permute-start = (f32[128,128]{1,0:T(8,128)}, f32[128,128]{1,0:T(8,128)S(1)}, u32[]{:S(2)}, u32[]{:S(2)}) collective-permute-start(f32[128,128]{1,0:T(8,128)} %weigh.1.refs_0_), channel_id=1, source_target_pairs={{0,1},{1,0},{2,3},{3,2},{4,5},{5,4},{6,7},{7,6},{8,9},{9,8},{10,11... | collective-permute-start | bytes 196616 | tf_op jit(solution)/shard_map/ppermute | solution.py:66
  35.4 21.7 %collective-permute-start.1 = (f32[128,128]{1,0:T(8,128)}, f32[128,128]{1,0:T(8,128)S(1)}, u32[]{:S(2)}, u32[]{:S(2)}) collective-permute-start(f32[128,128]{1,0:T(8,128)} %weigh.1.refs_0_), channel_id=1, source_target_pairs={{0,2},{1,3},{2,0},{3,1},{4,6},{5,7},{6,4},{7,5},{8,10},{9,11},{10,... | collective-permute-start | bytes 196616 | tf_op jit(solution)/shard_map/ppermute | solution.py:66
  37.8 19.3 %collective-permute-start.2 = (f32[128,128]{1,0:T(8,128)}, f32[128,128]{1,0:T(8,128)S(1)}, u32[]{:S(2)}, u32[]{:S(2)}) collective-permute-start(f32[128,128]{1,0:T(8,128)} %weigh.1.refs_0_), channel_id=1, source_target_pairs={{0,3},{1,2},{2,1},{3,0},{4,7},{5,6},{6,5},{7,4},{8,11},{9,10},{10,... | collective-permute-start | bytes 196616 | tf_op jit(solution)/shard_map/ppermute | solution.py:66
  37.9 6.7 %collective-permute-start.8 = (f32[8,128]{1,0:T(8,128)S(1)}, f32[8,128]{1,0:T(8,128)S(1)}, u32[]{:S(2)}, u32[]{:S(2)}) collective-permute-start(f32[8,128]{1,0:T(8,128)S(1)} %add.18), channel_id=1, source_target_pairs={{0,128},{32,160},{64,192},{96,224},{128,0},{160,32},{192,64},{224,... | collective-permute-start | bytes 12296 | tf_op jit(solution)/shard_map/ppermute | solution.py:428
  48.9 18.0 %all-to-all-start.1 = ((f32[8,64,128]{2,1,0:T(8,128)}), f32[8,64,128]{2,1,0:T(8,128)S(1)}, u32[]{:S(2)}, u32[]{:S(2)}) async-start(f32[8,64,128]{2,1,0:T(8,128)} %get-tuple-element.53), calls=%async_computation.1 | async-start | bytes 524288 | tf_op jit(solution)/shard_map/all_to_all | solution.py:438
  57.2 25.3 %copy-start.6 = (f32[128]{0:T(128)S(1)}, f32[128]{0:T(128)}, u32[]{:S(2)}) copy-start(f32[128]{0:T(128)} %param.11) | copy-start | bytes 1540
  59.0 2.6 %collective-permute-start.10 = (f32[128,128]{1,0:T(8,128)S(1)}, f32[128,128]{1,0:T(8,128)S(1)}, u32[]{:S(2)}, u32[]{:S(2)}) collective-permute-start(f32[128,128]{1,0:T(8,128)S(1)} %get-tuple-element.44.refs_1_), channel_id=1, source_target_pairs={{0,4},{4,0},{1,5},{5,1},{2,6},{6,2},{3,7},{7,3},{8,12},{12,8},{9,1... | collective-permute-start | bytes 196616 | tf_op jit(solution)/shard_map/ppermute | solution.py:459
  62.4 8.9 %collective-permute-start.11 = (f32[128,128]{1,0:T(8,128)S(1)}, f32[128,128]{1,0:T(8,128)S(1)}, u32[]{:S(2)}, u32[]{:S(2)}) collective-permute-start(f32[128,128]{1,0:T(8,128)S(1)} %get-tuple-element.45.refs_1_), channel_id=1, source_target_pairs={{0,8},{8,0},{16,24},{24,16},{1,9},{9,1},{17,25},{25,17},{2,10},{10... | collective-permute-start | bytes 196616 | tf_op jit(solution)/shard_map/ppermute | solution.py:464
  63.7 7.6 %collective-permute-start.12 = (f32[128,128]{1,0:T(8,128)S(1)}, f32[128,128]{1,0:T(8,128)S(1)}, u32[]{:S(2)}, u32[]{:S(2)}) collective-permute-start(f32[128,128]{1,0:T(8,128)S(1)} %get-tuple-element.45.refs_1_), channel_id=1, source_target_pairs={{0,16},{8,24},{16,0},{24,8},{1,17},{9,25},{17,1},{25,9},{2,18},{10... | collective-permute-start | bytes 196616 | tf_op jit(solution)/shard_map/ppermute | solution.py:464
  65.3 5.9 %collective-permute-start.13 = (f32[128,128]{1,0:T(8,128)S(1)}, f32[128,128]{1,0:T(8,128)S(1)}, u32[]{:S(2)}, u32[]{:S(2)}) collective-permute-start(f32[128,128]{1,0:T(8,128)S(1)} %get-tuple-element.45.refs_1_), channel_id=1, source_target_pairs={{0,24},{8,16},{16,8},{24,0},{1,25},{9,17},{17,9},{25,1},{2,26},{10... | collective-permute-start | bytes 196616 | tf_op jit(solution)/shard_map/ppermute | solution.py:464
  66.9 11.6 %collective-permute-start.17 = (f32[64,128]{1,0:T(8,128)S(1)}, f32[64,128]{1,0:T(8,128)S(1)}, u32[]{:S(2)}, u32[]{:S(2)}) collective-permute-start(f32[64,128]{1,0:T(8,128)S(1)} %reduce_sum.9.refs_1_), channel_id=1, source_target_pairs={{0,1},{1,0},{2,3},{3,2},{4,5},{5,4},{6,7},{7,6},{8,9},{9,8},{10,11... | collective-permute-start | bytes 98312 | tf_op jit(solution)/shard_map/ppermute | solution.py:66
  71.9 12.1 %collective-permute-start.14 = (f32[128,128]{1,0:T(8,128)S(1)}, f32[128,128]{1,0:T(8,128)S(1)}, u32[]{:S(2)}, u32[]{:S(2)}) collective-permute-start(f32[128,128]{1,0:T(8,128)S(1)} %get-tuple-element.50), channel_id=1, source_target_pairs={{0,32},{32,0},{64,96},{96,64},{128,160},{160,128},{192,224},{224,1... | collective-permute-start | bytes 196616 | tf_op jit(solution)/shard_map/ppermute | solution.py:471
  72.5 11.5 %collective-permute-start.15 = (f32[128,128]{1,0:T(8,128)S(1)}, f32[128,128]{1,0:T(8,128)S(1)}, u32[]{:S(2)}, u32[]{:S(2)}) collective-permute-start(f32[128,128]{1,0:T(8,128)S(1)} %get-tuple-element.50), channel_id=1, source_target_pairs={{0,64},{32,96},{64,0},{96,32},{128,192},{160,224},{192,128},{224,1... | collective-permute-start | bytes 196616 | tf_op jit(solution)/shard_map/ppermute | solution.py:471
  74.6 9.4 %collective-permute-start.16 = (f32[128,128]{1,0:T(8,128)S(1)}, f32[128,128]{1,0:T(8,128)S(1)}, u32[]{:S(2)}, u32[]{:S(2)}) collective-permute-start(f32[128,128]{1,0:T(8,128)S(1)} %get-tuple-element.50), channel_id=1, source_target_pairs={{0,96},{32,64},{64,32},{96,0},{128,224},{160,192},{192,160},{224,1... | collective-permute-start | bytes 196616 | tf_op jit(solution)/shard_map/ppermute | solution.py:471
  75.5 4.3 %collective-permute-start.18 = (f32[64,128]{1,0:T(8,128)S(1)}, f32[64,128]{1,0:T(8,128)S(1)}, u32[]{:S(2)}, u32[]{:S(2)}) collective-permute-start(f32[64,128]{1,0:T(8,128)S(1)} %reduce_sum.9.refs_1_), channel_id=1, source_target_pairs={{0,2},{1,3},{2,0},{3,1},{4,6},{5,7},{6,4},{7,5},{8,10},{9,11},{10,... | collective-permute-start | bytes 98312 | tf_op jit(solution)/shard_map/ppermute | solution.py:66
  78.6 4.0 %collective-permute-start.19 = (f32[64,128]{1,0:T(8,128)S(1)}, f32[64,128]{1,0:T(8,128)S(1)}, u32[]{:S(2)}, u32[]{:S(2)}) collective-permute-start(f32[64,128]{1,0:T(8,128)S(1)} %reduce_sum.9.refs_1_), channel_id=1, source_target_pairs={{0,3},{1,2},{2,1},{3,0},{4,7},{5,6},{6,5},{7,4},{8,11},{9,10},{10,... | collective-permute-start | bytes 98312 | tf_op jit(solution)/shard_map/ppermute | solution.py:66
  85.7 19.0 %all-to-all-start.2 = ((f32[64,1,128]{2,1,0:T(1,128)}), f32[64,1,128]{2,1,0:T(1,128)S(1)}, u32[]{:S(2)}, u32[]{:S(2)}) async-start(f32[64,1,128]{2,1,0:T(1,128)} %bitcast.10), calls=%async_computation.2 | async-start | bytes 65536 | tf_op jit(solution)/shard_map/all_to_all | solution.py:484
